TPU v7x, 256 devices: a whole 4x4x8 slice. The times are simulated.
256 devices in a mesh: gx: 8 (over z), gy: 32 (over x, y, core).
Axes of the slice: x: 4, y: 4, z: 8, core: 2. Of those that a mesh axis runs over, the one named last changes fastest.
Arguments:
- starting_heat_state: float32 [128, 1024, 128], P('gx', 'gy'), may hold values from -5 to 5
- material_zone_ids: int32 [64, 512, 64], P('gx', 'gy'), may hold values from 0 to 15
- zone_diffusivity_lookup: float32 [16], replicated, may hold values from 1 to 10
Outputs:
- new_temperature: float32 [128, 1024, 128], P('gx', 'gy')
All inputs are finite; a program needn't handle non-finite values.
Results may differ from a plain program's by a relative error of at most 0.017.
Values sent between devices are 32-bit elements; how exact they have to be, the bound alone decides.
No kernel may reach another device: no remote copies, remote signals or barrier semaphores. Data moves between devices by JAX's collectives and lax.ppermute only.
A program may use at most 64 MiB of HBM per device.

v0:
```python
import jax
import jax.numpy as jnp
from jax import lax
from jax.experimental import pallas as pl
from jax.experimental.pallas import tpu as pltpu
from jax.sharding import PartitionSpec as P

NX, NY, NZ = 16, 32, 128
MX, MY = NX // 2, NY // 2
XROWS = 104
YROWS = 48
f32 = jnp.float32


def lanes(shape):
    return lax.broadcasted_iota(jnp.int32, shape, 1)


def rows_of(shape):
    return lax.broadcasted_iota(jnp.int32, shape, 0)


def pack(first, second):
    return jnp.where(lanes(first.shape) % 2 == 0, first, second)


def unpack(both):
    even = lanes(both.shape) % 2 == 0
    first = jnp.where(even, both, pltpu.roll(both, 1, 1))
    second = jnp.where(even, pltpu.roll(both, NZ - 1, 1), both)
    return first, second


def through(near, far, link, beyond, leak, near_src, far_src, src):
    total = far + leak
    q = total + link
    cross = total * link
    f = beyond / ((near + beyond) * q + cross)
    new_leak = f * (near * q + cross)
    new_src = [f * (n * q + (e + s) * link) for n, e, s in zip(near_src, far_src, src)]
    return new_leak, new_src


def two_nodes(first, last, link, first_src, last_src):
    inv = 1.0 / (first * last + link * (first + last))
    low = [((last + link) * a + link * b) * inv for a, b in zip(first_src, last_src)]
    high = [((first + link) * b + link * a) * inv for a, b in zip(first_src, last_src)]
    return low, high


def eliminate(conduct, put):
    alpha = jnp.ones_like(conduct[0])
    beta = jnp.ones_like(conduct[0])
    link = conduct[0]
    for t in range(1, len(conduct)):
        g = conduct[t]
        inv = 1.0 / (link + beta + g)
        hd = link * inv
        gd = g * inv
        put(t - 1, gd, hd, inv)
        alpha = alpha + beta * hd
        link = link * gd
        beta = 1.0 + beta * gd
    return alpha, beta, link


def prepare_kernel(ids_ref, table_ref, heat_ref, k_ref, low_ref, high_ref, wide):
    ids = ids_ref[...]
    k = jnp.zeros(ids.shape, f32)
    for region in range(table_ref.shape[0]):
        k = jnp.where(ids == region, table_ref[region], k)
    wide[...] = jnp.zeros(wide.shape, f32)
    wide[:, : NZ // 2] = k
    index = lanes(wide.shape) // 2
    k_ref[...] = jnp.take_along_axis(wide[...], index, axis=1, mode="promise_in_bounds")
    low_ref[:NX] = heat_ref[pl.ds(0, NX, stride=NY), :]
    high_ref[:NX] = heat_ref[pl.ds(NY - 1, NX, stride=NY), :]
    low_ref[NX:] = k_ref[pl.ds(0, MX, stride=MY), :]
    high_ref[NX:] = k_ref[pl.ds(MY - 1, MX, stride=MY), :]


def matrix_kernel(
    k_ref, gx_ref, hx_ref, ix_ref, px_ref, gy_ref, hy_ref, iy_ref, my_ref, za_ref, zc_ref, zi_ref
):
    at_x, at_y = lax.axis_index("gx"), lax.axis_index("gy")
    last_x, last_y = lax.axis_size("gx") - 1, lax.axis_size("gy") - 1

    def chain(k):
        joints = []
        for m in range(len(k)):
            joints.append(2000.0 * k[m])
            if m + 1 < len(k):
                joints.append(1000.0 * (k[m] + k[m + 1]))
        return joints

    kx = [k_ref[m * MY : (m + 1) * MY, :] for m in range(MX)]

    def put_x(t, gd, hd, inv):
        gx_ref[t * MY : (t + 1) * MY, :] = gd
        hx_ref[t * MY : (t + 1) * MY, :] = hd
        ix_ref[t * MY : (t + 1) * MY, :] = inv

    alpha, beta, link = eliminate(chain(kx), put_x)
    alpha = alpha + jnp.where(at_x == 0, 1000.0, 0.0) * kx[0]
    beta = beta + jnp.where(at_x == last_x, 1000.0, 0.0) * kx[-1]
    px_ref[0:16, :] = pack(alpha, beta)
    px_ref[16:32, :] = pack(link, kx[0])
    px_ref[32:40, :] = pack(kx[-1][:8], kx[-1][8:])

    ky = [k_ref[pl.ds(n, MX, stride=MY), :] for n in range(MY)]

    def put_y(t, gd, hd, inv):
        gy_ref[t * MX : (t + 1) * MX, :] = gd
        hy_ref[t * MX : (t + 1) * MX, :] = hd
        iy_ref[t * MX : (t + 1) * MX, :] = inv

    alpha, beta, link = eliminate(chain(ky), put_y)
    my_ref[0:8, :] = alpha + jnp.where(at_y == 0, 1000.0, 0.0) * ky[0]
    my_ref[8:16, :] = beta + jnp.where(at_y == last_y, 1000.0, 0.0) * ky[-1]
    my_ref[16:24, :] = link

    group = 4
    for start in range(0, MY, group):
        k = jnp.concatenate(ky[start : start + group], 0)
        lane = lanes(k.shape)
        west = 0.25 * (k + jnp.where(lane == 0, 0.0, pltpu.roll(k, 1, 1)))
        east = 0.25 * (k + jnp.where(lane == NZ - 1, 0.0, pltpu.roll(k, NZ - 1, 1)))
        diag = 1.0 + (west + east)
        a = jnp.where(lane == 0, 0.0, west)
        c = jnp.where(lane == NZ - 1, 0.0, east)
        size = MX * group
        for s in range(7):
            step = 1 << s
            inv = 1.0 / diag
            low = a * pltpu.roll(inv, step, 1)
            high = c * pltpu.roll(inv, NZ - step, 1)
            at = s * MX * MY + start * MX
            za_ref[at : at + size, :] = low
            zc_ref[at : at + size, :] = high
            diag = diag - (low * pltpu.roll(c, step, 1) + high * pltpu.roll(a, NZ - step, 1))
            a = low * pltpu.roll(a, step, 1)
            c = high * pltpu.roll(c, NZ - step, 1)
        zi_ref[start * MX : start * MX + size, :] = 1.0 / diag


def right_side_kernel(heat_ref, k_ref, low_ref, high_ref, gx_ref, hx_ref, px_ref, send_ref, rb_ref):
    at_y = lax.axis_index("gy")
    inside_low = jnp.where(at_y == 0, 0.0, 1.0)
    inside_high = jnp.where(at_y == lax.axis_size("gy") - 1, 0.0, 1.0)
    shape = (MY, NZ)
    lane, row = lanes(shape), rows_of(shape)
    ra = None
    rb = None
    for m in range(MX):
        k = k_ref[m * MY : (m + 1) * MY, :]
        k_low = inside_low * low_ref[NX + m : NX + m + 1, :]
        k_high = inside_high * high_ref[NX + m : NX + m + 1, :]
        face_low = 2000.0 * (k + jnp.where(row == 0, k_low, pltpu.roll(k, 1, 0)))
        face_high = 2000.0 * (k + jnp.where(row == MY - 1, k_high, pltpu.roll(k, MY - 1, 0)))
        face_mid = 4000.0 * k
        west = 0.5 * (k + jnp.where(lane == 0, 0.0, pltpu.roll(k, 1, 1)))
        east = 0.5 * (k + jnp.where(lane == NZ - 1, 0.0, pltpu.roll(k, NZ - 1, 1)))
        middle = 2.0 - (west + east)
        west = jnp.where(lane == 0, 0.0, west)
        east = jnp.where(lane == NZ - 1, 0.0, east)
        for x in (2 * m, 2 * m + 1):
            even = heat_ref[pl.ds(x * NY, MY, stride=2), :]
            odd = heat_ref[pl.ds(x * NY + 1, MY, stride=2), :]
            before = jnp.where(row == 0, inside_low * low_ref[x : x + 1, :], pltpu.roll(odd, 1, 0))
            after = jnp.where(
                row == MY - 1, inside_high * high_ref[x : x + 1, :], pltpu.roll(even, MY - 1, 0)
            )
            flow = face_mid * (odd - even)
            r = []
            for v, along_y in (
                (even, flow - face_low * (even - before)),
                (odd, face_high * (after - odd) - flow),
            ):
                along_z = west * pltpu.roll(v, 1, 1) + east * pltpu.roll(v, NZ - 1, 1)
                r.append(along_y + (along_z + middle * v))
            if x == 0:
                ra = r
            elif x == 1:
                rb = r
            else:
                t = x - 2
                gd = gx_ref[t * MY : (t + 1) * MY, :]
                hd = hx_ref[t * MY : (t + 1) * MY, :]
                for q in range(2):
                    rb_ref[t * NY + q * MY : t * NY + (q + 1) * MY, :] = rb[q]
                ra = [a + b * hd for a, b in zip(ra, rb)]
                rb = [n + b * gd for n, b in zip(r, rb)]
    p = px_ref[...]
    for d in range(send_ref.shape[0]):
        send_ref[d, 0:16, :] = ra[0]
        send_ref[d, 16:32, :] = ra[1]
        send_ref[d, 32:48, :] = rb[0]
        send_ref[d, 48:64, :] = rb[1]
        send_ref[d, 64:104, :] = p


def x_solve_kernel(
    recv_ref, heat_ref, k_ref, low_ref, high_ref, rb_ref, gx_ref, hx_ref, ix_ref, gy_ref, hy_ref, my_ref,
    core_ref, mid_ref, rby_ref, first,
):
    at = lax.axis_index("gx")
    count = recv_ref.shape[0]

    def segment(d):
        alpha, beta = unpack(recv_ref[d, 64:80, :])
        link, k_first = unpack(recv_ref[d, 80:96, :])
        k_last = jnp.concatenate(unpack(recv_ref[d, 96:104, :]), 0)
        ra = [recv_ref[d, 0:16, :], recv_ref[d, 16:32, :]]
        rb = [recv_ref[d, 32:48, :], recv_ref[d, 48:64, :]]
        return alpha, beta, link, k_first, k_last, ra, rb

    segments = [segment(d) for d in range(count)]
    joints = [1000.0 * (segments[d][4] + segments[d + 1][3]) for d in range(count - 1)]
    zero = jnp.zeros((MY, NZ), f32)
    left, left_src = zero, [zero, zero]
    right, right_src = zero, [zero, zero]
    for step in range(count - 1):
        d = step
        alpha, beta, link, _, _, ra, rb = segments[d]
        new, new_src = through(beta, alpha, link, joints[d], left, rb, ra, left_src)
        left = jnp.where(d < at, new, left)
        left_src = [jnp.where(d < at, n, o) for n, o in zip(new_src, left_src)]
        d = count - 1 - step
        alpha, beta, link, _, _, ra, rb = segments[d]
        new, new_src = through(alpha, beta, link, joints[d - 1], right, ra, rb, right_src)
        right = jnp.where(d > at, new, right)
        right_src = [jnp.where(d > at, n, o) for n, o in zip(new_src, right_src)]
    alpha, beta, link, _, _, ra, rb = segment(at)
    u_first, u_next = two_nodes(
        alpha + left,
        beta + right,
        link,
        [a + s for a, s in zip(ra, left_src)],
        [b + s for b, s in zip(rb, right_src)],
    )

    def keep(x, u):
        for q in range(2):
            heat = heat_ref[pl.ds(x * NY + q, MY, stride=2), :]
            first[x * NY + q * MY : x * NY + (q + 1) * MY, :] = u[q] - 2.0 * heat

    keep(0, u_first)
    keep(NX - 1, u_next)
    for x in range(NX - 2, 0, -1):
        t = x - 1
        gd = gx_ref[t * MY : (t + 1) * MY, :]
        hd = hx_ref[t * MY : (t + 1) * MY, :]
        inv = ix_ref[t * MY : (t + 1) * MY, :]
        b = [rb_ref[t * NY + q * MY : t * NY + (q + 1) * MY, :] for q in range(2)]
        u_next = [(inv * b[q] + hd * u_first[q]) + gd * u_next[q] for q in range(2)]
        keep(x, u_next)

    def side(y):
        start = (y % 2) * MY + y // 2
        return [first[pl.ds(p * NY + start, MX, stride=2 * NY), :] for p in range(2)]

    ra = side(0)
    rb = side(1)
    for t in range(NY - 2):
        gd = gy_ref[t * MX : (t + 1) * MX, :]
        hd = hy_ref[t * MX : (t + 1) * MX, :]
        for p in range(2):
            rby_ref[t * NX + p * MX : t * NX + (p + 1) * MX, :] = rb[p]
        new = side(t + 2)
        ra = [a + b * hd for a, b in zip(ra, rb)]
        rb = [n + b * gd for n, b in zip(new, rb)]
    core = lax.rem(lax.axis_index("gy"), 2)
    joint_low = 1000.0 * (low_ref[NX:, :] + k_ref[pl.ds(0, MX, stride=MY), :])
    joint_high = 1000.0 * (high_ref[NX:, :] + k_ref[pl.ds(MY - 1, MX, stride=MY), :])
    mid_ref[...] = jnp.where(core == 0, joint_high, joint_low)
    outer = jnp.where(core == 0, joint_low, joint_high)
    core_ref[0:8, :] = ra[0]
    core_ref[8:16, :] = ra[1]
    core_ref[16:24, :] = rb[0]
    core_ref[24:32, :] = rb[1]
    core_ref[32:40, :] = pack(my_ref[0:8, :], my_ref[8:16, :])
    core_ref[40:48, :] = pack(my_ref[16:24, :], outer)


def y_segment(rows):
    alpha, beta = unpack(rows(32))
    link, joint = unpack(rows(40))
    return alpha, beta, link, joint, [rows(0), rows(8)], [rows(16), rows(24)]


def chip_kernel(own_ref, other_ref, mid_ref, send_ref):
    core = lax.rem(lax.axis_index("gy"), 2)
    own = y_segment(lambda r: own_ref[r : r + 8, :])
    other = y_segment(lambda r: other_ref[r : r + 8, :])

    def choose(a, b):
        return jnp.where(core == 0, a, b)

    a0, b0, h0, joint, ra0, rb0 = jax.tree.map(choose, own, other)
    a1, b1, h1, _, ra1, rb1 = jax.tree.map(choose, other, own)
    mid = mid_ref[...]
    inv = 1.0 / (h0 + b0 + mid)
    hd, gd = h0 * inv, mid * inv
    alpha = a0 + b0 * hd
    link = h0 * gd
    between = a1 + b0 * gd
    ra = [a + b * hd for a, b in zip(ra0, rb0)]
    rm = [a + b * gd for a, b in zip(ra1, rb0)]
    inv = 1.0 / (link + between + h1)
    hd, gd = link * inv, h1 * inv
    alpha = alpha + between * hd
    beta = b1 + between * gd
    ra = [a + m * hd for a, m in zip(ra, rm)]
    rb = [b + m * gd for b, m in zip(rb1, rm)]
    out = jnp.concatenate([*ra, *rb, pack(alpha, beta), pack(link * gd, joint)], 0)
    for d in range(send_ref.shape[0]):
        send_ref[d] = out


def y_solve_kernel(
    recv_ref, own_ref, other_ref, mid_ref, rb_ref, gy_ref, hy_ref, iy_ref, za_ref, zc_ref, zi_ref, heat_ref,
    out_ref, second,
):
    at_y = lax.axis_index("gy")
    core, chip = lax.rem(at_y, 2), lax.div(at_y, 2)
    count = recv_ref.shape[0]
    segments = [y_segment(lambda r, d=d: recv_ref[d, r : r + 8, :]) for d in range(count)]
    zero = jnp.zeros((MX, NZ), f32)
    left, left_src = zero, [zero, zero]
    right, right_src = zero, [zero, zero]
    for step in range(count - 1):
        d = step
        alpha, beta, link, _, ra, rb = segments[d]
        new, new_src = through(beta, alpha, link, segments[d + 1][3], left, rb, ra, left_src)
        left = jnp.where(d < chip, new, left)
        left_src = [jnp.where(d < chip, n, o) for n, o in zip(new_src, left_src)]
        d = count - 1 - step
        alpha, beta, link, joint, ra, rb = segments[d]
        new, new_src = through(alpha, beta, link, joint, right, ra, rb, right_src)
        right = jnp.where(d > chip, new, right)
        right_src = [jnp.where(d > chip, n, o) for n, o in zip(new_src, right_src)]

    def choose(a, b):
        return jnp.where(core == 0, a, b)

    alpha, beta, link, _, ra, rb = y_segment(lambda r: other_ref[r : r + 8, :])
    near, far = choose(alpha, beta), choose(beta, alpha)
    near_src = [choose(a, b) for a, b in zip(ra, rb)]
    far_src = [choose(b, a) for a, b in zip(ra, rb)]
    leak = choose(right, left)
    src = [choose(r, l) for r, l in zip(right_src, left_src)]
    new, new_src = through(near, far, link, mid_ref[...], leak, near_src, far_src, src)
    left, right = choose(left, new), choose(new, right)
    left_src, right_src = (
        [choose(l, n) for l, n in zip(left_src, new_src)],
        [choose(n, r) for n, r in zip(new_src, right_src)],
    )
    alpha, beta, link, _, ra, rb = y_segment(lambda r: own_ref[r : r + 8, :])
    u_first, u_next = two_nodes(
        alpha + left,
        beta + right,
        link,
        [a + s for a, s in zip(ra, left_src)],
        [b + s for b, s in zip(rb, right_src)],
    )

    def keep(y, u):
        for p in range(2):
            second[y * NX + p * MX : y * NX + (p + 1) * MX, :] = u[p]

    keep(0, u_first)
    keep(NY - 1, u_next)
    for y in range(NY - 2, 0, -1):
        t = y - 1
        gd = gy_ref[t * MX : (t + 1) * MX, :]
        hd = hy_ref[t * MX : (t + 1) * MX, :]
        inv = iy_ref[t * MX : (t + 1) * MX, :]
        b = [rb_ref[t * NX + p * MX : t * NX + (p + 1) * MX, :] for p in range(2)]
        u_next = [(inv * b[p] + hd * u_first[p]) + gd * u_next[p] for p in range(2)]
        keep(y, u_next)

    for n in range(MY):
        cells = [(2 * n + q, p) for q in range(2) for p in range(2)]
        v = [second[y * NX + p * MX : y * NX + (p + 1) * MX, :] for y, p in cells]
        for s in range(7):
            step = 1 << s
            at = s * MX * MY + n * MX
            low, high = za_ref[at : at + MX, :], zc_ref[at : at + MX, :]
            v = [w + (low * pltpu.roll(w, step, 1) + high * pltpu.roll(w, NZ - step, 1)) for w in v]
        inv = zi_ref[n * MX : (n + 1) * MX, :]
        for (y, p), w in zip(cells, v):
            where = pl.ds(p * NY + y, MX, stride=2 * NY)
            out_ref[where, :] = heat_ref[where, :] + inv * w


def call(kernel, ins, outs, scratch=(), smem=(), cost=20000):
    vm = pl.BlockSpec(memory_space=pltpu.VMEM)
    sm = pl.BlockSpec(memory_space=pltpu.SMEM)
    return pl.pallas_call(
        kernel,
        out_shape=tuple(jax.ShapeDtypeStruct(s, f32) for s in outs),
        in_specs=[sm if i in smem else vm for i in range(len(ins))],
        out_specs=tuple(vm for _ in outs),
        scratch_shapes=[pltpu.VMEM(s, f32) for s in scratch],
        cost_estimate=pl.CostEstimate(flops=cost, bytes_accessed=cost, transcendentals=0),
    )(*ins)


def on_device(starting_heat_state, material_zone_ids, zone_diffusivity_lookup):
    heat = starting_heat_state.reshape(NX * NY, NZ)
    ids = material_zone_ids.reshape(MX * MY, NZ // 2)
    nx, ny = lax.axis_size("gx"), lax.axis_size("gy")
    k, low_row, high_row = call(
        prepare_kernel,
        (ids, zone_diffusivity_lookup, heat),
        [(MX * MY, NZ), (NX + MX, NZ), (NX + MX, NZ)],
        scratch=[(MX * MY, NZ)],
        smem=(1,),
    )
    low = lax.ppermute(high_row, "gy", [(i, (i + 1) % ny) for i in range(ny)])
    high = lax.ppermute(low_row, "gy", [((i + 1) % ny, i) for i in range(ny)])
    tx, ty = NX - 2, NY - 2
    gx, hx, ix, px, gy, hy, iy, my, za, zc, zi = call(
        matrix_kernel,
        (k,),
        [(tx * MY, NZ)] * 3
        + [(40, NZ)]
        + [(ty * MX, NZ)] * 3
        + [(24, NZ)]
        + [(7 * MX * MY, NZ)] * 2
        + [(MX * MY, NZ)],
        cost=4000000,
    )
    send, rbx = call(
        right_side_kernel,
        (heat, k, low, high, gx, hx, px),
        [(nx, XROWS, NZ), (tx * NY, NZ)],
    )
    recv = lax.all_to_all(send, "gx", 0, 0)
    own, mid, rby = call(
        x_solve_kernel,
        (recv, heat, k, low, high, rbx, gx, hx, ix, gy, hy, my),
        [(YROWS, NZ), (MX, NZ), (ty * NX, NZ)],
        scratch=[(NX * NY, NZ)],
    )
    other = lax.ppermute(own, "gy", [(i, i ^ 1) for i in range(ny)])
    (send,) = call(chip_kernel, (own, other, mid), [(ny // 2, YROWS, NZ)])
    groups = [list(range(c, ny, 2)) for c in range(2)]
    recv = lax.all_to_all(send, "gy", 0, 0, axis_index_groups=groups)
    (out,) = call(
        y_solve_kernel,
        (recv, own, other, mid, rby, gy, hy, iy, za, zc, zi, heat),
        [(NX * NY, NZ)],
        scratch=[(NX * NY, NZ)],
    )
    return out.reshape(starting_heat_state.shape)


def solution(mesh):
    return jax.shard_map(
        on_device,
        mesh=mesh,
        in_specs=(P("gx", "gy", None), P("gx", "gy", None), P()),
        out_specs=P("gx", "gy", None),
        check_vma=False,
    )
```

profile of v0, /device:TPU:1, one launch (start us, length us, event | category | flops | bytes accessed | tf_op | source)
XLA Modules:
  0.0 62.1 jit_solution(5775533746369316223)
XLA Ops:
  0.0 1.8 %shard_map.37 = (f32[128,128]{1,0:T(8,128)}, f32[24,128]{1,0:T(8,128)}, f32[24,128]{1,0:T(8,128)}) custom-call(s32[128,64]{1,0:T(8,128)} %bitcast.7, f32[16]{0:T(128)} %table_ref.1, f32[512,128]{1,0:T(8,128)} %bitcast.3), custom_call_target="tpu_custom_call" | custom-call | flops 20000 | bytes 20000 | tf_op jit(solution)/shard_map/pallas_call | solution.py:399
  1.8 2.7 %collective-permute-start = (f32[24,128]{1,0:T(8,128)}, f32[24,128]{1,0:T(8,128)S(1)}, u32[]{:S(2)}, u32[]{:S(2)}) collective-permute-start(f32[24,128]{1,0:T(8,128)} %get-tuple-element.25), channel_id=1, source_target_pairs={{0,1},{1,2},{2,3},{3,4},{4,5},{5,6},{6,7},{7,8},{8,9},{9,10},{10,1... | collective-permute-start | bytes 36872 | tf_op jit(solution)/shard_map/ppermute | solution.py:420
  4.5 0.6 collective-permute-start.1
  5.0 3.2 %shard_map.38 = (f32[224,128]{1,0:T(8,128)}, f32[224,128]{1,0:T(8,128)}, f32[224,128]{1,0:T(8,128)}, f32[40,128]{1,0:T(8,128)}, f32[240,128]{1,0:T(8,128)}, /*in...) custom-call(f32[128,128]{1,0:T(8,128)} %get-tuple-element.24.k_ref), custom_call_target="tpu_custom_call" | custom-call | flops 4000000 | bytes 4000000 | tf_op jit(solution)/shard_map/pallas_call | solution.py:399
  8.2 0.0 collective-permute-done.low_ref
  8.2 0.0 copy-start.1
  8.2 0.0 collective-permute-done.1.high_ref
  8.2 0.0 copy-start.2
  8.2 0.6 copy-done.1
  8.8 0.0 copy-done.2
  8.8 2.2 %shard_map.39 = (f32[8,104,128]{2,1,0:T(8,128)}, f32[448,128]{1,0:T(8,128)}) custom-call(f32[512,128]{1,0:T(8,128)} %bitcast.4, f32[128,128]{1,0:T(8,128)} %get-tuple-element.24.k_ref, f32[24,128]{1,0:T(8,128)} %copy-done.1, f32[24,128]{1,0:T(8,128)} %copy-done.2, f32[224,128]{1,0:T(8,128)} %get-tuple-element.27.gx_ref, ...), custom_call_target="tpu_custom_call" | custom-call | flops 20000 | bytes 20000 | tf_op jit(solution)/shard_map/pallas_call | solution.py:399
  11.0 19.2 %all_to_all.10.recv_ref = f32[8,104,128]{2,1,0:T(8,128)} all-to-all(f32[8,104,128]{2,1,0:T(8,128)} %get-tuple-element.30), channel_id=1, replica_groups=mesh['gx'=8,'gy'=32] {'gx'}, dimensions={0} | all-to-all | bytes 851968 | tf_op jit(solution)/shard_map/all_to_all | solution.py:439
  30.3 2.6 %shard_map.40 = (f32[48,128]{1,0:T(8,128)}, f32[8,128]{1,0:T(8,128)}, f32[480,128]{1,0:T(8,128)}) custom-call(f32[8,104,128]{2,1,0:T(8,128)} %all_to_all.10.recv_ref, f32[512,128]{1,0:T(8,128)} %bitcast.5, f32[128,128]{1,0:T(8,128)} %get-tuple-element.24.k_ref, f32[24,128]{1,0:T(8,128)} %copy-done.1, f32[24,128]{1,0:T(8,128)} %copy-done.2, ...), custom_call_target="tpu_custom_call" | custom-call | flops 20000 | bytes 20000 | tf_op jit(solution)/shard_map/pallas_call | solution.py:399
  32.8 5.3 %collective-permute-start.2 = (f32[48,128]{1,0:T(8,128)}, f32[48,128]{1,0:T(8,128)S(1)}, u32[]{:S(2)}, u32[]{:S(2)}) collective-permute-start(f32[48,128]{1,0:T(8,128)} %get-tuple-element.36.own_ref), channel_id=1, source_target_pairs={{0,1},{1,0},{2,3},{3,2},{4,5},{5,4},{6,7},{7,6},{8,9},{9,8},{10,11... | collective-permute-start | bytes 73736 | tf_op jit(solution)/shard_map/ppermute | solution.py:446
  38.1 1.1 %collective-permute-done.2.other_ref = f32[48,128]{1,0:T(8,128)S(1)} collective-permute-done((f32[48,128]{1,0:T(8,128)}, f32[48,128]{1,0:T(8,128)S(1)}, u32[]{:S(2)}, u32[]{:S(2)}) %collective-permute-start.2) | collective-permute-done | bytes 24608 | tf_op jit(solution)/shard_map/ppermute | solution.py:446
  39.2 0.0 copy-start
  39.2 0.6 copy-done
  39.8 1.6 %shard_map.41 = f32[16,48,128]{2,1,0:T(8,128)} custom-call(f32[48,128]{1,0:T(8,128)} %get-tuple-element.36.own_ref, f32[48,128]{1,0:T(8,128)} %copy-done, f32[8,128]{1,0:T(8,128)} %get-tuple-element.37.mid_ref), custom_call_target="tpu_custom_call" | custom-call | flops 20000 | bytes 20000 | tf_op jit(solution)/shard_map/pallas_call | solution.py:399
  41.4 16.8 %all_to_all.11.recv_ref = f32[16,48,128]{2,1,0:T(8,128)} all-to-all(f32[16,48,128]{2,1,0:T(8,128)} %shard_map.41), channel_id=1, replica_groups={{0,2,4,6,8,10,12,14,16,18,20,22,24,26,28,30},{1,3,5,7,9,11,13,15,17,19,..., dimensions={0} | all-to-all | bytes 786432 | tf_op jit(solution)/shard_map/all_to_all | solution.py:449
  58.2 3.9 %shard_map.42 = f32[512,128]{1,0:T(8,128)} custom-call(f32[16,48,128]{2,1,0:T(8,128)} %all_to_all.11.recv_ref, f32[48,128]{1,0:T(8,128)} %get-tuple-element.36.own_ref, f32[48,128]{1,0:T(8,128)} %copy-done, f32[8,128]{1,0:T(8,128)} %get-tuple-element.37.mid_ref, f32[480,128]{1,0:T(8,128)} %get-tuple-element.38.rb_ref, f32[240,128]{1,0:T(8,128)} %get-tuple-element.33.gy_ref, ...), custom_call_target="tpu_custom_call" | custom-call | flops 20000 | bytes 20000 | tf_op jit(solution)/shard_map/pallas_call | solution.py:399
Async XLA Ops:
  1.8 6.4 %collective-permute-start = (f32[24,128]{1,0:T(8,128)}, f32[24,128]{1,0:T(8,128)S(1)}, u32[]{:S(2)}, u32[]{:S(2)}) collective-permute-start(f32[24,128]{1,0:T(8,128)} %get-tuple-element.25), channel_id=1, source_target_pairs={{0,1},{1,2},{2,3},{3,4},{4,5},{5,6},{6,7},{7,8},{8,9},{9,10},{10,1... | collective-permute-start | bytes 36872 | tf_op jit(solution)/shard_map/ppermute | solution.py:420
  4.5 3.7 %collective-permute-start.1 = (f32[24,128]{1,0:T(8,128)}, f32[24,128]{1,0:T(8,128)S(1)}, u32[]{:S(2)}, u32[]{:S(2)}) collective-permute-start(f32[24,128]{1,0:T(8,128)} %get-tuple-element.26), channel_id=1, source_target_pairs={{1,0},{2,1},{3,2},{4,3},{5,4},{6,5},{7,6},{8,7},{9,8},{10,9},{11,1... | collective-permute-start | bytes 36872 | tf_op jit(solution)/shard_map/ppermute | solution.py:421
  8.2 0.6 copy-start.1
  8.2 0.6 copy-start.2
  32.8 6.3 %collective-permute-start.2 = (f32[48,128]{1,0:T(8,128)}, f32[48,128]{1,0:T(8,128)S(1)}, u32[]{:S(2)}, u32[]{:S(2)}) collective-permute-start(f32[48,128]{1,0:T(8,128)} %get-tuple-element.36.own_ref), channel_id=1, source_target_pairs={{0,1},{1,0},{2,3},{3,2},{4,5},{5,4},{6,7},{7,6},{8,9},{9,8},{10,11... | collective-permute-start | bytes 73736 | tf_op jit(solution)/shard_map/ppermute | solution.py:446
  39.2 0.6 copy-start
where the time goes:
time: 62.6 us; the launch traced here: 62.1 us
  blocking collectives  36 us (58%)
  Pallas kernels  15.3 us (24%)
  starting transfers between devices  8.5 us (14%)
  local copies, waits for them, and re-layouts  1.19 us (2%)
  waiting for transfers between devices  1.07 us (2%)
    all_to_all x1, blocking collectives, on_device(): recv = lax.all_to_all(send, 'gx', 0, 0)  19.2 us
    all_to_all x1, blocking collectives, on_device(): recv = lax.all_to_all(send, 'gy', 0, 0, axis_index_groups=groups)  16.8 us
    pallas_call x6, Pallas kernels, call(): pl.pallas_call(kernel, out_shape=tuple((jax.ShapeDtypeStruct(s, f32) for...  15.3 us
    ppermute x1, starting transfers between devices, on_device(): other = lax.ppermute(own, 'gy', [(i, i ^ 1) for i in range(ny)])  5.26 us
    ppermute x1, starting transfers between devices, on_device(): low = lax.ppermute(high_row, 'gy', [(i, (i + 1) % ny) for i in range(ny)])  2.69 us
  transfers between devices with their start and end apart: 3, of which 1 were waited for; matrix products, arithmetic and copies ran while one was open for 0% of the time, Pallas kernels for 5%

commit v1 on v0

--- a/solution.py
+++ b/solution.py
@@ -402,6 +402,7 @@
         in_specs=[sm if i in smem else vm for i in range(len(ins))],
         out_specs=tuple(vm for _ in outs),
         scratch_shapes=[pltpu.VMEM(s, f32) for s in scratch],
+        compiler_params=pltpu.CompilerParams(vmem_limit_bytes=8 << 20),
         cost_estimate=pl.CostEstimate(flops=cost, bytes_accessed=cost, transcendentals=0),
     )(*ins)
 

time: 62.6 us -> 53.1 us (0.85)
  Pallas kernels: 15.3 us -> 5.05 us
  local copies, waits for them, and re-layouts: 1.19 us -> 2.45 us
  waiting for transfers between devices: 1.07 us -> 2.16 us
  starting transfers between devices: 8.5 us -> 7.65 us
    pallas_call x6, Pallas kernels: 15.3 us -> 5.05 us  [call(): pl.pallas_call(kernel, out_shape=tuple((jax.ShapeDtypeStruct(s, f32) for...]
    all_to_all x1, blocking collectives: 16.8 us -> 15.1 us  [on_device(): recv = lax.all_to_all(send, 'gy', 0, 0, axis_index_groups=groups)]
    ppermute x1, waiting for transfers between devices: 0.01 us -> 1.31 us  [on_device(): high = lax.ppermute(low_row, 'gy', [((i + 1) % ny, i) for i in range(ny)])]
    unnamed x6 -> x8, local copies, waits for them, and re-layouts: 1.19 us -> 2.45 us
    all_to_all x1, blocking collectives: 19.2 us -> 20.4 us  [on_device(): recv = lax.all_to_all(send, 'gx', 0, 0)]
    ppermute x1, starting transfers between devices: 5.26 us -> 4.26 us  [on_device(): other = lax.ppermute(own, 'gy', [(i, i ^ 1) for i in range(ny)])]
  transfers between devices with their start and end apart: 3 -> 3, of which waited for: 1 -> 2; matrix products, arithmetic and copies ran while one was open for 0% -> 0% of each run, Pallas kernels for 5% -> 2%
where the time goes in v1:
time: 53.1 us; the launch traced here: 52.9 us
  blocking collectives  35.5 us (67%)
  starting transfers between devices  7.65 us (14%)
  Pallas kernels  5.05 us (10%)
  local copies, waits for them, and re-layouts  2.45 us (5%)
  waiting for transfers between devices  2.16 us (4%)
    all_to_all x1, blocking collectives, on_device(): recv = lax.all_to_all(send, 'gx', 0, 0)  20.4 us
    all_to_all x1, blocking collectives, on_device(): recv = lax.all_to_all(send, 'gy', 0, 0, axis_index_groups=groups)  15.1 us
    pallas_call x6, Pallas kernels, call(): pl.pallas_call(kernel, out_shape=tuple((jax.ShapeDtypeStruct(s, f32) for...  5.05 us
    ppermute x1, starting transfers between devices, on_device(): other = lax.ppermute(own, 'gy', [(i, i ^ 1) for i in range(ny)])  4.26 us
    ppermute x1, starting transfers between devices, on_device(): low = lax.ppermute(high_row, 'gy', [(i, (i + 1) % ny) for i in range(ny)])  2.74 us
    unnamed x8, local copies, waits for them, and re-layouts  2.45 us
    ppermute x1, waiting for transfers between devices, on_device(): high = lax.ppermute(low_row, 'gy', [((i + 1) % ny, i) for i in range(ny)])  1.31 us
  transfers between devices with their start and end apart: 3, of which 2 were waited for; matrix products, arithmetic and copies ran while one was open for 0% of the time, Pallas kernels for 2%

profile of v1, /device:TPU:1, one launch (start us, length us, event | category | flops | bytes accessed | tf_op | source)
XLA Modules:
  0.0 52.9 jit_solution(10037112949226514935)
XLA Ops:
  0.0 0.0 copy-start.3
  0.0 0.7 %copy-done.3 = f32[16]{0:T(128)S(1)} copy-done((f32[16]{0:T(128)S(1)}, f32[16]{0:T(128)}, u32[]{:S(2)}) %copy-start.3) | copy-done | bytes 88
  0.7 0.0 copy-start
  0.7 0.9 %copy-done = f32[16,32,128]{2,1,0:T(8,128)S(1)} copy-done((f32[16,32,128]{2,1,0:T(8,128)S(1)}, f32[16,32,128]{2,1,0:T(8,128)}, u32[]{:S(2)}) %copy-start) | copy-done | bytes 262168
  1.6 0.0 copy-start.2
  1.6 0.8 %copy-done.2 = s32[8,16,64]{2,1,0:T(8,128)S(1)} copy-done((s32[8,16,64]{2,1,0:T(8,128)S(1)}, s32[8,16,64]{2,1,0:T(8,128)}, u32[]{:S(2)}) %copy-start.2) | copy-done | bytes 32792
  2.4 0.0 copy-start.1
  2.4 0.7 %shard_map.37 = (f32[128,128]{1,0:T(8,128)S(1)}, f32[24,128]{1,0:T(8,128)S(1)}, f32[24,128]{1,0:T(8,128)S(1)}) custom-call(s32[128,64]{1,0:T(8,128)S(1)} %bitcast.7, f32[16]{0:T(128)S(1)} %copy-done.3, f32[512,128]{1,0:T(8,128)S(1)} %bitcast.3), custom_call_target="tpu_custom_call" | custom-call | flops 20000 | bytes 20000 | tf_op jit(solution)/shard_map/pallas_call | solution.py:399
  3.2 2.7 %collective-permute-start = (f32[24,128]{1,0:T(8,128)S(1)}, f32[24,128]{1,0:T(8,128)S(1)}, u32[]{:S(2)}, u32[]{:S(2)}) collective-permute-start(f32[24,128]{1,0:T(8,128)S(1)} %get-tuple-element.25), channel_id=1, source_target_pairs={{0,1},{1,2},{2,3},{3,4},{4,5},{5,6},{6,7},{7,8},{8,9},{9,10},{10,1... | collective-permute-start | bytes 36872 | tf_op jit(solution)/shard_map/ppermute | solution.py:421
  5.9 0.6 %collective-permute-start.1 = (f32[24,128]{1,0:T(8,128)S(1)}, f32[24,128]{1,0:T(8,128)S(1)}, u32[]{:S(2)}, u32[]{:S(2)}) collective-permute-start(f32[24,128]{1,0:T(8,128)S(1)} %get-tuple-element.26), channel_id=1, source_target_pairs={{1,0},{2,1},{3,2},{4,3},{5,4},{6,5},{7,6},{8,7},{9,8},{10,9},{11,1... | collective-permute-start | bytes 36872 | tf_op jit(solution)/shard_map/ppermute | solution.py:422
  6.6 1.2 %shard_map.38 = (f32[224,128]{1,0:T(8,128)S(1)}, f32[224,128]{1,0:T(8,128)S(1)}, f32[224,128]{1,0:T(8,128)S(1)}, f32[40,128]{1,0:T(8,128)S(1)}, f32[240,128]{1,0...) custom-call(f32[128,128]{1,0:T(8,128)S(1)} %get-tuple-element.24.k_ref), custom_call_target="tpu_custom_call" | custom-call | flops 4000000 | bytes 4000000 | tf_op jit(solution)/shard_map/pallas_call | solution.py:399
  7.7 0.0 collective-permute-done.low_ref
  7.7 1.3 %collective-permute-done.1.high_ref = f32[24,128]{1,0:T(8,128)S(1)} collective-permute-done((f32[24,128]{1,0:T(8,128)S(1)}, f32[24,128]{1,0:T(8,128)S(1)}, u32[]{:S(2)}, u32[]{:S(2)}) %collective-permute-start.1) | collective-permute-done | bytes 12320 | tf_op jit(solution)/shard_map/ppermute | solution.py:422
  9.0 0.0 copy-done.1
  9.0 0.3 shard_map.39
  9.3 20.4 %all_to_all.10.recv_ref = f32[8,104,128]{2,1,0:T(8,128)S(1)} all-to-all(f32[8,104,128]{2,1,0:T(8,128)S(1)} %get-tuple-element.30), channel_id=1, replica_groups=mesh['gx'=8,'gy'=32] {'gx'}, dimensions={0} | all-to-all | bytes 851968 | tf_op jit(solution)/shard_map/all_to_all | solution.py:440
  29.8 0.5 shard_map.40
  30.2 4.3 %collective-permute-start.2 = (f32[48,128]{1,0:T(8,128)S(1)}, f32[48,128]{1,0:T(8,128)S(1)}, u32[]{:S(2)}, u32[]{:S(2)}) collective-permute-start(f32[48,128]{1,0:T(8,128)S(1)} %get-tuple-element.36.own_ref), channel_id=1, source_target_pairs={{0,1},{1,0},{2,3},{3,2},{4,5},{5,4},{6,7},{7,6},{8,9},{9,8},{10,11... | collective-permute-start | bytes 73736 | tf_op jit(solution)/shard_map/ppermute | solution.py:447
  34.5 0.8 %collective-permute-done.2.other_ref = f32[48,128]{1,0:T(8,128)S(1)} collective-permute-done((f32[48,128]{1,0:T(8,128)S(1)}, f32[48,128]{1,0:T(8,128)S(1)}, u32[]{:S(2)}, u32[]{:S(2)}) %collective-permute-start.2) | collective-permute-done | bytes 24608 | tf_op jit(solution)/shard_map/ppermute | solution.py:447
  35.3 0.1 shard_map.41
  35.5 15.1 %all_to_all.11.recv_ref = f32[16,48,128]{2,1,0:T(8,128)S(1)} all-to-all(f32[16,48,128]{2,1,0:T(8,128)S(1)} %shard_map.41), channel_id=1, replica_groups={{0,2,4,6,8,10,12,14,16,18,20,22,24,26,28,30},{1,3,5,7,9,11,13,15,17,19,..., dimensions={0} | all-to-all | bytes 786432 | tf_op jit(solution)/shard_map/all_to_all | solution.py:450
  50.6 2.3 %shard_map.42 = f32[512,128]{1,0:T(8,128)} custom-call(f32[16,48,128]{2,1,0:T(8,128)S(1)} %all_to_all.11.recv_ref, f32[48,128]{1,0:T(8,128)S(1)} %get-tuple-element.36.own_ref, f32[48,128]{1,0:T(8,128)S(1)} %collective-permute-done.2.other_ref, f32[8,128]{1,0:T(8,128)S(1)} %get-tuple-element.37.mid_ref, f32[480,128]{1,0:T(8,128)S(1)} %get-tuple-element.38.rb_ref, ...), custom_call_target="tpu_custom_call" | custom-call | flops 20000 | bytes 20000 | tf_op jit(solution)/shard_map/pallas_call | solution.py:399
Async XLA Ops:
  0.0 0.7 %copy-start.3 = (f32[16]{0:T(128)S(1)}, f32[16]{0:T(128)}, u32[]{:S(2)}) copy-start(f32[16]{0:T(128)} %table_ref.1) | copy-start | bytes 196
  0.7 0.9 %copy-start = (f32[16,32,128]{2,1,0:T(8,128)S(1)}, f32[16,32,128]{2,1,0:T(8,128)}, u32[]{:S(2)}) copy-start(f32[16,32,128]{2,1,0:T(8,128)} %param.3) | copy-start | bytes 786436
  1.6 0.8 %copy-start.2 = (s32[8,16,64]{2,1,0:T(8,128)S(1)}, s32[8,16,64]{2,1,0:T(8,128)}, u32[]{:S(2)}) copy-start(s32[8,16,64]{2,1,0:T(8,128)} %param.4) | copy-start | bytes 98308
  2.4 6.6 %copy-start.1 = (f32[16,32,128]{2,1,0:T(8,128)S(1)}, f32[16,32,128]{2,1,0:T(8,128)}, u32[]{:S(2)}) copy-start(f32[16,32,128]{2,1,0:T(8,128)} %param.3) | copy-start | bytes 786436
  3.2 4.5 %collective-permute-start = (f32[24,128]{1,0:T(8,128)S(1)}, f32[24,128]{1,0:T(8,128)S(1)}, u32[]{:S(2)}, u32[]{:S(2)}) collective-permute-start(f32[24,128]{1,0:T(8,128)S(1)} %get-tuple-element.25), channel_id=1, source_target_pairs={{0,1},{1,2},{2,3},{3,4},{4,5},{5,6},{6,7},{7,8},{8,9},{9,10},{10,1... | collective-permute-start | bytes 36872 | tf_op jit(solution)/shard_map/ppermute | solution.py:421
  5.9 3.1 %collective-permute-start.1 = (f32[24,128]{1,0:T(8,128)S(1)}, f32[24,128]{1,0:T(8,128)S(1)}, u32[]{:S(2)}, u32[]{:S(2)}) collective-permute-start(f32[24,128]{1,0:T(8,128)S(1)} %get-tuple-element.26), channel_id=1, source_target_pairs={{1,0},{2,1},{3,2},{4,3},{5,4},{6,5},{7,6},{8,7},{9,8},{10,9},{11,1... | collective-permute-start | bytes 36872 | tf_op jit(solution)/shard_map/ppermute | solution.py:422
  30.2 5.1 %collective-permute-start.2 = (f32[48,128]{1,0:T(8,128)S(1)}, f32[48,128]{1,0:T(8,128)S(1)}, u32[]{:S(2)}, u32[]{:S(2)}) collective-permute-start(f32[48,128]{1,0:T(8,128)S(1)} %get-tuple-element.36.own_ref), channel_id=1, source_target_pairs={{0,1},{1,0},{2,3},{3,2},{4,5},{5,4},{6,7},{7,6},{8,9},{9,8},{10,11... | collective-permute-start | bytes 73736 | tf_op jit(solution)/shard_map/ppermute | solution.py:447

commit v2 on v1

--- a/solution.py
+++ b/solution.py
@@ -64,19 +64,33 @@
     return alpha, beta, link
 
 
-def prepare_kernel(ids_ref, table_ref, heat_ref, k_ref, low_ref, high_ref, wide):
+def prepare_kernel(
+    ids_hbm, table_hbm, heat_hbm, k_ref, inner_ref, outer_ref, heat_ref, ids_ref, table_ref, wide, sems
+):
+    copies = [
+        pltpu.make_async_copy(table_hbm, table_ref, sems.at[0]),
+        pltpu.make_async_copy(ids_hbm, ids_ref, sems.at[1]),
+        pltpu.make_async_copy(heat_hbm, heat_ref, sems.at[2]),
+    ]
+    for copy in copies:
+        copy.start()
+    wide[...] = jnp.zeros(wide.shape, f32)
+    copies[0].wait()
+    copies[1].wait()
     ids = ids_ref[...]
     k = jnp.zeros(ids.shape, f32)
     for region in range(table_ref.shape[0]):
         k = jnp.where(ids == region, table_ref[region], k)
-    wide[...] = jnp.zeros(wide.shape, f32)
     wide[:, : NZ // 2] = k
     index = lanes(wide.shape) // 2
     k_ref[...] = jnp.take_along_axis(wide[...], index, axis=1, mode="promise_in_bounds")
-    low_ref[:NX] = heat_ref[pl.ds(0, NX, stride=NY), :]
-    high_ref[:NX] = heat_ref[pl.ds(NY - 1, NX, stride=NY), :]
-    low_ref[NX:] = k_ref[pl.ds(0, MX, stride=MY), :]
-    high_ref[NX:] = k_ref[pl.ds(MY - 1, MX, stride=MY), :]
+    copies[2].wait()
+    low = [heat_ref[pl.ds(0, NX, stride=NY), :], k_ref[pl.ds(0, MX, stride=MY), :]]
+    high = [heat_ref[pl.ds(NY - 1, NX, stride=NY), :], k_ref[pl.ds(MY - 1, MX, stride=MY), :]]
+    core = lax.rem(lax.axis_index("gy"), 2)
+    low, high = jnp.concatenate(low, 0), jnp.concatenate(high, 0)
+    inner_ref[...] = jnp.where(core == 0, high, low)
+    outer_ref[...] = jnp.where(core == 0, low, high)
 
 
 def matrix_kernel(
@@ -143,18 +157,20 @@
         zi_ref[start * MX : start * MX + size, :] = 1.0 / diag
 
 
-def right_side_kernel(heat_ref, k_ref, low_ref, high_ref, gx_ref, hx_ref, px_ref, send_ref, rb_ref):
+def right_side_kernel(heat_ref, k_ref, inner_ref, outer_ref, gx_ref, hx_ref, px_ref, send_ref, rb_ref):
     at_y = lax.axis_index("gy")
-    inside_low = jnp.where(at_y == 0, 0.0, 1.0)
-    inside_high = jnp.where(at_y == lax.axis_size("gy") - 1, 0.0, 1.0)
+    core = lax.rem(at_y, 2)
+    inner, outer = inner_ref[...], outer_ref[...]
+    low = jnp.where(at_y == 0, 0.0, jnp.where(core == 0, outer, inner))
+    high = jnp.where(at_y == lax.axis_size("gy") - 1, 0.0, jnp.where(core == 0, inner, outer))
     shape = (MY, NZ)
     lane, row = lanes(shape), rows_of(shape)
     ra = None
     rb = None
     for m in range(MX):
         k = k_ref[m * MY : (m + 1) * MY, :]
-        k_low = inside_low * low_ref[NX + m : NX + m + 1, :]
-        k_high = inside_high * high_ref[NX + m : NX + m + 1, :]
+        k_low = low[NX + m : NX + m + 1]
+        k_high = high[NX + m : NX + m + 1]
         face_low = 2000.0 * (k + jnp.where(row == 0, k_low, pltpu.roll(k, 1, 0)))
         face_high = 2000.0 * (k + jnp.where(row == MY - 1, k_high, pltpu.roll(k, MY - 1, 0)))
         face_mid = 4000.0 * k
@@ -166,10 +182,8 @@
         for x in (2 * m, 2 * m + 1):
             even = heat_ref[pl.ds(x * NY, MY, stride=2), :]
             odd = heat_ref[pl.ds(x * NY + 1, MY, stride=2), :]
-            before = jnp.where(row == 0, inside_low * low_ref[x : x + 1, :], pltpu.roll(odd, 1, 0))
-            after = jnp.where(
-                row == MY - 1, inside_high * high_ref[x : x + 1, :], pltpu.roll(even, MY - 1, 0)
-            )
+            before = jnp.where(row == 0, low[x : x + 1], pltpu.roll(odd, 1, 0))
+            after = jnp.where(row == MY - 1, high[x : x + 1], pltpu.roll(even, MY - 1, 0))
             flow = face_mid * (odd - even)
             r = []
             for v, along_y in (
@@ -190,47 +204,94 @@
                     rb_ref[t * NY + q * MY : t * NY + (q + 1) * MY, :] = rb[q]
                 ra = [a + b * hd for a, b in zip(ra, rb)]
                 rb = [n + b * gd for n, b in zip(r, rb)]
-    p = px_ref[...]
-    for d in range(send_ref.shape[0]):
-        send_ref[d, 0:16, :] = ra[0]
-        send_ref[d, 16:32, :] = ra[1]
-        send_ref[d, 32:48, :] = rb[0]
-        send_ref[d, 48:64, :] = rb[1]
-        send_ref[d, 64:104, :] = p
+    send_ref[0:16, :] = ra[0]
+    send_ref[16:32, :] = ra[1]
+    send_ref[32:48, :] = rb[0]
+    send_ref[48:64, :] = rb[1]
+    send_ref[64:104, :] = px_ref[...]
+
+
+def x_segment(rows):
+    alpha, beta = unpack(rows[64:80])
+    link, k_first = unpack(rows[80:96])
+    k_last = jnp.concatenate(unpack(rows[96:104]), 0)
+    return alpha, beta, link, k_first, k_last, [rows[0:16], rows[16:32]], [rows[32:48], rows[48:64]]
+
+
+def x_quarter(place, refs):
+    held = [r[...] for r in refs]
+    segments = []
+    for d in range(4):
+        rows = held[0]
+        for j in range(1, 4):
+            rows = jnp.where(place == d ^ j, held[j], rows)
+        segments.append(x_segment(rows))
+    return segments
+
+
+def x_half_kernel(own_ref, one_ref, two_ref, three_ref, send_ref):
+    at = lax.axis_index("gx")
+    upper = at >= 4
+    place = lax.rem(at, 4)
+    place = jnp.where(upper, 3 - place, place)
+
+    def turn(segment):
+        alpha, beta, link, k_first, k_last, ra, rb = segment
+
+        def pick(a, b):
+            return jnp.where(upper, a, b)
+
+        near, far = pick(alpha, beta), pick(beta, alpha)
+        k_near, k_far = pick(k_first, k_last), pick(k_last, k_first)
+        near_src = [pick(a, b) for a, b in zip(ra, rb)]
+        far_src = [pick(b, a) for a, b in zip(ra, rb)]
+        return near, far, link, k_near, k_far, near_src, far_src
+
+    segments = [turn(g) for g in x_quarter(place, (own_ref, one_ref, two_ref, three_ref))]
+    zero = jnp.zeros((MY, NZ), f32)
+    leak, src = zero, [zero, zero]
+    for d in range(3):
+        near, far, link, k_near, _, near_src, far_src = segments[d]
+        joint = 1000.0 * (k_near + segments[d + 1][4])
+        leak, src = through(near, far, link, joint, leak, near_src, far_src, src)
+    near, far, link, k_near, _, near_src, far_src = segments[3]
+    total = far + leak
+    part = link / (total + link)
+    send_ref[0:16, :] = near_src[0] + (far_src[0] + src[0]) * part
+    send_ref[16:32, :] = near_src[1] + (far_src[1] + src[1]) * part
+    send_ref[32:48, :] = pack(near + total * part, k_near)
 
 
 def x_solve_kernel(
-    recv_ref, heat_ref, k_ref, low_ref, high_ref, rb_ref, gx_ref, hx_ref, ix_ref, gy_ref, hy_ref, my_ref,
-    core_ref, mid_ref, rby_ref, first,
+    own_ref, one_ref, two_ref, three_ref, half_ref, heat_ref, k_ref, inner_ref, outer_ref, rb_ref, gx_ref,
+    hx_ref, ix_ref, gy_ref, hy_ref, my_ref, core_ref, mid_ref, rby_ref, first,
 ):
     at = lax.axis_index("gx")
-    count = recv_ref.shape[0]
-
-    def segment(d):
-        alpha, beta = unpack(recv_ref[d, 64:80, :])
-        link, k_first = unpack(recv_ref[d, 80:96, :])
-        k_last = jnp.concatenate(unpack(recv_ref[d, 96:104, :]), 0)
-        ra = [recv_ref[d, 0:16, :], recv_ref[d, 16:32, :]]
-        rb = [recv_ref[d, 32:48, :], recv_ref[d, 48:64, :]]
-        return alpha, beta, link, k_first, k_last, ra, rb
-
-    segments = [segment(d) for d in range(count)]
-    joints = [1000.0 * (segments[d][4] + segments[d + 1][3]) for d in range(count - 1)]
-    zero = jnp.zeros((MY, NZ), f32)
-    left, left_src = zero, [zero, zero]
-    right, right_src = zero, [zero, zero]
-    for step in range(count - 1):
+    place = lax.rem(at, 4)
+    segments = x_quarter(place, (own_ref, one_ref, two_ref, three_ref))
+    half_leak, half_k = unpack(half_ref[32:48, :])
+    upper = at >= 4
+    joint = 1000.0 * (half_k + jnp.where(upper, segments[0][3], segments[3][4]))
+    part = joint / (half_leak + joint)
+    half_leak = half_leak * part
+    half_src = [half_ref[0:16, :] * part, half_ref[16:32, :] * part]
+    left = jnp.where(upper, half_leak, 0.0)
+    left_src = [jnp.where(upper, v, 0.0) for v in half_src]
+    right = jnp.where(upper, 0.0, half_leak)
+    right_src = [jnp.where(upper, 0.0, v) for v in half_src]
+    joints = [1000.0 * (segments[d][4] + segments[d + 1][3]) for d in range(3)]
+    for step in range(3):
         d = step
         alpha, beta, link, _, _, ra, rb = segments[d]
         new, new_src = through(beta, alpha, link, joints[d], left, rb, ra, left_src)
-        left = jnp.where(d < at, new, left)
-        left_src = [jnp.where(d < at, n, o) for n, o in zip(new_src, left_src)]
-        d = count - 1 - step
+        left = jnp.where(d < place, new, left)
+        left_src = [jnp.where(d < place, n, o) for n, o in zip(new_src, left_src)]
+        d = 3 - step
         alpha, beta, link, _, _, ra, rb = segments[d]
         new, new_src = through(alpha, beta, link, joints[d - 1], right, ra, rb, right_src)
-        right = jnp.where(d > at, new, right)
-        right_src = [jnp.where(d > at, n, o) for n, o in zip(new_src, right_src)]
-    alpha, beta, link, _, _, ra, rb = segment(at)
+        right = jnp.where(d > place, new, right)
+        right_src = [jnp.where(d > place, n, o) for n, o in zip(new_src, right_src)]
+    alpha, beta, link, _, _, ra, rb = x_segment(own_ref[...])
     u_first, u_next = two_nodes(
         alpha + left,
         beta + right,
@@ -270,10 +331,10 @@
         ra = [a + b * hd for a, b in zip(ra, rb)]
         rb = [n + b * gd for n, b in zip(new, rb)]
     core = lax.rem(lax.axis_index("gy"), 2)
-    joint_low = 1000.0 * (low_ref[NX:, :] + k_ref[pl.ds(0, MX, stride=MY), :])
-    joint_high = 1000.0 * (high_ref[NX:, :] + k_ref[pl.ds(MY - 1, MX, stride=MY), :])
-    mid_ref[...] = jnp.where(core == 0, joint_high, joint_low)
-    outer = jnp.where(core == 0, joint_low, joint_high)
+    k_low = k_ref[pl.ds(0, MX, stride=MY), :]
+    k_high = k_ref[pl.ds(MY - 1, MX, stride=MY), :]
+    mid_ref[...] = 1000.0 * (inner_ref[NX:, :] + jnp.where(core == 0, k_high, k_low))
+    outer = 1000.0 * (outer_ref[NX:, :] + jnp.where(core == 0, k_low, k_high))
     core_ref[0:8, :] = ra[0]
     core_ref[8:16, :] = ra[1]
     core_ref[16:24, :] = rb[0]
@@ -393,15 +454,14 @@
             out_ref[where, :] = heat_ref[where, :] + inv * w
 
 
-def call(kernel, ins, outs, scratch=(), smem=(), cost=20000):
-    vm = pl.BlockSpec(memory_space=pltpu.VMEM)
-    sm = pl.BlockSpec(memory_space=pltpu.SMEM)
+def call(kernel, ins, outs, scratch=(), outside=False, cost=20000):
+    space = pltpu.HBM if outside else pltpu.VMEM
     return pl.pallas_call(
         kernel,
         out_shape=tuple(jax.ShapeDtypeStruct(s, f32) for s in outs),
-        in_specs=[sm if i in smem else vm for i in range(len(ins))],
-        out_specs=tuple(vm for _ in outs),
-        scratch_shapes=[pltpu.VMEM(s, f32) for s in scratch],
+        in_specs=[pl.BlockSpec(memory_space=space) for _ in ins],
+        out_specs=tuple(pl.BlockSpec(memory_space=pltpu.VMEM) for _ in outs),
+        scratch_shapes=scratch,
         compiler_params=pltpu.CompilerParams(vmem_limit_bytes=8 << 20),
         cost_estimate=pl.CostEstimate(flops=cost, bytes_accessed=cost, transcendentals=0),
     )(*ins)
@@ -411,15 +471,21 @@
     heat = starting_heat_state.reshape(NX * NY, NZ)
     ids = material_zone_ids.reshape(MX * MY, NZ // 2)
     nx, ny = lax.axis_size("gx"), lax.axis_size("gy")
-    k, low_row, high_row = call(
+    k, inner, outer, heat = call(
         prepare_kernel,
         (ids, zone_diffusivity_lookup, heat),
-        [(MX * MY, NZ), (NX + MX, NZ), (NX + MX, NZ)],
-        scratch=[(MX * MY, NZ)],
-        smem=(1,),
-    )
-    low = lax.ppermute(high_row, "gy", [(i, (i + 1) % ny) for i in range(ny)])
-    high = lax.ppermute(low_row, "gy", [((i + 1) % ny, i) for i in range(ny)])
+        [(MX * MY, NZ), (NX + MX, NZ), (NX + MX, NZ), (NX * NY, NZ)],
+        scratch=[
+            pltpu.VMEM(ids.shape, jnp.int32),
+            pltpu.SMEM(zone_diffusivity_lookup.shape, f32),
+            pltpu.VMEM((MX * MY, NZ), f32),
+            pltpu.SemaphoreType.DMA((3,)),
+        ],
+        outside=True,
+    )
+    cores = [(i, i ^ 1) for i in range(ny)]
+    outer = lax.ppermute(outer, "gy", [(i, (i + (1 if i % 2 else -1)) % ny) for i in range(ny)])
+    inner = lax.ppermute(inner, "gy", cores)
     tx, ty = NX - 2, NY - 2
     gx, hx, ix, px, gy, hy, iy, my, za, zc, zi = call(
         matrix_kernel,
@@ -434,17 +500,19 @@
     )
     send, rbx = call(
         right_side_kernel,
-        (heat, k, low, high, gx, hx, px),
-        [(nx, XROWS, NZ), (tx * NY, NZ)],
-    )
-    recv = lax.all_to_all(send, "gx", 0, 0)
+        (heat, k, inner, outer, gx, hx, px),
+        [(XROWS, NZ), (tx * NY, NZ)],
+    )
+    quarter = [send] + [lax.ppermute(send, "gx", [(i, i ^ d) for i in range(nx)]) for d in (1, 2, 3)]
+    (half,) = call(x_half_kernel, quarter, [(48, NZ)])
+    half = lax.ppermute(half, "gx", [(i, nx - 1 - i) for i in range(nx)])
     own, mid, rby = call(
         x_solve_kernel,
-        (recv, heat, k, low, high, rbx, gx, hx, ix, gy, hy, my),
-        [(YROWS, NZ), (MX, NZ), (ty * NX, NZ)],
-        scratch=[(NX * NY, NZ)],
-    )
-    other = lax.ppermute(own, "gy", [(i, i ^ 1) for i in range(ny)])
+        (*quarter, half, heat, k, inner, outer, rbx, gx, hx, ix, gy, hy, my),
+        [(YROWS, NZ), (MX, NZ), (ty * MX * 2, NZ)],
+        scratch=[pltpu.VMEM((NX * NY, NZ), f32)],
+    )
+    other = lax.ppermute(own, "gy", cores)
     (send,) = call(chip_kernel, (own, other, mid), [(ny // 2, YROWS, NZ)])
     groups = [list(range(c, ny, 2)) for c in range(2)]
     recv = lax.all_to_all(send, "gy", 0, 0, axis_index_groups=groups)
@@ -452,7 +520,7 @@
         y_solve_kernel,
         (recv, own, other, mid, rby, gy, hy, iy, za, zc, zi, heat),
         [(NX * NY, NZ)],
-        scratch=[(NX * NY, NZ)],
+        scratch=[pltpu.VMEM((NX * NY, NZ), f32)],
     )
     return out.reshape(starting_heat_state.shape)
 

time: 53.1 us -> 44.8 us (0.84)
  the two profiles are of different devices: /device:TPU:1 before, /device:TPU:32 now
where the time goes in v2:
time: 44.8 us; the launch traced here: 44.3 us
  starting transfers between devices  15.6 us (35%)
  blocking collectives  14.3 us (32%)
  waiting for transfers between devices  6.64 us (15%)
  Pallas kernels  5.15 us (11%)
  local copies, waits for them, and re-layouts  2.44 us (5%)
    all_to_all x1, blocking collectives, on_device(): recv = lax.all_to_all(send, 'gy', 0, 0, axis_index_groups=groups)  14.3 us
    ppermute x1, starting transfers between devices, on_device(): lax.ppermute(outer, 'gy', [(i, (i + (1 if i % 2 else -1)) % ny) for i in...  5.31 us
    ppermute x1, starting transfers between devices, on_device(): half = lax.ppermute(half, 'gx', [(i, nx - 1 - i) for i in range(nx)])  5.29 us
    pallas_call x7, Pallas kernels, call(): pl.pallas_call(kernel, out_shape=tuple((jax.ShapeDtypeStruct(s, f32) for...  5.15 us
    ppermute x3, starting transfers between devices, on_device(): lax.ppermute(send, 'gx', [(i, i ^ d) for i in range(nx)])  4.82 us
    ppermute x3, waiting for transfers between devices, on_device(): lax.ppermute(send, 'gx', [(i, i ^ d) for i in range(nx)])  3.42 us
    unnamed x6, local copies, waits for them, and re-layouts  2.44 us
    ppermute x1, waiting for transfers between devices, on_device(): half = lax.ppermute(half, 'gx', [(i, nx - 1 - i) for i in range(nx)])  1.81 us
  transfers between devices with their start and end apart: 7, of which 5 were waited for; matrix products, arithmetic and copies ran while one was open for 0% of the time, Pallas kernels for 3%

profile of v2, /device:TPU:32, one launch (start us, length us, event | category | flops | bytes accessed | tf_op | source)
XLA Modules:
  0.0 44.3 jit_solution(3302496610650198633)
XLA Ops:
  0.0 0.0 copy-start.2
  0.0 0.7 %copy-done.2 = f32[16]{0:T(128)S(1)} copy-done((f32[16]{0:T(128)S(1)}, f32[16]{0:T(128)}, u32[]{:S(2)}) %copy-start.2) | copy-done | bytes 88
  0.7 0.0 copy-start
  0.7 0.9 %copy-done = f32[16,32,128]{2,1,0:T(8,128)S(1)} copy-done((f32[16,32,128]{2,1,0:T(8,128)S(1)}, f32[16,32,128]{2,1,0:T(8,128)}, u32[]{:S(2)}) %copy-start) | copy-done | bytes 262168
  1.6 0.0 copy-start.1
  1.6 0.8 %copy-done.1 = s32[8,16,64]{2,1,0:T(8,128)S(1)} copy-done((s32[8,16,64]{2,1,0:T(8,128)S(1)}, s32[8,16,64]{2,1,0:T(8,128)}, u32[]{:S(2)}) %copy-start.1) | copy-done | bytes 32792
  2.4 0.8 %shard_map.37 = (f32[128,128]{1,0:T(8,128)S(1)}, f32[24,128]{1,0:T(8,128)S(1)}, f32[24,128]{1,0:T(8,128)S(1)}, f32[512,128]{1,0:T(8,128)S(1)}) custom-call(s32[128,64]{1,0:T(8,128)S(1)} %bitcast.4, f32[16]{0:T(128)S(1)} %copy-done.2, f32[512,128]{1,0:T(8,128)S(1)} %bitcast.3), custom_call_target="tpu_custom_call" | custom-call | flops 20000 | bytes 20000 | tf_op jit(solution)/shard_map/pallas_call | solution.py:459
  3.2 0.1 collective-permute-start
  3.3 5.3 %collective-permute-start.1 = (f32[24,128]{1,0:T(8,128)S(1)}, f32[24,128]{1,0:T(8,128)S(1)}, u32[]{:S(2)}, u32[]{:S(2)}) collective-permute-start(f32[24,128]{1,0:T(8,128)S(1)} %get-tuple-element.28), channel_id=1, source_target_pairs={{0,31},{1,2},{2,1},{3,4},{4,3},{5,6},{6,5},{7,8},{8,7},{9,10},{10,... | collective-permute-start | bytes 36872 | tf_op jit(solution)/shard_map/ppermute | solution.py:487
  8.6 1.2 %shard_map.38 = (f32[224,128]{1,0:T(8,128)S(1)}, f32[224,128]{1,0:T(8,128)S(1)}, f32[224,128]{1,0:T(8,128)S(1)}, f32[40,128]{1,0:T(8,128)S(1)}, f32[240,128]{1,0...) custom-call(f32[128,128]{1,0:T(8,128)S(1)} %get-tuple-element.26.k_ref), custom_call_target="tpu_custom_call" | custom-call | flops 4000000 | bytes 4000000 | tf_op jit(solution)/shard_map/pallas_call | solution.py:459
  9.8 0.0 collective-permute-done.inner_ref
  9.8 0.2 collective-permute-done.1.outer_ref
  10.0 0.3 shard_map.39
  10.3 2.0 %collective-permute-start.4 = (f32[104,128]{1,0:T(8,128)S(1)}, f32[104,128]{1,0:T(8,128)S(1)}, u32[]{:S(2)}, u32[]{:S(2)}) collective-permute-start(f32[104,128]{1,0:T(8,128)S(1)} %get-tuple-element.32.own_ref), channel_id=1, source_target_pairs={{0,96},{32,64},{64,32},{96,0},{128,224},{160,192},{192,160},{224,1... | collective-permute-start | bytes 159752 | tf_op jit(solution)/shard_map/ppermute | solution.py:506
  12.3 2.1 %collective-permute-start.3 = (f32[104,128]{1,0:T(8,128)S(1)}, f32[104,128]{1,0:T(8,128)S(1)}, u32[]{:S(2)}, u32[]{:S(2)}) collective-permute-start(f32[104,128]{1,0:T(8,128)S(1)} %get-tuple-element.32.own_ref), channel_id=1, source_target_pairs={{0,64},{32,96},{64,0},{96,32},{128,192},{160,224},{192,128},{224,1... | collective-permute-start | bytes 159752 | tf_op jit(solution)/shard_map/ppermute | solution.py:506
  14.4 0.7 %collective-permute-start.2 = (f32[104,128]{1,0:T(8,128)S(1)}, f32[104,128]{1,0:T(8,128)S(1)}, u32[]{:S(2)}, u32[]{:S(2)}) collective-permute-start(f32[104,128]{1,0:T(8,128)S(1)} %get-tuple-element.32.own_ref), channel_id=1, source_target_pairs={{0,32},{32,0},{64,96},{96,64},{128,160},{160,128},{192,224},{224,1... | collective-permute-start | bytes 159752 | tf_op jit(solution)/shard_map/ppermute | solution.py:506
  15.1 0.0 collective-permute-done.4.three_ref
  15.1 2.2 %collective-permute-done.3.two_ref = f32[104,128]{1,0:T(8,128)S(1)} collective-permute-done((f32[104,128]{1,0:T(8,128)S(1)}, f32[104,128]{1,0:T(8,128)S(1)}, u32[]{:S(2)}, u32[]{:S(2)}) %collective-permute-start.3) | collective-permute-done | bytes 53280 | tf_op jit(solution)/shard_map/ppermute | solution.py:506
  17.3 1.2 %collective-permute-done.2.one_ref = f32[104,128]{1,0:T(8,128)S(1)} collective-permute-done((f32[104,128]{1,0:T(8,128)S(1)}, f32[104,128]{1,0:T(8,128)S(1)}, u32[]{:S(2)}, u32[]{:S(2)}) %collective-permute-start.2) | collective-permute-done | bytes 53280 | tf_op jit(solution)/shard_map/ppermute | solution.py:506
  18.5 0.1 shard_map.40
  18.7 5.3 %collective-permute-start.5 = (f32[48,128]{1,0:T(8,128)S(1)}, f32[48,128]{1,0:T(8,128)S(1)}, u32[]{:S(2)}, u32[]{:S(2)}) collective-permute-start(f32[48,128]{1,0:T(8,128)S(1)} %shard_map.40), channel_id=1, source_target_pairs={{0,224},{32,192},{64,160},{96,128},{128,96},{160,64},{192,32},{224... | collective-permute-start | bytes 73736 | tf_op jit(solution)/shard_map/ppermute | solution.py:508
  24.0 1.8 %collective-permute-done.5.half_ref = f32[48,128]{1,0:T(8,128)S(1)} collective-permute-done((f32[48,128]{1,0:T(8,128)S(1)}, f32[48,128]{1,0:T(8,128)S(1)}, u32[]{:S(2)}, u32[]{:S(2)}) %collective-permute-start.5) | collective-permute-done | bytes 24608 | tf_op jit(solution)/shard_map/ppermute | solution.py:508
  25.8 0.4 shard_map.41
  26.2 0.1 collective-permute-start.6
  26.3 1.2 %collective-permute-done.6.other_ref = f32[48,128]{1,0:T(8,128)S(1)} collective-permute-done((f32[48,128]{1,0:T(8,128)S(1)}, f32[48,128]{1,0:T(8,128)S(1)}, u32[]{:S(2)}, u32[]{:S(2)}) %collective-permute-start.6) | collective-permute-done | bytes 24608 | tf_op jit(solution)/shard_map/ppermute | solution.py:515
  27.5 0.1 shard_map.42
  27.6 14.3 %all_to_all.5.recv_ref = f32[16,48,128]{2,1,0:T(8,128)S(1)} all-to-all(f32[16,48,128]{2,1,0:T(8,128)S(1)} %shard_map.42), channel_id=1, replica_groups={{0,2,4,6,8,10,12,14,16,18,20,22,24,26,28,30},{1,3,5,7,9,11,13,15,17,19,..., dimensions={0} | all-to-all | bytes 786432 | tf_op jit(solution)/shard_map/all_to_all | solution.py:518
  41.9 2.3 %shard_map.43 = f32[512,128]{1,0:T(8,128)} custom-call(f32[16,48,128]{2,1,0:T(8,128)S(1)} %all_to_all.5.recv_ref, f32[48,128]{1,0:T(8,128)S(1)} %get-tuple-element.38.own_ref, f32[48,128]{1,0:T(8,128)S(1)} %collective-permute-done.6.other_ref, f32[8,128]{1,0:T(8,128)S(1)} %get-tuple-element.39.mid_ref, f32[480,128]{1,0:T(8,128)S(1)} %get-tuple-element.40.rb_ref, ...), custom_call_target="tpu_custom_call" | custom-call | flops 20000 | bytes 20000 | tf_op jit(solution)/shard_map/pallas_call | solution.py:459
Async XLA Ops:
  0.0 0.7 %copy-start.2 = (f32[16]{0:T(128)S(1)}, f32[16]{0:T(128)}, u32[]{:S(2)}) copy-start(f32[16]{0:T(128)} %table_hbm.1) | copy-start | bytes 196
  0.7 0.9 %copy-start = (f32[16,32,128]{2,1,0:T(8,128)S(1)}, f32[16,32,128]{2,1,0:T(8,128)}, u32[]{:S(2)}) copy-start(f32[16,32,128]{2,1,0:T(8,128)} %param.3) | copy-start | bytes 786436
  1.6 0.8 %copy-start.1 = (s32[8,16,64]{2,1,0:T(8,128)S(1)}, s32[8,16,64]{2,1,0:T(8,128)}, u32[]{:S(2)}) copy-start(s32[8,16,64]{2,1,0:T(8,128)} %param.4) | copy-start | bytes 98308
  3.2 6.6 %collective-permute-start = (f32[24,128]{1,0:T(8,128)S(1)}, f32[24,128]{1,0:T(8,128)S(1)}, u32[]{:S(2)}, u32[]{:S(2)}) collective-permute-start(f32[24,128]{1,0:T(8,128)S(1)} %get-tuple-element.27), channel_id=1, source_target_pairs={{0,1},{1,0},{2,3},{3,2},{4,5},{5,4},{6,7},{7,6},{8,9},{9,8},{10,11... | collective-permute-start | bytes 36872 | tf_op jit(solution)/shard_map/ppermute | solution.py:488
  3.3 6.7 %collective-permute-start.1 = (f32[24,128]{1,0:T(8,128)S(1)}, f32[24,128]{1,0:T(8,128)S(1)}, u32[]{:S(2)}, u32[]{:S(2)}) collective-permute-start(f32[24,128]{1,0:T(8,128)S(1)} %get-tuple-element.28), channel_id=1, source_target_pairs={{0,31},{1,2},{2,1},{3,4},{4,3},{5,6},{6,5},{7,8},{8,7},{9,10},{10,... | collective-permute-start | bytes 36872 | tf_op jit(solution)/shard_map/ppermute | solution.py:487
  10.3 4.8 %collective-permute-start.4 = (f32[104,128]{1,0:T(8,128)S(1)}, f32[104,128]{1,0:T(8,128)S(1)}, u32[]{:S(2)}, u32[]{:S(2)}) collective-permute-start(f32[104,128]{1,0:T(8,128)S(1)} %get-tuple-element.32.own_ref), channel_id=1, source_target_pairs={{0,96},{32,64},{64,32},{96,0},{128,224},{160,192},{192,160},{224,1... | collective-permute-start | bytes 159752 | tf_op jit(solution)/shard_map/ppermute | solution.py:506
  12.3 5.0 %collective-permute-start.3 = (f32[104,128]{1,0:T(8,128)S(1)}, f32[104,128]{1,0:T(8,128)S(1)}, u32[]{:S(2)}, u32[]{:S(2)}) collective-permute-start(f32[104,128]{1,0:T(8,128)S(1)} %get-tuple-element.32.own_ref), channel_id=1, source_target_pairs={{0,64},{32,96},{64,0},{96,32},{128,192},{160,224},{192,128},{224,1... | collective-permute-start | bytes 159752 | tf_op jit(solution)/shard_map/ppermute | solution.py:506
  14.4 4.1 %collective-permute-start.2 = (f32[104,128]{1,0:T(8,128)S(1)}, f32[104,128]{1,0:T(8,128)S(1)}, u32[]{:S(2)}, u32[]{:S(2)}) collective-permute-start(f32[104,128]{1,0:T(8,128)S(1)} %get-tuple-element.32.own_ref), channel_id=1, source_target_pairs={{0,32},{32,0},{64,96},{96,64},{128,160},{160,128},{192,224},{224,1... | collective-permute-start | bytes 159752 | tf_op jit(solution)/shard_map/ppermute | solution.py:506
  18.7 7.1 %collective-permute-start.5 = (f32[48,128]{1,0:T(8,128)S(1)}, f32[48,128]{1,0:T(8,128)S(1)}, u32[]{:S(2)}, u32[]{:S(2)}) collective-permute-start(f32[48,128]{1,0:T(8,128)S(1)} %shard_map.40), channel_id=1, source_target_pairs={{0,224},{32,192},{64,160},{96,128},{128,96},{160,64},{192,32},{224... | collective-permute-start | bytes 73736 | tf_op jit(solution)/shard_map/ppermute | solution.py:508
  26.2 1.3 %collective-permute-start.6 = (f32[48,128]{1,0:T(8,128)S(1)}, f32[48,128]{1,0:T(8,128)S(1)}, u32[]{:S(2)}, u32[]{:S(2)}) collective-permute-start(f32[48,128]{1,0:T(8,128)S(1)} %get-tuple-element.38.own_ref), channel_id=1, source_target_pairs={{0,1},{1,0},{2,3},{3,2},{4,5},{5,4},{6,7},{7,6},{8,9},{9,8},{10,11... | collective-permute-start | bytes 73736 | tf_op jit(solution)/shard_map/ppermute | solution.py:515

commit v3 on v2

--- a/solution.py
+++ b/solution.py
@@ -65,12 +65,13 @@
 
 
 def prepare_kernel(
-    ids_hbm, table_hbm, heat_hbm, k_ref, inner_ref, outer_ref, heat_ref, ids_ref, table_ref, wide, sems
+    ids_hbm, table_hbm, heat_hbm, k_ref, inner_ref, outer_ref, ids_ref, table_ref, low_ref, high_ref, wide, sems
 ):
     copies = [
         pltpu.make_async_copy(table_hbm, table_ref, sems.at[0]),
         pltpu.make_async_copy(ids_hbm, ids_ref, sems.at[1]),
-        pltpu.make_async_copy(heat_hbm, heat_ref, sems.at[2]),
+        pltpu.make_async_copy(heat_hbm.at[:, 0:8, :], low_ref, sems.at[2]),
+        pltpu.make_async_copy(heat_hbm.at[:, NY - 8 : NY, :], high_ref, sems.at[3]),
     ]
     for copy in copies:
         copy.start()
@@ -85,10 +86,10 @@
     index = lanes(wide.shape) // 2
     k_ref[...] = jnp.take_along_axis(wide[...], index, axis=1, mode="promise_in_bounds")
     copies[2].wait()
-    low = [heat_ref[pl.ds(0, NX, stride=NY), :], k_ref[pl.ds(0, MX, stride=MY), :]]
-    high = [heat_ref[pl.ds(NY - 1, NX, stride=NY), :], k_ref[pl.ds(MY - 1, MX, stride=MY), :]]
+    copies[3].wait()
+    low = jnp.concatenate([low_ref[:, 0, :], k_ref[pl.ds(0, MX, stride=MY), :]], 0)
+    high = jnp.concatenate([high_ref[:, 7, :], k_ref[pl.ds(MY - 1, MX, stride=MY), :]], 0)
     core = lax.rem(lax.axis_index("gy"), 2)
-    low, high = jnp.concatenate(low, 0), jnp.concatenate(high, 0)
     inner_ref[...] = jnp.where(core == 0, high, low)
     outer_ref[...] = jnp.where(core == 0, low, high)
 
@@ -218,14 +219,14 @@
     return alpha, beta, link, k_first, k_last, [rows[0:16], rows[16:32]], [rows[32:48], rows[48:64]]
 
 
-def x_quarter(place, refs):
+def quarter(place, refs, segment):
     held = [r[...] for r in refs]
     segments = []
     for d in range(4):
         rows = held[0]
         for j in range(1, 4):
             rows = jnp.where(place == d ^ j, held[j], rows)
-        segments.append(x_segment(rows))
+        segments.append(segment(rows))
     return segments
 
 
@@ -247,7 +248,7 @@
         far_src = [pick(b, a) for a, b in zip(ra, rb)]
         return near, far, link, k_near, k_far, near_src, far_src
 
-    segments = [turn(g) for g in x_quarter(place, (own_ref, one_ref, two_ref, three_ref))]
+    segments = [turn(g) for g in quarter(place, (own_ref, one_ref, two_ref, three_ref), x_segment)]
     zero = jnp.zeros((MY, NZ), f32)
     leak, src = zero, [zero, zero]
     for d in range(3):
@@ -268,7 +269,7 @@
 ):
     at = lax.axis_index("gx")
     place = lax.rem(at, 4)
-    segments = x_quarter(place, (own_ref, one_ref, two_ref, three_ref))
+    segments = quarter(place, (own_ref, one_ref, two_ref, three_ref), x_segment)
     half_leak, half_k = unpack(half_ref[32:48, :])
     upper = at >= 4
     joint = 1000.0 * (half_k + jnp.where(upper, segments[0][3], segments[3][4]))
@@ -344,24 +345,16 @@
 
 
 def y_segment(rows):
-    alpha, beta = unpack(rows(32))
-    link, joint = unpack(rows(40))
-    return alpha, beta, link, joint, [rows(0), rows(8)], [rows(16), rows(24)]
-
-
-def chip_kernel(own_ref, other_ref, mid_ref, send_ref):
-    core = lax.rem(lax.axis_index("gy"), 2)
-    own = y_segment(lambda r: own_ref[r : r + 8, :])
-    other = y_segment(lambda r: other_ref[r : r + 8, :])
-
-    def choose(a, b):
-        return jnp.where(core == 0, a, b)
-
-    a0, b0, h0, joint, ra0, rb0 = jax.tree.map(choose, own, other)
-    a1, b1, h1, _, ra1, rb1 = jax.tree.map(choose, other, own)
-    mid = mid_ref[...]
-    inv = 1.0 / (h0 + b0 + mid)
-    hd, gd = h0 * inv, mid * inv
+    alpha, beta = unpack(rows[32:40])
+    link, joint = unpack(rows[40:48])
+    return alpha, beta, link, joint, [rows[0:8], rows[8:16]], [rows[16:24], rows[24:32]]
+
+
+def merge(first, second, joint):
+    a0, b0, h0, outer, ra0, rb0 = first
+    a1, b1, h1, _, ra1, rb1 = second
+    inv = 1.0 / (h0 + b0 + joint)
+    hd, gd = h0 * inv, joint * inv
     alpha = a0 + b0 * hd
     link = h0 * gd
     between = a1 + b0 * gd
@@ -373,38 +366,59 @@
     beta = b1 + between * gd
     ra = [a + m * hd for a, m in zip(ra, rm)]
     rb = [b + m * gd for b, m in zip(rb1, rm)]
-    out = jnp.concatenate([*ra, *rb, pack(alpha, beta), pack(link * gd, joint)], 0)
-    for d in range(send_ref.shape[0]):
-        send_ref[d] = out
+    return alpha, beta, link * gd, outer, ra, rb
+
+
+def store_segment(ref, segment):
+    alpha, beta, link, joint, ra, rb = segment
+    ref[...] = jnp.concatenate([*ra, *rb, pack(alpha, beta), pack(link, joint)], 0)
+
+
+def chip_kernel(own_ref, other_ref, mid_ref, send_ref):
+    core = lax.rem(lax.axis_index("gy"), 2)
+    own, other = own_ref[...], other_ref[...]
+    first = y_segment(jnp.where(core == 0, own, other))
+    second = y_segment(jnp.where(core == 0, other, own))
+    store_segment(send_ref, merge(first, second, mid_ref[...]))
+
+
+def y_four_kernel(own_ref, one_ref, two_ref, three_ref, send_ref):
+    place = lax.rem(lax.div(lax.axis_index("gy"), 2), 4)
+    a, b, c, d = quarter(place, (own_ref, one_ref, two_ref, three_ref), y_segment)
+    store_segment(send_ref, merge(merge(a, b, b[3]), merge(c, d, d[3]), c[3]))
+
+
+def y_sweeps(segments, place, left, left_src, right, right_src):
+    for step in range(3):
+        d = step
+        alpha, beta, link, _, ra, rb = segments[d]
+        new, new_src = through(beta, alpha, link, segments[d + 1][3], left, rb, ra, left_src)
+        left = jnp.where(d < place, new, left)
+        left_src = [jnp.where(d < place, n, o) for n, o in zip(new_src, left_src)]
+        d = 3 - step
+        alpha, beta, link, joint, ra, rb = segments[d]
+        new, new_src = through(alpha, beta, link, joint, right, ra, rb, right_src)
+        right = jnp.where(d > place, new, right)
+        right_src = [jnp.where(d > place, n, o) for n, o in zip(new_src, right_src)]
+    return left, left_src, right, right_src
 
 
 def y_solve_kernel(
-    recv_ref, own_ref, other_ref, mid_ref, rb_ref, gy_ref, hy_ref, iy_ref, za_ref, zc_ref, zi_ref, heat_ref,
-    out_ref, second,
+    large0, large1, large2, large3, small0, small1, small2, small3, own_ref, other_ref, mid_ref, rb_ref, gy_ref,
+    hy_ref, iy_ref, za_ref, zc_ref, zi_ref, heat_ref, out_ref, second,
 ):
     at_y = lax.axis_index("gy")
     core, chip = lax.rem(at_y, 2), lax.div(at_y, 2)
-    count = recv_ref.shape[0]
-    segments = [y_segment(lambda r, d=d: recv_ref[d, r : r + 8, :]) for d in range(count)]
     zero = jnp.zeros((MX, NZ), f32)
-    left, left_src = zero, [zero, zero]
-    right, right_src = zero, [zero, zero]
-    for step in range(count - 1):
-        d = step
-        alpha, beta, link, _, ra, rb = segments[d]
-        new, new_src = through(beta, alpha, link, segments[d + 1][3], left, rb, ra, left_src)
-        left = jnp.where(d < chip, new, left)
-        left_src = [jnp.where(d < chip, n, o) for n, o in zip(new_src, left_src)]
-        d = count - 1 - step
-        alpha, beta, link, joint, ra, rb = segments[d]
-        new, new_src = through(alpha, beta, link, joint, right, ra, rb, right_src)
-        right = jnp.where(d > chip, new, right)
-        right_src = [jnp.where(d > chip, n, o) for n, o in zip(new_src, right_src)]
+    large = quarter(lax.div(chip, 4), (large0, large1, large2, large3), y_segment)
+    small = quarter(lax.rem(chip, 4), (small0, small1, small2, small3), y_segment)
+    state = y_sweeps(large, lax.div(chip, 4), zero, [zero, zero], zero, [zero, zero])
+    left, left_src, right, right_src = y_sweeps(small, lax.rem(chip, 4), *state)
 
     def choose(a, b):
         return jnp.where(core == 0, a, b)
 
-    alpha, beta, link, _, ra, rb = y_segment(lambda r: other_ref[r : r + 8, :])
+    alpha, beta, link, _, ra, rb = y_segment(other_ref[...])
     near, far = choose(alpha, beta), choose(beta, alpha)
     near_src = [choose(a, b) for a, b in zip(ra, rb)]
     far_src = [choose(b, a) for a, b in zip(ra, rb)]
@@ -416,7 +430,7 @@
         [choose(l, n) for l, n in zip(left_src, new_src)],
         [choose(n, r) for n, r in zip(new_src, right_src)],
     )
-    alpha, beta, link, _, ra, rb = y_segment(lambda r: own_ref[r : r + 8, :])
+    alpha, beta, link, _, ra, rb = y_segment(own_ref[...])
     u_first, u_next = two_nodes(
         alpha + left,
         beta + right,
@@ -454,7 +468,7 @@
             out_ref[where, :] = heat_ref[where, :] + inv * w
 
 
-def call(kernel, ins, outs, scratch=(), outside=False, cost=20000):
+def call(kernel, ins, outs, scratch=(), outside=False, cost=20000, limit=8 << 20):
     space = pltpu.HBM if outside else pltpu.VMEM
     return pl.pallas_call(
         kernel,
@@ -462,7 +476,7 @@
         in_specs=[pl.BlockSpec(memory_space=space) for _ in ins],
         out_specs=tuple(pl.BlockSpec(memory_space=pltpu.VMEM) for _ in outs),
         scratch_shapes=scratch,
-        compiler_params=pltpu.CompilerParams(vmem_limit_bytes=8 << 20),
+        compiler_params=pltpu.CompilerParams(vmem_limit_bytes=limit),
         cost_estimate=pl.CostEstimate(flops=cost, bytes_accessed=cost, transcendentals=0),
     )(*ins)
 
@@ -471,21 +485,24 @@
     heat = starting_heat_state.reshape(NX * NY, NZ)
     ids = material_zone_ids.reshape(MX * MY, NZ // 2)
     nx, ny = lax.axis_size("gx"), lax.axis_size("gy")
-    k, inner, outer, heat = call(
+    k, inner, outer = call(
         prepare_kernel,
-        (ids, zone_diffusivity_lookup, heat),
-        [(MX * MY, NZ), (NX + MX, NZ), (NX + MX, NZ), (NX * NY, NZ)],
+        (ids, zone_diffusivity_lookup, starting_heat_state),
+        [(MX * MY, NZ), (NX + MX, NZ), (NX + MX, NZ)],
         scratch=[
             pltpu.VMEM(ids.shape, jnp.int32),
             pltpu.SMEM(zone_diffusivity_lookup.shape, f32),
+            pltpu.VMEM((NX, 8, NZ), f32),
+            pltpu.VMEM((NX, 8, NZ), f32),
             pltpu.VMEM((MX * MY, NZ), f32),
-            pltpu.SemaphoreType.DMA((3,)),
+            pltpu.SemaphoreType.DMA((4,)),
         ],
         outside=True,
+        limit=55500 << 10,
     )
     cores = [(i, i ^ 1) for i in range(ny)]
+    inner = lax.ppermute(inner, "gy", cores)
     outer = lax.ppermute(outer, "gy", [(i, (i + (1 if i % 2 else -1)) % ny) for i in range(ny)])
-    inner = lax.ppermute(inner, "gy", cores)
     tx, ty = NX - 2, NY - 2
     gx, hx, ix, px, gy, hy, iy, my, za, zc, zi = call(
         matrix_kernel,
@@ -503,22 +520,23 @@
         (heat, k, inner, outer, gx, hx, px),
         [(XROWS, NZ), (tx * NY, NZ)],
     )
-    quarter = [send] + [lax.ppermute(send, "gx", [(i, i ^ d) for i in range(nx)]) for d in (1, 2, 3)]
-    (half,) = call(x_half_kernel, quarter, [(48, NZ)])
+    near = [send] + [lax.ppermute(send, "gx", [(i, i ^ d) for i in range(nx)]) for d in (1, 2, 3)]
+    (half,) = call(x_half_kernel, near, [(48, NZ)])
     half = lax.ppermute(half, "gx", [(i, nx - 1 - i) for i in range(nx)])
     own, mid, rby = call(
         x_solve_kernel,
-        (*quarter, half, heat, k, inner, outer, rbx, gx, hx, ix, gy, hy, my),
+        (*near, half, heat, k, inner, outer, rbx, gx, hx, ix, gy, hy, my),
         [(YROWS, NZ), (MX, NZ), (ty * MX * 2, NZ)],
         scratch=[pltpu.VMEM((NX * NY, NZ), f32)],
     )
     other = lax.ppermute(own, "gy", cores)
-    (send,) = call(chip_kernel, (own, other, mid), [(ny // 2, YROWS, NZ)])
-    groups = [list(range(c, ny, 2)) for c in range(2)]
-    recv = lax.all_to_all(send, "gy", 0, 0, axis_index_groups=groups)
+    (chip,) = call(chip_kernel, (own, other, mid), [(YROWS, NZ)])
+    small = [chip] + [lax.ppermute(chip, "gy", [(i, i ^ (2 * d)) for i in range(ny)]) for d in (1, 2, 3)]
+    (four,) = call(y_four_kernel, small, [(YROWS, NZ)])
+    large = [four] + [lax.ppermute(four, "gy", [(i, i ^ (8 * d)) for i in range(ny)]) for d in (1, 2, 3)]
     (out,) = call(
         y_solve_kernel,
-        (recv, own, other, mid, rby, gy, hy, iy, za, zc, zi, heat),
+        (*large, *small, own, other, mid, rby, gy, hy, iy, za, zc, zi, heat),
         [(NX * NY, NZ)],
         scratch=[pltpu.VMEM((NX * NY, NZ), f32)],
     )

time: 44.8 us -> 42.8 us (0.955)
  blocking collectives: 14.3 us -> 0 us
  starting transfers between devices: 15.6 us -> 24.1 us
  waiting for transfers between devices: 6.64 us -> 11.5 us
  local copies, waits for them, and re-layouts: 2.44 us -> 0.85 us
  Pallas kernels: 5.15 us -> 6.11 us
    all_to_all x1 -> x0, blocking collectives: 14.3 us -> none  [on_device(): recv = lax.all_to_all(send, 'gy', 0, 0, axis_index_groups=groups)]
    ppermute x0 -> x6, starting transfers between devices: none -> 8.35 us  [the longest x3 4.18 us: on_device(): lax.ppermute(four, 'gy', [(i, i ^ 8 * d) for i in range(ny)])]
    ppermute x0 -> x6, waiting for transfers between devices: none -> 5.24 us  [the longest x3 3.18 us: on_device(): lax.ppermute(four, 'gy', [(i, i ^ 8 * d) for i in range(ny)])]
    unnamed x6, local copies, waits for them, and re-layouts: 2.44 us -> 0.85 us
    pallas_call x7 -> x8, Pallas kernels: 5.15 us -> 6.11 us  [call(): pl.pallas_call(kernel, out_shape=tuple((jax.ShapeDtypeStruct(s, f32) for...]
  transfers between devices with their start and end apart: 7 -> 13, of which waited for: 5 -> 9; matrix products, arithmetic and copies ran while one was open for 0% -> 0% of each run, Pallas kernels for 3% -> 3%
where the time goes in v3:
time: 42.8 us; the launch traced here: 42.7 us
  starting transfers between devices  24.1 us (56%)
  waiting for transfers between devices  11.5 us (27%)
  Pallas kernels  6.11 us (14%)
  local copies, waits for them, and re-layouts  0.85 us (2%)
    pallas_call x8, Pallas kernels, call(): pl.pallas_call(kernel, out_shape=tuple((jax.ShapeDtypeStruct(s, f32) for...  6.11 us
    ppermute x1, starting transfers between devices, on_device(): half = lax.ppermute(half, 'gx', [(i, nx - 1 - i) for i in range(nx)])  5.46 us
    ppermute x1, starting transfers between devices, on_device(): lax.ppermute(outer, 'gy', [(i, (i + (1 if i % 2 else -1)) % ny) for i in...  5.31 us
    ppermute x3, starting transfers between devices, on_device(): lax.ppermute(send, 'gx', [(i, i ^ d) for i in range(nx)])  4.82 us
    ppermute x3, starting transfers between devices, on_device(): lax.ppermute(four, 'gy', [(i, i ^ 8 * d) for i in range(ny)])  4.18 us
    ppermute x3, starting transfers between devices, on_device(): lax.ppermute(chip, 'gy', [(i, i ^ 2 * d) for i in range(ny)])  4.17 us
    ppermute x3, waiting for transfers between devices, on_device(): lax.ppermute(send, 'gx', [(i, i ^ d) for i in range(nx)])  3.24 us
    ppermute x3, waiting for transfers between devices, on_device(): lax.ppermute(four, 'gy', [(i, i ^ 8 * d) for i in range(ny)])  3.18 us
  transfers between devices with their start and end apart: 13, of which 9 were waited for; matrix products, arithmetic and copies ran while one was open for 0% of the time, Pallas kernels for 3%

profile of v3, /device:TPU:32, one launch (start us, length us, event | category | flops | bytes accessed | tf_op | source)
XLA Modules:
  0.0 42.7 jit_solution(662497862386403085)
XLA Ops:
  0.0 0.0 copy-start
  0.0 1.7 %shard_map.37 = (f32[128,128]{1,0:T(8,128)}, f32[24,128]{1,0:T(8,128)}, f32[24,128]{1,0:T(8,128)}) custom-call(s32[128,64]{1,0:T(8,128)} %bitcast.6, f32[16]{0:T(128)} %table_hbm.1, f32[16,32,128]{2,1,0:T(8,128)} %heat_hbm.1), custom_call_target="tpu_custom_call" | custom-call | flops 20000 | bytes 20000 | tf_op jit(solution)/shard_map/pallas_call | solution.py:473
  1.7 0.1 collective-permute-start
  1.8 5.3 %collective-permute-start.1 = (f32[24,128]{1,0:T(8,128)}, f32[24,128]{1,0:T(8,128)S(1)}, u32[]{:S(2)}, u32[]{:S(2)}) collective-permute-start(f32[24,128]{1,0:T(8,128)} %get-tuple-element.26), channel_id=1, source_target_pairs={{0,31},{1,2},{2,1},{3,4},{4,3},{5,6},{6,5},{7,8},{8,7},{9,10},{10,... | collective-permute-start | bytes 36872 | tf_op jit(solution)/shard_map/ppermute | solution.py:505
  7.1 0.0 copy-start.1
  7.1 0.8 %copy-done.1 = f32[128,128]{1,0:T(8,128)S(1)} copy-done((f32[128,128]{1,0:T(8,128)S(1)}, f32[128,128]{1,0:T(8,128)}, u32[]{:S(2)}) %copy-start.1) | copy-done | bytes 65560
  8.0 1.2 %shard_map.38 = (f32[224,128]{1,0:T(8,128)S(1)}, f32[224,128]{1,0:T(8,128)S(1)}, f32[224,128]{1,0:T(8,128)S(1)}, f32[40,128]{1,0:T(8,128)S(1)}, f32[240,128]{1,0...) custom-call(f32[128,128]{1,0:T(8,128)S(1)} %copy-done.1), custom_call_target="tpu_custom_call" | custom-call | flops 4000000 | bytes 4000000 | tf_op jit(solution)/shard_map/pallas_call | solution.py:473
  9.1 0.0 collective-permute-done.inner_ref
  9.2 0.0 collective-permute-done.1.outer_ref
  9.2 0.0 copy-done
  9.2 0.3 shard_map.39
  9.5 0.0 copy-start.2
  9.5 2.0 %collective-permute-start.4 = (f32[104,128]{1,0:T(8,128)S(1)}, f32[104,128]{1,0:T(8,128)S(1)}, u32[]{:S(2)}, u32[]{:S(2)}) collective-permute-start(f32[104,128]{1,0:T(8,128)S(1)} %get-tuple-element.30.own_ref), channel_id=1, source_target_pairs={{0,96},{32,64},{64,32},{96,0},{128,224},{160,192},{192,160},{224,1... | collective-permute-start | bytes 159752 | tf_op jit(solution)/shard_map/ppermute | solution.py:523
  11.5 1.7 %collective-permute-start.3 = (f32[104,128]{1,0:T(8,128)S(1)}, f32[104,128]{1,0:T(8,128)S(1)}, u32[]{:S(2)}, u32[]{:S(2)}) collective-permute-start(f32[104,128]{1,0:T(8,128)S(1)} %get-tuple-element.30.own_ref), channel_id=1, source_target_pairs={{0,64},{32,96},{64,0},{96,32},{128,192},{160,224},{192,128},{224,1... | collective-permute-start | bytes 159752 | tf_op jit(solution)/shard_map/ppermute | solution.py:523
  13.2 1.1 %collective-permute-start.2 = (f32[104,128]{1,0:T(8,128)S(1)}, f32[104,128]{1,0:T(8,128)S(1)}, u32[]{:S(2)}, u32[]{:S(2)}) collective-permute-start(f32[104,128]{1,0:T(8,128)S(1)} %get-tuple-element.30.own_ref), channel_id=1, source_target_pairs={{0,32},{32,0},{64,96},{96,64},{128,160},{160,128},{192,224},{224,1... | collective-permute-start | bytes 159752 | tf_op jit(solution)/shard_map/ppermute | solution.py:523
  14.3 0.0 collective-permute-done.4.three_ref
  14.3 2.2 %collective-permute-done.3.two_ref = f32[104,128]{1,0:T(8,128)S(1)} collective-permute-done((f32[104,128]{1,0:T(8,128)S(1)}, f32[104,128]{1,0:T(8,128)S(1)}, u32[]{:S(2)}, u32[]{:S(2)}) %collective-permute-start.3) | collective-permute-done | bytes 53280 | tf_op jit(solution)/shard_map/ppermute | solution.py:523
  16.5 1.0 %collective-permute-done.2.one_ref = f32[104,128]{1,0:T(8,128)S(1)} collective-permute-done((f32[104,128]{1,0:T(8,128)S(1)}, f32[104,128]{1,0:T(8,128)S(1)}, u32[]{:S(2)}, u32[]{:S(2)}) %collective-permute-start.2) | collective-permute-done | bytes 53280 | tf_op jit(solution)/shard_map/ppermute | solution.py:523
  17.5 0.1 shard_map.40
  17.7 5.5 %collective-permute-start.5 = (f32[48,128]{1,0:T(8,128)S(1)}, f32[48,128]{1,0:T(8,128)S(1)}, u32[]{:S(2)}, u32[]{:S(2)}) collective-permute-start(f32[48,128]{1,0:T(8,128)S(1)} %shard_map.40), channel_id=1, source_target_pairs={{0,224},{32,192},{64,160},{96,128},{128,96},{160,64},{192,32},{224... | collective-permute-start | bytes 73736 | tf_op jit(solution)/shard_map/ppermute | solution.py:525
  23.1 1.8 %collective-permute-done.5.half_ref = f32[48,128]{1,0:T(8,128)S(1)} collective-permute-done((f32[48,128]{1,0:T(8,128)S(1)}, f32[48,128]{1,0:T(8,128)S(1)}, u32[]{:S(2)}, u32[]{:S(2)}) %collective-permute-start.5) | collective-permute-done | bytes 24608 | tf_op jit(solution)/shard_map/ppermute | solution.py:525
  24.9 0.0 copy-done.2
  25.0 0.4 shard_map.41
  25.4 0.1 collective-permute-start.6
  25.5 1.2 %collective-permute-done.6.other_ref = f32[48,128]{1,0:T(8,128)S(1)} collective-permute-done((f32[48,128]{1,0:T(8,128)S(1)}, f32[48,128]{1,0:T(8,128)S(1)}, u32[]{:S(2)}, u32[]{:S(2)}) %collective-permute-start.6) | collective-permute-done | bytes 24608 | tf_op jit(solution)/shard_map/ppermute | solution.py:532
  26.6 0.1 shard_map.42.own_ref.small0
  26.7 0.1 collective-permute-start.9
  26.8 0.6 %collective-permute-start.8 = (f32[48,128]{1,0:T(8,128)S(1)}, f32[48,128]{1,0:T(8,128)S(1)}, u32[]{:S(2)}, u32[]{:S(2)}) collective-permute-start(f32[48,128]{1,0:T(8,128)S(1)} %shard_map.42.own_ref.small0), channel_id=1, source_target_pairs={{0,4},{1,5},{2,6},{3,7},{4,0},{5,1},{6,2},{7,3},{8,12},{9,13},{10,... | collective-permute-start | bytes 73736 | tf_op jit(solution)/shard_map/ppermute | solution.py:534
  27.4 3.5 %collective-permute-start.7 = (f32[48,128]{1,0:T(8,128)S(1)}, f32[48,128]{1,0:T(8,128)S(1)}, u32[]{:S(2)}, u32[]{:S(2)}) collective-permute-start(f32[48,128]{1,0:T(8,128)S(1)} %shard_map.42.own_ref.small0), channel_id=1, source_target_pairs={{0,2},{1,3},{2,0},{3,1},{4,6},{5,7},{6,4},{7,5},{8,10},{9,11},{10,... | collective-permute-start | bytes 73736 | tf_op jit(solution)/shard_map/ppermute | solution.py:534
  30.9 0.9 %collective-permute-done.9.three_ref.small3 = f32[48,128]{1,0:T(8,128)S(1)} collective-permute-done((f32[48,128]{1,0:T(8,128)S(1)}, f32[48,128]{1,0:T(8,128)S(1)}, u32[]{:S(2)}, u32[]{:S(2)}) %collective-permute-start.9) | collective-permute-done | bytes 24608 | tf_op jit(solution)/shard_map/ppermute | solution.py:534
  31.9 0.6 %collective-permute-done.8.two_ref.small2 = f32[48,128]{1,0:T(8,128)S(1)} collective-permute-done((f32[48,128]{1,0:T(8,128)S(1)}, f32[48,128]{1,0:T(8,128)S(1)}, u32[]{:S(2)}, u32[]{:S(2)}) %collective-permute-start.8) | collective-permute-done | bytes 24608 | tf_op jit(solution)/shard_map/ppermute | solution.py:534
  32.5 0.5 %collective-permute-done.7.one_ref.small1 = f32[48,128]{1,0:T(8,128)S(1)} collective-permute-done((f32[48,128]{1,0:T(8,128)S(1)}, f32[48,128]{1,0:T(8,128)S(1)}, u32[]{:S(2)}, u32[]{:S(2)}) %collective-permute-start.7) | collective-permute-done | bytes 24608 | tf_op jit(solution)/shard_map/ppermute | solution.py:534
  33.0 0.1 shard_map.43.large0
  33.1 2.0 %collective-permute-start.12 = (f32[48,128]{1,0:T(8,128)S(1)}, f32[48,128]{1,0:T(8,128)S(1)}, u32[]{:S(2)}, u32[]{:S(2)}) collective-permute-start(f32[48,128]{1,0:T(8,128)S(1)} %shard_map.43.large0), channel_id=1, source_target_pairs={{0,24},{1,25},{2,26},{3,27},{4,28},{5,29},{6,30},{7,31},{8,16},{9,... | collective-permute-start | bytes 73736 | tf_op jit(solution)/shard_map/ppermute | solution.py:536
  35.1 0.4 collective-permute-start.11
  35.5 1.8 %collective-permute-start.10 = (f32[48,128]{1,0:T(8,128)S(1)}, f32[48,128]{1,0:T(8,128)S(1)}, u32[]{:S(2)}, u32[]{:S(2)}) collective-permute-start(f32[48,128]{1,0:T(8,128)S(1)} %shard_map.43.large0), channel_id=1, source_target_pairs={{0,8},{1,9},{2,10},{3,11},{4,12},{5,13},{6,14},{7,15},{8,0},{9,1},... | collective-permute-start | bytes 73736 | tf_op jit(solution)/shard_map/ppermute | solution.py:536
  37.3 1.1 %collective-permute-done.12.large3 = f32[48,128]{1,0:T(8,128)S(1)} collective-permute-done((f32[48,128]{1,0:T(8,128)S(1)}, f32[48,128]{1,0:T(8,128)S(1)}, u32[]{:S(2)}, u32[]{:S(2)}) %collective-permute-start.12) | collective-permute-done | bytes 24608 | tf_op jit(solution)/shard_map/ppermute | solution.py:536
  38.4 2.1 %collective-permute-done.11.large2 = f32[48,128]{1,0:T(8,128)S(1)} collective-permute-done((f32[48,128]{1,0:T(8,128)S(1)}, f32[48,128]{1,0:T(8,128)S(1)}, u32[]{:S(2)}, u32[]{:S(2)}) %collective-permute-start.11) | collective-permute-done | bytes 24608 | tf_op jit(solution)/shard_map/ppermute | solution.py:536
  40.5 0.0 collective-permute-done.10.large1
  40.5 2.2 %shard_map.44 = f32[512,128]{1,0:T(8,128)} custom-call(f32[48,128]{1,0:T(8,128)S(1)} %shard_map.43.large0, f32[48,128]{1,0:T(8,128)S(1)} %collective-permute-done.10.large1, f32[48,128]{1,0:T(8,128)S(1)} %collective-permute-done.11.large2, f32[48,128]{1,0:T(8,128)S(1)} %collective-permute-done.12.large3, f32[48,128]{1,0:T(8,128)S(1)} %shard_map.42.own_ref.small0, ...), custom_call_target="tpu_custom_call" | custom-call | flops 20000 | bytes 20000 | tf_op jit(solution)/shard_map/pallas_call | solution.py:473
Async XLA Ops:
  0.0 9.2 %copy-start = (f32[16,32,128]{2,1,0:T(8,128)S(1)}, f32[16,32,128]{2,1,0:T(8,128)}, u32[]{:S(2)}) copy-start(f32[16,32,128]{2,1,0:T(8,128)} %heat_hbm.1) | copy-start | bytes 786436
  1.7 7.4 %collective-permute-start = (f32[24,128]{1,0:T(8,128)}, f32[24,128]{1,0:T(8,128)S(1)}, u32[]{:S(2)}, u32[]{:S(2)}) collective-permute-start(f32[24,128]{1,0:T(8,128)} %get-tuple-element.25), channel_id=1, source_target_pairs={{0,1},{1,0},{2,3},{3,2},{4,5},{5,4},{6,7},{7,6},{8,9},{9,8},{10,11... | collective-permute-start | bytes 36872 | tf_op jit(solution)/shard_map/ppermute | solution.py:504
  1.8 7.3 %collective-permute-start.1 = (f32[24,128]{1,0:T(8,128)}, f32[24,128]{1,0:T(8,128)S(1)}, u32[]{:S(2)}, u32[]{:S(2)}) collective-permute-start(f32[24,128]{1,0:T(8,128)} %get-tuple-element.26), channel_id=1, source_target_pairs={{0,31},{1,2},{2,1},{3,4},{4,3},{5,6},{6,5},{7,8},{8,7},{9,10},{10,... | collective-permute-start | bytes 36872 | tf_op jit(solution)/shard_map/ppermute | solution.py:505
  7.1 0.8 %copy-start.1 = (f32[128,128]{1,0:T(8,128)S(1)}, f32[128,128]{1,0:T(8,128)}, u32[]{:S(2)}) copy-start(f32[128,128]{1,0:T(8,128)} %get-tuple-element.24.k_ref) | copy-start | bytes 196612
  9.5 15.5 %copy-start.2 = (f32[128,128]{1,0:T(8,128)S(1)}, f32[128,128]{1,0:T(8,128)}, u32[]{:S(2)}) copy-start(f32[128,128]{1,0:T(8,128)} %get-tuple-element.24.k_ref) | copy-start | bytes 196612
  9.5 4.8 %collective-permute-start.4 = (f32[104,128]{1,0:T(8,128)S(1)}, f32[104,128]{1,0:T(8,128)S(1)}, u32[]{:S(2)}, u32[]{:S(2)}) collective-permute-start(f32[104,128]{1,0:T(8,128)S(1)} %get-tuple-element.30.own_ref), channel_id=1, source_target_pairs={{0,96},{32,64},{64,32},{96,0},{128,224},{160,192},{192,160},{224,1... | collective-permute-start | bytes 159752 | tf_op jit(solution)/shard_map/ppermute | solution.py:523
  11.5 5.0 %collective-permute-start.3 = (f32[104,128]{1,0:T(8,128)S(1)}, f32[104,128]{1,0:T(8,128)S(1)}, u32[]{:S(2)}, u32[]{:S(2)}) collective-permute-start(f32[104,128]{1,0:T(8,128)S(1)} %get-tuple-element.30.own_ref), channel_id=1, source_target_pairs={{0,64},{32,96},{64,0},{96,32},{128,192},{160,224},{192,128},{224,1... | collective-permute-start | bytes 159752 | tf_op jit(solution)/shard_map/ppermute | solution.py:523
  13.2 4.4 %collective-permute-start.2 = (f32[104,128]{1,0:T(8,128)S(1)}, f32[104,128]{1,0:T(8,128)S(1)}, u32[]{:S(2)}, u32[]{:S(2)}) collective-permute-start(f32[104,128]{1,0:T(8,128)S(1)} %get-tuple-element.30.own_ref), channel_id=1, source_target_pairs={{0,32},{32,0},{64,96},{96,64},{128,160},{160,128},{192,224},{224,1... | collective-permute-start | bytes 159752 | tf_op jit(solution)/shard_map/ppermute | solution.py:523
  17.7 7.3 %collective-permute-start.5 = (f32[48,128]{1,0:T(8,128)S(1)}, f32[48,128]{1,0:T(8,128)S(1)}, u32[]{:S(2)}, u32[]{:S(2)}) collective-permute-start(f32[48,128]{1,0:T(8,128)S(1)} %shard_map.40), channel_id=1, source_target_pairs={{0,224},{32,192},{64,160},{96,128},{128,96},{160,64},{192,32},{224... | collective-permute-start | bytes 73736 | tf_op jit(solution)/shard_map/ppermute | solution.py:525
  25.4 1.3 %collective-permute-start.6 = (f32[48,128]{1,0:T(8,128)S(1)}, f32[48,128]{1,0:T(8,128)S(1)}, u32[]{:S(2)}, u32[]{:S(2)}) collective-permute-start(f32[48,128]{1,0:T(8,128)S(1)} %get-tuple-element.36.own_ref), channel_id=1, source_target_pairs={{0,1},{1,0},{2,3},{3,2},{4,5},{5,4},{6,7},{7,6},{8,9},{9,8},{10,11... | collective-permute-start | bytes 73736 | tf_op jit(solution)/shard_map/ppermute | solution.py:532
  26.7 5.1 %collective-permute-start.9 = (f32[48,128]{1,0:T(8,128)S(1)}, f32[48,128]{1,0:T(8,128)S(1)}, u32[]{:S(2)}, u32[]{:S(2)}) collective-permute-start(f32[48,128]{1,0:T(8,128)S(1)} %shard_map.42.own_ref.small0), channel_id=1, source_target_pairs={{0,6},{1,7},{2,4},{3,5},{4,2},{5,3},{6,0},{7,1},{8,14},{9,15},{10,... | collective-permute-start | bytes 73736 | tf_op jit(solution)/shard_map/ppermute | solution.py:534
  26.8 5.7 %collective-permute-start.8 = (f32[48,128]{1,0:T(8,128)S(1)}, f32[48,128]{1,0:T(8,128)S(1)}, u32[]{:S(2)}, u32[]{:S(2)}) collective-permute-start(f32[48,128]{1,0:T(8,128)S(1)} %shard_map.42.own_ref.small0), channel_id=1, source_target_pairs={{0,4},{1,5},{2,6},{3,7},{4,0},{5,1},{6,2},{7,3},{8,12},{9,13},{10,... | collective-permute-start | bytes 73736 | tf_op jit(solution)/shard_map/ppermute | solution.py:534
  27.4 5.6 %collective-permute-start.7 = (f32[48,128]{1,0:T(8,128)S(1)}, f32[48,128]{1,0:T(8,128)S(1)}, u32[]{:S(2)}, u32[]{:S(2)}) collective-permute-start(f32[48,128]{1,0:T(8,128)S(1)} %shard_map.42.own_ref.small0), channel_id=1, source_target_pairs={{0,2},{1,3},{2,0},{3,1},{4,6},{5,7},{6,4},{7,5},{8,10},{9,11},{10,... | collective-permute-start | bytes 73736 | tf_op jit(solution)/shard_map/ppermute | solution.py:534
  33.1 5.3 %collective-permute-start.12 = (f32[48,128]{1,0:T(8,128)S(1)}, f32[48,128]{1,0:T(8,128)S(1)}, u32[]{:S(2)}, u32[]{:S(2)}) collective-permute-start(f32[48,128]{1,0:T(8,128)S(1)} %shard_map.43.large0), channel_id=1, source_target_pairs={{0,24},{1,25},{2,26},{3,27},{4,28},{5,29},{6,30},{7,31},{8,16},{9,... | collective-permute-start | bytes 73736 | tf_op jit(solution)/shard_map/ppermute | solution.py:536
  35.1 5.3 %collective-permute-start.11 = (f32[48,128]{1,0:T(8,128)S(1)}, f32[48,128]{1,0:T(8,128)S(1)}, u32[]{:S(2)}, u32[]{:S(2)}) collective-permute-start(f32[48,128]{1,0:T(8,128)S(1)} %shard_map.43.large0), channel_id=1, source_target_pairs={{0,16},{1,17},{2,18},{3,19},{4,20},{5,21},{6,22},{7,23},{8,24},{9,... | collective-permute-start | bytes 73736 | tf_op jit(solution)/shard_map/ppermute | solution.py:536
  35.5 4.9 %collective-permute-start.10 = (f32[48,128]{1,0:T(8,128)S(1)}, f32[48,128]{1,0:T(8,128)S(1)}, u32[]{:S(2)}, u32[]{:S(2)}) collective-permute-start(f32[48,128]{1,0:T(8,128)S(1)} %shard_map.43.large0), channel_id=1, source_target_pairs={{0,8},{1,9},{2,10},{3,11},{4,12},{5,13},{6,14},{7,15},{8,0},{9,1},... | collective-permute-start | bytes 73736 | tf_op jit(solution)/shard_map/ppermute | solution.py:536

commit v4 on v3

--- a/solution.py
+++ b/solution.py
@@ -65,49 +65,62 @@
 
 
 def prepare_kernel(
-    ids_hbm, table_hbm, heat_hbm, k_ref, inner_ref, outer_ref, ids_ref, table_ref, low_ref, high_ref, wide, sems
+    ids_hbm, heat_hbm, inner_ref, outer_ref, ids_low, ids_high, heat_low, heat_high, sems
 ):
     copies = [
-        pltpu.make_async_copy(table_hbm, table_ref, sems.at[0]),
-        pltpu.make_async_copy(ids_hbm, ids_ref, sems.at[1]),
-        pltpu.make_async_copy(heat_hbm.at[:, 0:8, :], low_ref, sems.at[2]),
-        pltpu.make_async_copy(heat_hbm.at[:, NY - 8 : NY, :], high_ref, sems.at[3]),
+        pltpu.make_async_copy(source, place, sems.at[i])
+        for i, (source, place) in enumerate(
+            (
+                (heat_hbm.at[:, 0:8, :], heat_low),
+                (heat_hbm.at[:, NY - 8 : NY, :], heat_high),
+                (ids_hbm.at[:, 0:8, :], ids_low),
+                (ids_hbm.at[:, MY - 8 : MY, :], ids_high),
+            )
+        )
     ]
     for copy in copies:
         copy.start()
-    wide[...] = jnp.zeros(wide.shape, f32)
-    copies[0].wait()
-    copies[1].wait()
+    core = lax.rem(lax.axis_index("gy"), 2)
+    inner_ref[NX:, :] = jnp.zeros((MX, NZ), f32)
+    outer_ref[NX:, :] = jnp.zeros((MX, NZ), f32)
+    for copy in copies:
+        copy.wait()
+    low, high = heat_low[:, 0, :], heat_high[:, 7, :]
+    inner_ref[:NX, :] = jnp.where(core == 0, high, low)
+    outer_ref[:NX, :] = jnp.where(core == 0, low, high)
+    low, high = ids_low[:, 0, :], ids_high[:, 7, :]
+    inner_ref[NX:, : NZ // 2] = jnp.where(core == 0, high, low).astype(f32)
+    outer_ref[NX:, : NZ // 2] = jnp.where(core == 0, low, high).astype(f32)
+
+
+def take(values, index):
+    return jnp.take_along_axis(values, index, axis=1, mode="promise_in_bounds")
+
+
+def chain(k):
+    joints = []
+    for m in range(len(k)):
+        joints.append(2000.0 * k[m])
+        if m + 1 < len(k):
+            joints.append(1000.0 * (k[m] + k[m + 1]))
+    return joints
+
+
+def x_matrix_kernel(
+    ids_ref, table_ref, k_ref, lookup_ref, gx_ref, hx_ref, ix_ref, px_ref, wide
+):
     ids = ids_ref[...]
     k = jnp.zeros(ids.shape, f32)
+    lookup = jnp.zeros(lookup_ref.shape, f32)
     for region in range(table_ref.shape[0]):
         k = jnp.where(ids == region, table_ref[region], k)
+        lookup = jnp.where(lanes(lookup.shape) == region, table_ref[region], lookup)
+    lookup_ref[...] = lookup
+    wide[...] = jnp.zeros(wide.shape, f32)
     wide[:, : NZ // 2] = k
-    index = lanes(wide.shape) // 2
-    k_ref[...] = jnp.take_along_axis(wide[...], index, axis=1, mode="promise_in_bounds")
-    copies[2].wait()
-    copies[3].wait()
-    low = jnp.concatenate([low_ref[:, 0, :], k_ref[pl.ds(0, MX, stride=MY), :]], 0)
-    high = jnp.concatenate([high_ref[:, 7, :], k_ref[pl.ds(MY - 1, MX, stride=MY), :]], 0)
-    core = lax.rem(lax.axis_index("gy"), 2)
-    inner_ref[...] = jnp.where(core == 0, high, low)
-    outer_ref[...] = jnp.where(core == 0, low, high)
-
-
-def matrix_kernel(
-    k_ref, gx_ref, hx_ref, ix_ref, px_ref, gy_ref, hy_ref, iy_ref, my_ref, za_ref, zc_ref, zi_ref
-):
-    at_x, at_y = lax.axis_index("gx"), lax.axis_index("gy")
-    last_x, last_y = lax.axis_size("gx") - 1, lax.axis_size("gy") - 1
-
-    def chain(k):
-        joints = []
-        for m in range(len(k)):
-            joints.append(2000.0 * k[m])
-            if m + 1 < len(k):
-                joints.append(1000.0 * (k[m] + k[m + 1]))
-        return joints
-
+    k_ref[...] = take(wide[...], lanes(wide.shape) // 2)
+    at_x = lax.axis_index("gx")
+    last_x = lax.axis_size("gx") - 1
     kx = [k_ref[m * MY : (m + 1) * MY, :] for m in range(MX)]
 
     def put_x(t, gd, hd, inv):
@@ -122,7 +135,16 @@
     px_ref[16:32, :] = pack(link, kx[0])
     px_ref[32:40, :] = pack(kx[-1][:8], kx[-1][8:])
 
+
+def yz_matrix_kernel(
+    k_ref, beside_ref, gy_ref, hy_ref, iy_ref, my_ref, mid_ref, za_ref, zc_ref, zi_ref, zo_ref
+):
+    at_y = lax.axis_index("gy")
+    last_y = lax.axis_size("gy") - 1
+    core = lax.rem(at_y, 2)
     ky = [k_ref[pl.ds(n, MX, stride=MY), :] for n in range(MY)]
+    mid_ref[...] = 1000.0 * (beside_ref[:MX, :] + jnp.where(core == 0, ky[-1], ky[0]))
+    outer = 1000.0 * (beside_ref[MX:, :] + jnp.where(core == 0, ky[0], ky[-1]))
 
     def put_y(t, gd, hd, inv):
         gy_ref[t * MX : (t + 1) * MX, :] = gd
@@ -130,9 +152,10 @@
         iy_ref[t * MX : (t + 1) * MX, :] = inv
 
     alpha, beta, link = eliminate(chain(ky), put_y)
-    my_ref[0:8, :] = alpha + jnp.where(at_y == 0, 1000.0, 0.0) * ky[0]
-    my_ref[8:16, :] = beta + jnp.where(at_y == last_y, 1000.0, 0.0) * ky[-1]
-    my_ref[16:24, :] = link
+    alpha = alpha + jnp.where(at_y == 0, 1000.0, 0.0) * ky[0]
+    beta = beta + jnp.where(at_y == last_y, 1000.0, 0.0) * ky[-1]
+    my_ref[0:8, :] = pack(alpha, beta)
+    my_ref[8:16, :] = pack(link, outer)
 
     group = 4
     for start in range(0, MY, group):
@@ -144,24 +167,45 @@
         a = jnp.where(lane == 0, 0.0, west)
         c = jnp.where(lane == NZ - 1, 0.0, east)
         size = MX * group
+
+        def double(coefficient):
+            return jnp.where(lane % 2 == 0, coefficient, pltpu.roll(coefficient, 1, 1))
+
         for s in range(7):
             step = 1 << s
             inv = 1.0 / diag
+            if s == 0:
+                for i, odd in enumerate((inv, a * inv, c * inv)):
+                    at = i * MX * MY + start * MX
+                    zo_ref[at : at + size, :] = odd
             low = a * pltpu.roll(inv, step, 1)
             high = c * pltpu.roll(inv, NZ - step, 1)
             at = s * MX * MY + start * MX
-            za_ref[at : at + size, :] = low
-            zc_ref[at : at + size, :] = high
+            if 2 * step == NZ:
+                za_ref[at : at + size, :] = double(low + high)
+            else:
+                za_ref[at : at + size, :] = double(low)
+                zc_ref[at : at + size, :] = double(high)
             diag = diag - (low * pltpu.roll(c, step, 1) + high * pltpu.roll(a, NZ - step, 1))
             a = low * pltpu.roll(a, step, 1)
             c = high * pltpu.roll(c, NZ - step, 1)
-        zi_ref[start * MX : start * MX + size, :] = 1.0 / diag
-
-
-def right_side_kernel(heat_ref, k_ref, inner_ref, outer_ref, gx_ref, hx_ref, px_ref, send_ref, rb_ref):
+        zi_ref[start * MX : start * MX + size, :] = double(1.0 / diag)
+
+
+def right_side_kernel(
+    heat_ref, k_ref, lookup_ref, outer_ref, inner_ref, gx_ref, hx_ref, px_ref, send_ref, rb_ref, beside_ref
+):
     at_y = lax.axis_index("gy")
     core = lax.rem(at_y, 2)
-    inner, outer = inner_ref[...], outer_ref[...]
+
+    def conduct(ref):
+        index = take(ref[NX:, :], lanes((MX, NZ)) // 2).astype(jnp.int32)
+        return take(lookup_ref[...], index)
+
+    inner = jnp.concatenate([inner_ref[:NX, :], conduct(inner_ref)], 0)
+    outer = jnp.concatenate([outer_ref[:NX, :], conduct(outer_ref)], 0)
+    beside_ref[:MX, :] = inner[NX:]
+    beside_ref[MX:, :] = outer[NX:]
     low = jnp.where(at_y == 0, 0.0, jnp.where(core == 0, outer, inner))
     high = jnp.where(at_y == lax.axis_size("gy") - 1, 0.0, jnp.where(core == 0, inner, outer))
     shape = (MY, NZ)
@@ -264,8 +308,8 @@
 
 
 def x_solve_kernel(
-    own_ref, one_ref, two_ref, three_ref, half_ref, heat_ref, k_ref, inner_ref, outer_ref, rb_ref, gx_ref,
-    hx_ref, ix_ref, gy_ref, hy_ref, my_ref, core_ref, mid_ref, rby_ref, first,
+    own_ref, one_ref, two_ref, three_ref, half_ref, heat_ref, rb_ref, gx_ref, hx_ref, ix_ref, gy_ref, hy_ref,
+    my_ref, core_ref, rby_ref, first,
 ):
     at = lax.axis_index("gx")
     place = lax.rem(at, 4)
@@ -331,17 +375,11 @@
         new = side(t + 2)
         ra = [a + b * hd for a, b in zip(ra, rb)]
         rb = [n + b * gd for n, b in zip(new, rb)]
-    core = lax.rem(lax.axis_index("gy"), 2)
-    k_low = k_ref[pl.ds(0, MX, stride=MY), :]
-    k_high = k_ref[pl.ds(MY - 1, MX, stride=MY), :]
-    mid_ref[...] = 1000.0 * (inner_ref[NX:, :] + jnp.where(core == 0, k_high, k_low))
-    outer = 1000.0 * (outer_ref[NX:, :] + jnp.where(core == 0, k_low, k_high))
     core_ref[0:8, :] = ra[0]
     core_ref[8:16, :] = ra[1]
     core_ref[16:24, :] = rb[0]
     core_ref[24:32, :] = rb[1]
-    core_ref[32:40, :] = pack(my_ref[0:8, :], my_ref[8:16, :])
-    core_ref[40:48, :] = pack(my_ref[16:24, :], outer)
+    core_ref[32:48, :] = my_ref[...]
 
 
 def y_segment(rows):
@@ -405,7 +443,7 @@
 
 def y_solve_kernel(
     large0, large1, large2, large3, small0, small1, small2, small3, own_ref, other_ref, mid_ref, rb_ref, gy_ref,
-    hy_ref, iy_ref, za_ref, zc_ref, zi_ref, heat_ref, out_ref, second,
+    hy_ref, iy_ref, za_ref, zc_ref, zi_ref, zo_ref, heat_ref, out_ref, second,
 ):
     at_y = lax.axis_index("gy")
     core, chip = lax.rem(at_y, 2), lax.div(at_y, 2)
@@ -454,26 +492,47 @@
         u_next = [(inv * b[p] + hd * u_first[p]) + gd * u_next[p] for p in range(2)]
         keep(y, u_next)
 
+    even = lanes((MX, NZ)) % 2 == 0
+
+    def turned(v, step):
+        return pltpu.roll(v, step % NZ, 1)
+
     for n in range(MY):
-        cells = [(2 * n + q, p) for q in range(2) for p in range(2)]
-        v = [second[y * NX + p * MX : y * NX + (p + 1) * MX, :] for y, p in cells]
-        for s in range(7):
-            step = 1 << s
-            at = s * MX * MY + n * MX
-            low, high = za_ref[at : at + MX, :], zc_ref[at : at + MX, :]
-            v = [w + (low * pltpu.roll(w, step, 1) + high * pltpu.roll(w, NZ - step, 1)) for w in v]
-        inv = zi_ref[n * MX : (n + 1) * MX, :]
-        for (y, p), w in zip(cells, v):
-            where = pl.ds(p * NY + y, MX, stride=2 * NY)
-            out_ref[where, :] = heat_ref[where, :] + inv * w
-
-
-def call(kernel, ins, outs, scratch=(), outside=False, cost=20000, limit=8 << 20):
+        rows = slice(n * MX, (n + 1) * MX)
+        inv, odd, odd_low, odd_high = zi_ref[rows, :], *(
+            zo_ref[i * MX * MY + n * MX : i * MX * MY + (n + 1) * MX, :] for i in range(3)
+        )
+        for p in range(2):
+            a, b = (second[y * NX + p * MX : y * NX + (p + 1) * MX, :] for y in (2 * n, 2 * n + 1))
+            w = jnp.where(even, a, turned(b, 1))
+            before = jnp.where(even, turned(a, 1), turned(b, 2))
+            after = jnp.where(even, turned(a, -1), b)
+            for s in range(7):
+                step = 1 << s
+                at = slice(s * MX * MY + n * MX, s * MX * MY + (n + 1) * MX)
+                if s > 0:
+                    before = turned(w, step)
+                if 2 * step == NZ:
+                    w = w + za_ref[at, :] * before
+                else:
+                    if s > 0:
+                        after = turned(w, -step)
+                    w = w + (za_ref[at, :] * before + zc_ref[at, :] * after)
+            w = inv * w
+            next_w = turned(w, -1)
+            a = jnp.where(even, w, odd * a + (odd_low * turned(w, 1) + odd_high * next_w))
+            b = jnp.where(even, next_w, odd * b + (odd_low * w + odd_high * turned(w, -2)))
+            for y, v in ((2 * n, a), (2 * n + 1, b)):
+                where = pl.ds(p * NY + y, MX, stride=2 * NY)
+                out_ref[where, :] = heat_ref[where, :] + v
+
+
+def call(kernel, ins, outs, scratch=(), outside=False, smem=(), cost=20000, limit=8 << 20):
     space = pltpu.HBM if outside else pltpu.VMEM
     return pl.pallas_call(
         kernel,
         out_shape=tuple(jax.ShapeDtypeStruct(s, f32) for s in outs),
-        in_specs=[pl.BlockSpec(memory_space=space) for _ in ins],
+        in_specs=[pl.BlockSpec(memory_space=pltpu.SMEM if i in smem else space) for i in range(len(ins))],
         out_specs=tuple(pl.BlockSpec(memory_space=pltpu.VMEM) for _ in outs),
         scratch_shapes=scratch,
         compiler_params=pltpu.CompilerParams(vmem_limit_bytes=limit),
@@ -485,48 +544,52 @@
     heat = starting_heat_state.reshape(NX * NY, NZ)
     ids = material_zone_ids.reshape(MX * MY, NZ // 2)
     nx, ny = lax.axis_size("gx"), lax.axis_size("gy")
-    k, inner, outer = call(
+    inner, outer = call(
         prepare_kernel,
-        (ids, zone_diffusivity_lookup, starting_heat_state),
-        [(MX * MY, NZ), (NX + MX, NZ), (NX + MX, NZ)],
+        (material_zone_ids, starting_heat_state),
+        [(NX + MX, NZ)] * 2,
         scratch=[
-            pltpu.VMEM(ids.shape, jnp.int32),
-            pltpu.SMEM(zone_diffusivity_lookup.shape, f32),
+            pltpu.VMEM((MX, 8, NZ // 2), jnp.int32),
+            pltpu.VMEM((MX, 8, NZ // 2), jnp.int32),
             pltpu.VMEM((NX, 8, NZ), f32),
             pltpu.VMEM((NX, 8, NZ), f32),
-            pltpu.VMEM((MX * MY, NZ), f32),
             pltpu.SemaphoreType.DMA((4,)),
         ],
         outside=True,
-        limit=55500 << 10,
+        limit=55180 << 10,
     )
     cores = [(i, i ^ 1) for i in range(ny)]
     inner = lax.ppermute(inner, "gy", cores)
     outer = lax.ppermute(outer, "gy", [(i, (i + (1 if i % 2 else -1)) % ny) for i in range(ny)])
     tx, ty = NX - 2, NY - 2
-    gx, hx, ix, px, gy, hy, iy, my, za, zc, zi = call(
-        matrix_kernel,
-        (k,),
-        [(tx * MY, NZ)] * 3
-        + [(40, NZ)]
-        + [(ty * MX, NZ)] * 3
-        + [(24, NZ)]
-        + [(7 * MX * MY, NZ)] * 2
-        + [(MX * MY, NZ)],
+    k, lookup, gx, hx, ix, px = call(
+        x_matrix_kernel,
+        (ids, zone_diffusivity_lookup),
+        [(MX * MY, NZ), (8, NZ)] + [(tx * MY, NZ)] * 3 + [(40, NZ)],
+        scratch=[pltpu.VMEM((MX * MY, NZ), f32)],
+        smem=(1,),
+        cost=2000000,
+    )
+    send, rbx, beside = call(
+        right_side_kernel,
+        (heat, k, lookup, outer, inner, gx, hx, px),
+        [(XROWS, NZ), (tx * NY, NZ), (2 * MX, NZ)],
+    )
+    near = [send] + [lax.ppermute(send, "gx", [(i, i ^ d) for i in range(nx)]) for d in (1, 2, 3)]
+    gy, hy, iy, my, mid, za, zc, zi, zo = call(
+        yz_matrix_kernel,
+        (k, beside),
+        [(ty * MX, NZ)] * 3
+        + [(2 * MX, NZ), (MX, NZ)]
+        + [(7 * MX * MY, NZ), (6 * MX * MY, NZ), (MX * MY, NZ), (3 * MX * MY, NZ)],
         cost=4000000,
     )
-    send, rbx = call(
-        right_side_kernel,
-        (heat, k, inner, outer, gx, hx, px),
-        [(XROWS, NZ), (tx * NY, NZ)],
-    )
-    near = [send] + [lax.ppermute(send, "gx", [(i, i ^ d) for i in range(nx)]) for d in (1, 2, 3)]
     (half,) = call(x_half_kernel, near, [(48, NZ)])
     half = lax.ppermute(half, "gx", [(i, nx - 1 - i) for i in range(nx)])
-    own, mid, rby = call(
+    own, rby = call(
         x_solve_kernel,
-        (*near, half, heat, k, inner, outer, rbx, gx, hx, ix, gy, hy, my),
-        [(YROWS, NZ), (MX, NZ), (ty * MX * 2, NZ)],
+        (*near, half, heat, rbx, gx, hx, ix, gy, hy, my),
+        [(YROWS, NZ), (ty * NX, NZ)],
         scratch=[pltpu.VMEM((NX * NY, NZ), f32)],
     )
     other = lax.ppermute(own, "gy", cores)
@@ -536,7 +599,7 @@
     large = [four] + [lax.ppermute(four, "gy", [(i, i ^ (8 * d)) for i in range(ny)]) for d in (1, 2, 3)]
     (out,) = call(
         y_solve_kernel,
-        (*large, *small, own, other, mid, rby, gy, hy, iy, za, zc, zi, heat),
+        (*large, *small, own, other, mid, rby, gy, hy, iy, za, zc, zi, zo, heat),
         [(NX * NY, NZ)],
         scratch=[pltpu.VMEM((NX * NY, NZ), f32)],
     )

time: 42.8 us -> 41.4 us (0.967)
  starting transfers between devices: 24.1 us -> 23.1 us
  waiting for transfers between devices: 11.5 us -> 10.9 us
  Pallas kernels: 6.11 us -> 6.58 us
    ppermute x1, waiting for transfers between devices: 1.81 us -> 0.01 us  [on_device(): half = lax.ppermute(half, 'gx', [(i, nx - 1 - i) for i in range(nx)])]
    ppermute x1, starting transfers between devices: 5.31 us -> 4.74 us  [on_device(): lax.ppermute(outer, 'gy', [(i, (i + (1 if i % 2 else -1)) % ny) for i in...]
    ppermute x3, waiting for transfers between devices: 3.18 us -> 3.69 us  [on_device(): lax.ppermute(four, 'gy', [(i, i ^ 8 * d) for i in range(ny)])]
    pallas_call x8 -> x9, Pallas kernels: 6.11 us -> 6.58 us  [call(): pl.pallas_call(kernel, out_shape=tuple((jax.ShapeDtypeStruct(s, f32) for...]
  transfers between devices with their start and end apart: 13 -> 13, of which waited for: 9 -> 9; matrix products, arithmetic and copies ran while one was open for 0% -> 0% of each run, Pallas kernels for 3% -> 7%
where the time goes in v4:
time: 41.4 us; the launch traced here: 41.3 us
  starting transfers between devices  23.1 us (56%)
  waiting for transfers between devices  10.9 us (26%)
  Pallas kernels  6.58 us (16%)
  local copies, waits for them, and re-layouts  0.66 us (2%)
    pallas_call x9, Pallas kernels, call(): pl.pallas_call(kernel, out_shape=tuple((jax.ShapeDtypeStruct(s, f32) for...  6.58 us
    ppermute x1, starting transfers between devices, on_device(): half = lax.ppermute(half, 'gx', [(i, nx - 1 - i) for i in range(nx)])  5.1 us
    ppermute x3, starting transfers between devices, on_device(): lax.ppermute(send, 'gx', [(i, i ^ d) for i in range(nx)])  4.82 us
    ppermute x1, starting transfers between devices, on_device(): lax.ppermute(outer, 'gy', [(i, (i + (1 if i % 2 else -1)) % ny) for i in...  4.74 us
    ppermute x3, starting transfers between devices, on_device(): lax.ppermute(chip, 'gy', [(i, i ^ 2 * d) for i in range(ny)])  4.18 us
    ppermute x3, starting transfers between devices, on_device(): lax.ppermute(four, 'gy', [(i, i ^ 8 * d) for i in range(ny)])  4.18 us
    ppermute x3, waiting for transfers between devices, on_device(): lax.ppermute(four, 'gy', [(i, i ^ 8 * d) for i in range(ny)])  3.69 us
    ppermute x3, waiting for transfers between devices, on_device(): lax.ppermute(send, 'gx', [(i, i ^ d) for i in range(nx)])  3.6 us
  transfers between devices with their start and end apart: 13, of which 9 were waited for; matrix products, arithmetic and copies ran while one was open for 0% of the time, Pallas kernels for 7%

profile of v4, /device:TPU:32, one launch (start us, length us, event | category | flops | bytes accessed | tf_op | source)
XLA Modules:
  0.0 41.3 jit_solution(4521459594200878606)
XLA Ops:
  0.0 0.0 copy-start.1
  0.0 0.0 copy-start
  0.0 1.0 %shard_map.38 = (f32[24,128]{1,0:T(8,128)S(1)}, f32[24,128]{1,0:T(8,128)S(1)}) custom-call(s32[8,16,64]{2,1,0:T(8,128)} %ids_hbm.1, f32[16,32,128]{2,1,0:T(8,128)} %heat_hbm.1), custom_call_target="tpu_custom_call" | custom-call | flops 20000 | bytes 20000 | tf_op jit(solution)/shard_map/pallas_call | solution.py:532
  1.0 4.7 %collective-permute-start = (f32[24,128]{1,0:T(8,128)S(1)}, f32[24,128]{1,0:T(8,128)S(1)}, u32[]{:S(2)}, u32[]{:S(2)}) collective-permute-start(f32[24,128]{1,0:T(8,128)S(1)} %get-tuple-element.29), channel_id=1, source_target_pairs={{0,31},{1,2},{2,1},{3,4},{4,3},{5,6},{6,5},{7,8},{8,7},{9,10},{10,... | collective-permute-start | bytes 36872 | tf_op jit(solution)/shard_map/ppermute | solution.py:563
  5.7 0.0 copy-start.2
  5.7 0.0 collective-permute-start.1
  5.7 0.0 copy-done.1
  5.7 0.6 %copy-done.2 = f32[16]{0:T(128)S(1)} copy-done((f32[16]{0:T(128)S(1)}, f32[16]{0:T(128)}, u32[]{:S(2)}) %copy-start.2) | copy-done | bytes 88
  6.4 0.8 %shard_map.37 = (f32[128,128]{1,0:T(8,128)S(1)}, f32[8,128]{1,0:T(8,128)S(1)}, f32[224,128]{1,0:T(8,128)S(1)}, f32[224,128]{1,0:T(8,128)S(1)}, f32[224,128]{1,0:T(8,128)S(1)}, /*index=5*/f32[40,128]{1,0:T(8,128)S(1)}) custom-call(s32[128,64]{1,0:T(8,128)S(1)} %bitcast.6, f32[16]{0:T(128)S(1)} %copy-done.2), custom_call_target="tpu_custom_call" | custom-call | flops 2000000 | bytes 2000000 | tf_op jit(solution)/shard_map/pallas_call | solution.py:532
  7.2 0.3 collective-permute-done.outer_ref
  7.5 0.0 collective-permute-done.1.inner_ref
  7.5 0.0 copy-done
  7.5 0.3 shard_map.39
  7.8 2.0 %collective-permute-start.4 = (f32[104,128]{1,0:T(8,128)S(1)}, f32[104,128]{1,0:T(8,128)S(1)}, u32[]{:S(2)}, u32[]{:S(2)}) collective-permute-start(f32[104,128]{1,0:T(8,128)S(1)} %get-tuple-element.34.own_ref), channel_id=1, source_target_pairs={{0,96},{32,64},{64,32},{96,0},{128,224},{160,192},{192,160},{224,1... | collective-permute-start | bytes 159752 | tf_op jit(solution)/shard_map/ppermute | solution.py:578
  9.8 2.3 %collective-permute-start.3 = (f32[104,128]{1,0:T(8,128)S(1)}, f32[104,128]{1,0:T(8,128)S(1)}, u32[]{:S(2)}, u32[]{:S(2)}) collective-permute-start(f32[104,128]{1,0:T(8,128)S(1)} %get-tuple-element.34.own_ref), channel_id=1, source_target_pairs={{0,64},{32,96},{64,0},{96,32},{128,192},{160,224},{192,128},{224,1... | collective-permute-start | bytes 159752 | tf_op jit(solution)/shard_map/ppermute | solution.py:578
  12.1 0.5 %collective-permute-start.2 = (f32[104,128]{1,0:T(8,128)S(1)}, f32[104,128]{1,0:T(8,128)S(1)}, u32[]{:S(2)}, u32[]{:S(2)}) collective-permute-start(f32[104,128]{1,0:T(8,128)S(1)} %get-tuple-element.34.own_ref), channel_id=1, source_target_pairs={{0,32},{32,0},{64,96},{96,64},{128,160},{160,128},{192,224},{224,1... | collective-permute-start | bytes 159752 | tf_op jit(solution)/shard_map/ppermute | solution.py:578
  12.7 0.0 collective-permute-done.4.three_ref
  12.7 2.3 %collective-permute-done.3.two_ref = f32[104,128]{1,0:T(8,128)S(1)} collective-permute-done((f32[104,128]{1,0:T(8,128)S(1)}, f32[104,128]{1,0:T(8,128)S(1)}, u32[]{:S(2)}, u32[]{:S(2)}) %collective-permute-start.3) | collective-permute-done | bytes 53280 | tf_op jit(solution)/shard_map/ppermute | solution.py:578
  14.9 1.3 %collective-permute-done.2.one_ref = f32[104,128]{1,0:T(8,128)S(1)} collective-permute-done((f32[104,128]{1,0:T(8,128)S(1)}, f32[104,128]{1,0:T(8,128)S(1)}, u32[]{:S(2)}, u32[]{:S(2)}) %collective-permute-start.2) | collective-permute-done | bytes 53280 | tf_op jit(solution)/shard_map/ppermute | solution.py:578
  16.3 0.1 shard_map.40
  16.4 5.1 %collective-permute-start.5 = (f32[48,128]{1,0:T(8,128)S(1)}, f32[48,128]{1,0:T(8,128)S(1)}, u32[]{:S(2)}, u32[]{:S(2)}) collective-permute-start(f32[48,128]{1,0:T(8,128)S(1)} %shard_map.40), channel_id=1, source_target_pairs={{0,224},{32,192},{64,160},{96,128},{128,96},{160,64},{192,32},{224... | collective-permute-start | bytes 73736 | tf_op jit(solution)/shard_map/ppermute | solution.py:588
  21.5 1.9 %shard_map.41 = (f32[240,128]{1,0:T(8,128)S(1)}, f32[240,128]{1,0:T(8,128)S(1)}, f32[240,128]{1,0:T(8,128)S(1)}, f32[16,128]{1,0:T(8,128)S(1)}, f32[8,128]{1,0:T...) custom-call(f32[128,128]{1,0:T(8,128)S(1)} %get-tuple-element.27.k_r, ...), custom_call_target="tpu_custom_call" | custom-call | flops 4000000 | bytes 4000000 | tf_op jit(solution)/shard_map/pallas_call | solution.py:532
  23.4 0.0 collective-permute-done.5.half_ref
  23.4 0.4 shard_map.42
  23.8 0.1 collective-permute-start.6
  23.9 1.2 %collective-permute-done.6.other_ref = f32[48,128]{1,0:T(8,128)S(1)} collective-permute-done((f32[48,128]{1,0:T(8,128)S(1)}, f32[48,128]{1,0:T(8,128)S(1)}, u32[]{:S(2)}, u32[]{:S(2)}) %collective-permute-start.6) | collective-permute-done | bytes 24608 | tf_op jit(solution)/shard_map/ppermute | solution.py:595
  25.1 0.1 shard_map.43.own_ref.small0
  25.2 0.2 collective-permute-start.9
  25.4 0.6 %collective-permute-start.8 = (f32[48,128]{1,0:T(8,128)S(1)}, f32[48,128]{1,0:T(8,128)S(1)}, u32[]{:S(2)}, u32[]{:S(2)}) collective-permute-start(f32[48,128]{1,0:T(8,128)S(1)} %shard_map.43.own_ref.small0), channel_id=1, source_target_pairs={{0,4},{1,5},{2,6},{3,7},{4,0},{5,1},{6,2},{7,3},{8,12},{9,13},{10,... | collective-permute-start | bytes 73736 | tf_op jit(solution)/shard_map/ppermute | solution.py:597
  26.0 3.4 %collective-permute-start.7 = (f32[48,128]{1,0:T(8,128)S(1)}, f32[48,128]{1,0:T(8,128)S(1)}, u32[]{:S(2)}, u32[]{:S(2)}) collective-permute-start(f32[48,128]{1,0:T(8,128)S(1)} %shard_map.43.own_ref.small0), channel_id=1, source_target_pairs={{0,2},{1,3},{2,0},{3,1},{4,6},{5,7},{6,4},{7,5},{8,10},{9,11},{10,... | collective-permute-start | bytes 73736 | tf_op jit(solution)/shard_map/ppermute | solution.py:597
  29.4 0.9 %collective-permute-done.9.three_ref.small3 = f32[48,128]{1,0:T(8,128)S(1)} collective-permute-done((f32[48,128]{1,0:T(8,128)S(1)}, f32[48,128]{1,0:T(8,128)S(1)}, u32[]{:S(2)}, u32[]{:S(2)}) %collective-permute-start.9) | collective-permute-done | bytes 24608 | tf_op jit(solution)/shard_map/ppermute | solution.py:597
  30.3 0.6 %collective-permute-done.8.two_ref.small2 = f32[48,128]{1,0:T(8,128)S(1)} collective-permute-done((f32[48,128]{1,0:T(8,128)S(1)}, f32[48,128]{1,0:T(8,128)S(1)}, u32[]{:S(2)}, u32[]{:S(2)}) %collective-permute-start.8) | collective-permute-done | bytes 24608 | tf_op jit(solution)/shard_map/ppermute | solution.py:597
  31.0 0.5 %collective-permute-done.7.one_ref.small1 = f32[48,128]{1,0:T(8,128)S(1)} collective-permute-done((f32[48,128]{1,0:T(8,128)S(1)}, f32[48,128]{1,0:T(8,128)S(1)}, u32[]{:S(2)}, u32[]{:S(2)}) %collective-permute-start.7) | collective-permute-done | bytes 24608 | tf_op jit(solution)/shard_map/ppermute | solution.py:597
  31.5 0.1 shard_map.44.large0
  31.6 2.5 %collective-permute-start.12 = (f32[48,128]{1,0:T(8,128)S(1)}, f32[48,128]{1,0:T(8,128)S(1)}, u32[]{:S(2)}, u32[]{:S(2)}) collective-permute-start(f32[48,128]{1,0:T(8,128)S(1)} %shard_map.44.large0), channel_id=1, source_target_pairs={{0,24},{1,25},{2,26},{3,27},{4,28},{5,29},{6,30},{7,31},{8,16},{9,... | collective-permute-start | bytes 73736 | tf_op jit(solution)/shard_map/ppermute | solution.py:599
  34.1 0.4 collective-permute-start.11
  34.5 1.3 %collective-permute-start.10 = (f32[48,128]{1,0:T(8,128)S(1)}, f32[48,128]{1,0:T(8,128)S(1)}, u32[]{:S(2)}, u32[]{:S(2)}) collective-permute-start(f32[48,128]{1,0:T(8,128)S(1)} %shard_map.44.large0), channel_id=1, source_target_pairs={{0,8},{1,9},{2,10},{3,11},{4,12},{5,13},{6,14},{7,15},{8,0},{9,1},... | collective-permute-start | bytes 73736 | tf_op jit(solution)/shard_map/ppermute | solution.py:599
  35.8 0.9 %collective-permute-done.12.large3 = f32[48,128]{1,0:T(8,128)S(1)} collective-permute-done((f32[48,128]{1,0:T(8,128)S(1)}, f32[48,128]{1,0:T(8,128)S(1)}, u32[]{:S(2)}, u32[]{:S(2)}) %collective-permute-start.12) | collective-permute-done | bytes 24608 | tf_op jit(solution)/shard_map/ppermute | solution.py:599
  36.7 2.7 %collective-permute-done.11.large2 = f32[48,128]{1,0:T(8,128)S(1)} collective-permute-done((f32[48,128]{1,0:T(8,128)S(1)}, f32[48,128]{1,0:T(8,128)S(1)}, u32[]{:S(2)}, u32[]{:S(2)}) %collective-permute-start.11) | collective-permute-done | bytes 24608 | tf_op jit(solution)/shard_map/ppermute | solution.py:599
  39.5 0.0 collective-permute-done.10.large1
  39.5 1.8 %shard_map.45 = f32[512,128]{1,0:T(8,128)} custom-call(f32[48,128]{1,0:T(8,128)S(1)} %shard_map.44.large0, f32[48,128]{1,0:T(8,128)S(1)} %collective-permute-done.10.large1, f32[48,128]{1,0:T(8,128)S(1)} %collective-permute-done.11.large2, f32[48,128]{1,0:T(8,128)S(1)} %collective-permute-done.12.large3, f32[48,128]{1,0:T(8,128)S(1)} %shard_map.43.own_ref.small0, ...), custom_call_target="tpu_custom_call" | custom-call | flops 20000 | bytes 20000 | tf_op jit(solution)/shard_map/pallas_call | solution.py:532
Async XLA Ops:
  0.0 5.7 %copy-start.1 = (s32[8,16,64]{2,1,0:T(8,128)S(1)}, s32[8,16,64]{2,1,0:T(8,128)}, u32[]{:S(2)}) copy-start(s32[8,16,64]{2,1,0:T(8,128)} %ids_hbm.1) | copy-start | bytes 98308
  0.0 7.5 %copy-start = (f32[16,32,128]{2,1,0:T(8,128)S(1)}, f32[16,32,128]{2,1,0:T(8,128)}, u32[]{:S(2)}) copy-start(f32[16,32,128]{2,1,0:T(8,128)} %heat_hbm.1) | copy-start | bytes 786436
  1.0 6.5 %collective-permute-start = (f32[24,128]{1,0:T(8,128)S(1)}, f32[24,128]{1,0:T(8,128)S(1)}, u32[]{:S(2)}, u32[]{:S(2)}) collective-permute-start(f32[24,128]{1,0:T(8,128)S(1)} %get-tuple-element.29), channel_id=1, source_target_pairs={{0,31},{1,2},{2,1},{3,4},{4,3},{5,6},{6,5},{7,8},{8,7},{9,10},{10,... | collective-permute-start | bytes 36872 | tf_op jit(solution)/shard_map/ppermute | solution.py:563
  5.7 0.7 %copy-start.2 = (f32[16]{0:T(128)S(1)}, f32[16]{0:T(128)}, u32[]{:S(2)}) copy-start(f32[16]{0:T(128)} %table_ref.1) | copy-start | bytes 196
  5.7 1.8 %collective-permute-start.1 = (f32[24,128]{1,0:T(8,128)S(1)}, f32[24,128]{1,0:T(8,128)S(1)}, u32[]{:S(2)}, u32[]{:S(2)}) collective-permute-start(f32[24,128]{1,0:T(8,128)S(1)} %get-tuple-element.30), channel_id=1, source_target_pairs={{0,1},{1,0},{2,3},{3,2},{4,5},{5,4},{6,7},{7,6},{8,9},{9,8},{10,11... | collective-permute-start | bytes 36872 | tf_op jit(solution)/shard_map/ppermute | solution.py:562
  7.8 4.8 %collective-permute-start.4 = (f32[104,128]{1,0:T(8,128)S(1)}, f32[104,128]{1,0:T(8,128)S(1)}, u32[]{:S(2)}, u32[]{:S(2)}) collective-permute-start(f32[104,128]{1,0:T(8,128)S(1)} %get-tuple-element.34.own_ref), channel_id=1, source_target_pairs={{0,96},{32,64},{64,32},{96,0},{128,224},{160,192},{192,160},{224,1... | collective-permute-start | bytes 159752 | tf_op jit(solution)/shard_map/ppermute | solution.py:578
  9.8 5.1 %collective-permute-start.3 = (f32[104,128]{1,0:T(8,128)S(1)}, f32[104,128]{1,0:T(8,128)S(1)}, u32[]{:S(2)}, u32[]{:S(2)}) collective-permute-start(f32[104,128]{1,0:T(8,128)S(1)} %get-tuple-element.34.own_ref), channel_id=1, source_target_pairs={{0,64},{32,96},{64,0},{96,32},{128,192},{160,224},{192,128},{224,1... | collective-permute-start | bytes 159752 | tf_op jit(solution)/shard_map/ppermute | solution.py:578
  12.1 4.1 %collective-permute-start.2 = (f32[104,128]{1,0:T(8,128)S(1)}, f32[104,128]{1,0:T(8,128)S(1)}, u32[]{:S(2)}, u32[]{:S(2)}) collective-permute-start(f32[104,128]{1,0:T(8,128)S(1)} %get-tuple-element.34.own_ref), channel_id=1, source_target_pairs={{0,32},{32,0},{64,96},{96,64},{128,160},{160,128},{192,224},{224,1... | collective-permute-start | bytes 159752 | tf_op jit(solution)/shard_map/ppermute | solution.py:578
  16.4 7.0 %collective-permute-start.5 = (f32[48,128]{1,0:T(8,128)S(1)}, f32[48,128]{1,0:T(8,128)S(1)}, u32[]{:S(2)}, u32[]{:S(2)}) collective-permute-start(f32[48,128]{1,0:T(8,128)S(1)} %shard_map.40), channel_id=1, source_target_pairs={{0,224},{32,192},{64,160},{96,128},{128,96},{160,64},{192,32},{224... | collective-permute-start | bytes 73736 | tf_op jit(solution)/shard_map/ppermute | solution.py:588
  23.8 1.3 %collective-permute-start.6 = (f32[48,128]{1,0:T(8,128)S(1)}, f32[48,128]{1,0:T(8,128)S(1)}, u32[]{:S(2)}, u32[]{:S(2)}) collective-permute-start(f32[48,128]{1,0:T(8,128)S(1)} %get-tuple-element.41.own_ref), channel_id=1, source_target_pairs={{0,1},{1,0},{2,3},{3,2},{4,5},{5,4},{6,7},{7,6},{8,9},{9,8},{10,11... | collective-permute-start | bytes 73736 | tf_op jit(solution)/shard_map/ppermute | solution.py:595
  25.2 5.1 %collective-permute-start.9 = (f32[48,128]{1,0:T(8,128)S(1)}, f32[48,128]{1,0:T(8,128)S(1)}, u32[]{:S(2)}, u32[]{:S(2)}) collective-permute-start(f32[48,128]{1,0:T(8,128)S(1)} %shard_map.43.own_ref.small0), channel_id=1, source_target_pairs={{0,6},{1,7},{2,4},{3,5},{4,2},{5,3},{6,0},{7,1},{8,14},{9,15},{10,... | collective-permute-start | bytes 73736 | tf_op jit(solution)/shard_map/ppermute | solution.py:597
  25.4 5.6 %collective-permute-start.8 = (f32[48,128]{1,0:T(8,128)S(1)}, f32[48,128]{1,0:T(8,128)S(1)}, u32[]{:S(2)}, u32[]{:S(2)}) collective-permute-start(f32[48,128]{1,0:T(8,128)S(1)} %shard_map.43.own_ref.small0), channel_id=1, source_target_pairs={{0,4},{1,5},{2,6},{3,7},{4,0},{5,1},{6,2},{7,3},{8,12},{9,13},{10,... | collective-permute-start | bytes 73736 | tf_op jit(solution)/shard_map/ppermute | solution.py:597
  26.0 5.5 %collective-permute-start.7 = (f32[48,128]{1,0:T(8,128)S(1)}, f32[48,128]{1,0:T(8,128)S(1)}, u32[]{:S(2)}, u32[]{:S(2)}) collective-permute-start(f32[48,128]{1,0:T(8,128)S(1)} %shard_map.43.own_ref.small0), channel_id=1, source_target_pairs={{0,2},{1,3},{2,0},{3,1},{4,6},{5,7},{6,4},{7,5},{8,10},{9,11},{10,... | collective-permute-start | bytes 73736 | tf_op jit(solution)/shard_map/ppermute | solution.py:597
  31.6 5.1 %collective-permute-start.12 = (f32[48,128]{1,0:T(8,128)S(1)}, f32[48,128]{1,0:T(8,128)S(1)}, u32[]{:S(2)}, u32[]{:S(2)}) collective-permute-start(f32[48,128]{1,0:T(8,128)S(1)} %shard_map.44.large0), channel_id=1, source_target_pairs={{0,24},{1,25},{2,26},{3,27},{4,28},{5,29},{6,30},{7,31},{8,16},{9,... | collective-permute-start | bytes 73736 | tf_op jit(solution)/shard_map/ppermute | solution.py:599
  34.1 5.3 %collective-permute-start.11 = (f32[48,128]{1,0:T(8,128)S(1)}, f32[48,128]{1,0:T(8,128)S(1)}, u32[]{:S(2)}, u32[]{:S(2)}) collective-permute-start(f32[48,128]{1,0:T(8,128)S(1)} %shard_map.44.large0), channel_id=1, source_target_pairs={{0,16},{1,17},{2,18},{3,19},{4,20},{5,21},{6,22},{7,23},{8,24},{9,... | collective-permute-start | bytes 73736 | tf_op jit(solution)/shard_map/ppermute | solution.py:599
  34.5 5.0 %collective-permute-start.10 = (f32[48,128]{1,0:T(8,128)S(1)}, f32[48,128]{1,0:T(8,128)S(1)}, u32[]{:S(2)}, u32[]{:S(2)}) collective-permute-start(f32[48,128]{1,0:T(8,128)S(1)} %shard_map.44.large0), channel_id=1, source_target_pairs={{0,8},{1,9},{2,10},{3,11},{4,12},{5,13},{6,14},{7,15},{8,0},{9,1},... | collective-permute-start | bytes 73736 | tf_op jit(solution)/shard_map/ppermute | solution.py:599

commit v5 on v4

--- a/solution.py
+++ b/solution.py
@@ -136,9 +136,7 @@
     px_ref[32:40, :] = pack(kx[-1][:8], kx[-1][8:])
 
 
-def yz_matrix_kernel(
-    k_ref, beside_ref, gy_ref, hy_ref, iy_ref, my_ref, mid_ref, za_ref, zc_ref, zi_ref, zo_ref
-):
+def y_matrix_kernel(k_ref, beside_ref, gy_ref, hy_ref, iy_ref, my_ref, mid_ref):
     at_y = lax.axis_index("gy")
     last_y = lax.axis_size("gy") - 1
     core = lax.rem(at_y, 2)
@@ -157,7 +155,10 @@
     my_ref[0:8, :] = pack(alpha, beta)
     my_ref[8:16, :] = pack(link, outer)
 
-    group = 4
+
+def z_matrix_kernel(k_ref, za_ref, zc_ref, zi_ref, zo_ref):
+    ky = [k_ref[pl.ds(n, MX, stride=MY), :] for n in range(MY)]
+    group = 16
     for start in range(0, MY, group):
         k = jnp.concatenate(ky[start : start + group], 0)
         lane = lanes(k.shape)
@@ -576,13 +577,11 @@
         [(XROWS, NZ), (tx * NY, NZ), (2 * MX, NZ)],
     )
     near = [send] + [lax.ppermute(send, "gx", [(i, i ^ d) for i in range(nx)]) for d in (1, 2, 3)]
-    gy, hy, iy, my, mid, za, zc, zi, zo = call(
-        yz_matrix_kernel,
+    gy, hy, iy, my, mid = call(
+        y_matrix_kernel,
         (k, beside),
-        [(ty * MX, NZ)] * 3
-        + [(2 * MX, NZ), (MX, NZ)]
-        + [(7 * MX * MY, NZ), (6 * MX * MY, NZ), (MX * MY, NZ), (3 * MX * MY, NZ)],
-        cost=4000000,
+        [(ty * MX, NZ)] * 3 + [(2 * MX, NZ), (MX, NZ)],
+        cost=2000000,
     )
     (half,) = call(x_half_kernel, near, [(48, NZ)])
     half = lax.ppermute(half, "gx", [(i, nx - 1 - i) for i in range(nx)])
@@ -594,6 +593,13 @@
     )
     other = lax.ppermute(own, "gy", cores)
     (chip,) = call(chip_kernel, (own, other, mid), [(YROWS, NZ)])
+    chip, k = lax.optimization_barrier((chip, k))
+    za, zc, zi, zo = call(
+        z_matrix_kernel,
+        (k,),
+        [(7 * MX * MY, NZ), (6 * MX * MY, NZ), (MX * MY, NZ), (3 * MX * MY, NZ)],
+        cost=4000000,
+    )
     small = [chip] + [lax.ppermute(chip, "gy", [(i, i ^ (2 * d)) for i in range(ny)]) for d in (1, 2, 3)]
     (four,) = call(y_four_kernel, small, [(YROWS, NZ)])
     large = [four] + [lax.ppermute(four, "gy", [(i, i ^ (8 * d)) for i in range(ny)]) for d in (1, 2, 3)]

time: 41.4 us -> 41.1 us (level)
    ppermute x3, waiting for transfers between devices: 3.69 us -> 2 us  [on_device(): lax.ppermute(four, 'gy', [(i, i ^ 8 * d) for i in range(ny)])]
    ppermute x1, waiting for transfers between devices: 0.01 us -> 1.59 us  [on_device(): half = lax.ppermute(half, 'gx', [(i, nx - 1 - i) for i in range(nx)])]
    pallas_call x9 -> x10, Pallas kernels: 6.58 us -> 6.36 us  [call(): pl.pallas_call(kernel, out_shape=tuple((jax.ShapeDtypeStruct(s, f32) for...]
  transfers between devices with their start and end apart: 13 -> 13, of which waited for: 9 -> 9; matrix products, arithmetic and copies ran while one was open for 0% -> 0% of each run, Pallas kernels for 7% -> 6%
where the time goes in v5:
time: 41.1 us; the launch traced here: 41 us
  starting transfers between devices  23.1 us (56%)
  waiting for transfers between devices  10.8 us (26%)
  Pallas kernels  6.36 us (15%)
  local copies, waits for them, and re-layouts  0.66 us (2%)
    pallas_call x10, Pallas kernels, call(): pl.pallas_call(kernel, out_shape=tuple((jax.ShapeDtypeStruct(s, f32) for...  6.36 us
    ppermute x1, starting transfers between devices, on_device(): half = lax.ppermute(half, 'gx', [(i, nx - 1 - i) for i in range(nx)])  5.1 us
    ppermute x3, starting transfers between devices, on_device(): lax.ppermute(send, 'gx', [(i, i ^ d) for i in range(nx)])  4.82 us
    ppermute x1, starting transfers between devices, on_device(): lax.ppermute(outer, 'gy', [(i, (i + (1 if i % 2 else -1)) % ny) for i in...  4.74 us
    ppermute x3, starting transfers between devices, on_device(): lax.ppermute(chip, 'gy', [(i, i ^ 2 * d) for i in range(ny)])  4.18 us
    ppermute x3, starting transfers between devices, on_device(): lax.ppermute(four, 'gy', [(i, i ^ 8 * d) for i in range(ny)])  4.18 us
    ppermute x3, waiting for transfers between devices, on_device(): lax.ppermute(send, 'gx', [(i, i ^ d) for i in range(nx)])  3.6 us
    ppermute x3, waiting for transfers between devices, on_device(): lax.ppermute(chip, 'gy', [(i, i ^ 2 * d) for i in range(ny)])  2.06 us
  transfers between devices with their start and end apart: 13, of which 9 were waited for; matrix products, arithmetic and copies ran while one was open for 0% of the time, Pallas kernels for 6%

profile of v5, /device:TPU:32, one launch (start us, length us, event | category | flops | bytes accessed | tf_op | source)
XLA Modules:
  0.0 41.0 jit_solution(9242831958293830137)
XLA Ops:
  0.0 0.0 copy-start.1
  0.0 0.0 copy-start
  0.0 1.0 %shard_map.38 = (f32[24,128]{1,0:T(8,128)S(1)}, f32[24,128]{1,0:T(8,128)S(1)}) custom-call(s32[8,16,64]{2,1,0:T(8,128)} %ids_hbm.1, f32[16,32,128]{2,1,0:T(8,128)} %heat_hbm.1), custom_call_target="tpu_custom_call" | custom-call | flops 20000 | bytes 20000 | tf_op jit(solution)/shard_map/pallas_call | solution.py:533
  1.0 4.7 %collective-permute-start = (f32[24,128]{1,0:T(8,128)S(1)}, f32[24,128]{1,0:T(8,128)S(1)}, u32[]{:S(2)}, u32[]{:S(2)}) collective-permute-start(f32[24,128]{1,0:T(8,128)S(1)} %get-tuple-element.31), channel_id=1, source_target_pairs={{0,31},{1,2},{2,1},{3,4},{4,3},{5,6},{6,5},{7,8},{8,7},{9,10},{10,... | collective-permute-start | bytes 36872 | tf_op jit(solution)/shard_map/ppermute | solution.py:564
  5.7 0.0 copy-start.2
  5.7 0.0 collective-permute-start.1
  5.7 0.0 copy-done.1
  5.7 0.6 %copy-done.2 = f32[16]{0:T(128)S(1)} copy-done((f32[16]{0:T(128)S(1)}, f32[16]{0:T(128)}, u32[]{:S(2)}) %copy-start.2) | copy-done | bytes 88
  6.4 0.8 %shard_map.37 = (f32[128,128]{1,0:T(8,128)S(1)}, f32[8,128]{1,0:T(8,128)S(1)}, f32[224,128]{1,0:T(8,128)S(1)}, f32[224,128]{1,0:T(8,128)S(1)}, f32[224,128]{1,0:T(8,128)S(1)}, /*index=5*/f32[40,128]{1,0:T(8,128)S(1)}) custom-call(s32[128,64]{1,0:T(8,128)S(1)} %bitcast.6, f32[16]{0:T(128)S(1)} %copy-done.2), custom_call_target="tpu_custom_call" | custom-call | flops 2000000 | bytes 2000000 | tf_op jit(solution)/shard_map/pallas_call | solution.py:533
  7.2 0.3 collective-permute-done.outer_ref
  7.5 0.0 collective-permute-done.1.inner_ref
  7.5 0.0 copy-done
  7.5 0.3 shard_map.39
  7.8 2.0 %collective-permute-start.4 = (f32[104,128]{1,0:T(8,128)S(1)}, f32[104,128]{1,0:T(8,128)S(1)}, u32[]{:S(2)}, u32[]{:S(2)}) collective-permute-start(f32[104,128]{1,0:T(8,128)S(1)} %get-tuple-element.36.own_ref), channel_id=1, source_target_pairs={{0,96},{32,64},{64,32},{96,0},{128,224},{160,192},{192,160},{224,1... | collective-permute-start | bytes 159752 | tf_op jit(solution)/shard_map/ppermute | solution.py:579
  9.8 2.3 %collective-permute-start.3 = (f32[104,128]{1,0:T(8,128)S(1)}, f32[104,128]{1,0:T(8,128)S(1)}, u32[]{:S(2)}, u32[]{:S(2)}) collective-permute-start(f32[104,128]{1,0:T(8,128)S(1)} %get-tuple-element.36.own_ref), channel_id=1, source_target_pairs={{0,64},{32,96},{64,0},{96,32},{128,192},{160,224},{192,128},{224,1... | collective-permute-start | bytes 159752 | tf_op jit(solution)/shard_map/ppermute | solution.py:579
  12.1 0.5 %collective-permute-start.2 = (f32[104,128]{1,0:T(8,128)S(1)}, f32[104,128]{1,0:T(8,128)S(1)}, u32[]{:S(2)}, u32[]{:S(2)}) collective-permute-start(f32[104,128]{1,0:T(8,128)S(1)} %get-tuple-element.36.own_ref), channel_id=1, source_target_pairs={{0,32},{32,0},{64,96},{96,64},{128,160},{160,128},{192,224},{224,1... | collective-permute-start | bytes 159752 | tf_op jit(solution)/shard_map/ppermute | solution.py:579
  12.6 0.0 collective-permute-done.4.three_ref
  12.6 2.3 %collective-permute-done.3.two_ref = f32[104,128]{1,0:T(8,128)S(1)} collective-permute-done((f32[104,128]{1,0:T(8,128)S(1)}, f32[104,128]{1,0:T(8,128)S(1)}, u32[]{:S(2)}, u32[]{:S(2)}) %collective-permute-start.3) | collective-permute-done | bytes 53280 | tf_op jit(solution)/shard_map/ppermute | solution.py:579
  14.9 1.3 %collective-permute-done.2.one_ref = f32[104,128]{1,0:T(8,128)S(1)} collective-permute-done((f32[104,128]{1,0:T(8,128)S(1)}, f32[104,128]{1,0:T(8,128)S(1)}, u32[]{:S(2)}, u32[]{:S(2)}) %collective-permute-start.2) | collective-permute-done | bytes 53280 | tf_op jit(solution)/shard_map/ppermute | solution.py:579
  16.2 0.1 shard_map.40
  16.4 5.1 %collective-permute-start.5 = (f32[48,128]{1,0:T(8,128)S(1)}, f32[48,128]{1,0:T(8,128)S(1)}, u32[]{:S(2)}, u32[]{:S(2)}) collective-permute-start(f32[48,128]{1,0:T(8,128)S(1)} %shard_map.40), channel_id=1, source_target_pairs={{0,224},{32,192},{64,160},{96,128},{128,96},{160,64},{192,32},{224... | collective-permute-start | bytes 73736 | tf_op jit(solution)/shard_map/ppermute | solution.py:587
  21.5 0.3 shard_map.41
  21.8 1.6 %collective-permute-done.5.half_ref = f32[48,128]{1,0:T(8,128)S(1)} collective-permute-done((f32[48,128]{1,0:T(8,128)S(1)}, f32[48,128]{1,0:T(8,128)S(1)}, u32[]{:S(2)}, u32[]{:S(2)}) %collective-permute-start.5) | collective-permute-done | bytes 24608 | tf_op jit(solution)/shard_map/ppermute | solution.py:587
  23.4 0.4 shard_map.42
  23.8 0.1 collective-permute-start.6
  23.9 1.2 %collective-permute-done.6.other_ref = f32[48,128]{1,0:T(8,128)S(1)} collective-permute-done((f32[48,128]{1,0:T(8,128)S(1)}, f32[48,128]{1,0:T(8,128)S(1)}, u32[]{:S(2)}, u32[]{:S(2)}) %collective-permute-start.6) | collective-permute-done | bytes 24608 | tf_op jit(solution)/shard_map/ppermute | solution.py:594
  25.1 0.1 shard_map.43.own_ref.small0
  25.2 0.2 collective-permute-start.9
  25.4 0.6 %collective-permute-start.8 = (f32[48,128]{1,0:T(8,128)S(1)}, f32[48,128]{1,0:T(8,128)S(1)}, u32[]{:S(2)}, u32[]{:S(2)}) collective-permute-start(f32[48,128]{1,0:T(8,128)S(1)} %shard_map.43.own_ref.small0), channel_id=1, source_target_pairs={{0,4},{1,5},{2,6},{3,7},{4,0},{5,1},{6,2},{7,3},{8,12},{9,13},{10,... | collective-permute-start | bytes 73736 | tf_op jit(solution)/shard_map/ppermute | solution.py:603
  26.0 3.4 %collective-permute-start.7 = (f32[48,128]{1,0:T(8,128)S(1)}, f32[48,128]{1,0:T(8,128)S(1)}, u32[]{:S(2)}, u32[]{:S(2)}) collective-permute-start(f32[48,128]{1,0:T(8,128)S(1)} %shard_map.43.own_ref.small0), channel_id=1, source_target_pairs={{0,2},{1,3},{2,0},{3,1},{4,6},{5,7},{6,4},{7,5},{8,10},{9,11},{10,... | collective-permute-start | bytes 73736 | tf_op jit(solution)/shard_map/ppermute | solution.py:603
  29.4 0.9 %collective-permute-done.9.three_ref.small3 = f32[48,128]{1,0:T(8,128)S(1)} collective-permute-done((f32[48,128]{1,0:T(8,128)S(1)}, f32[48,128]{1,0:T(8,128)S(1)}, u32[]{:S(2)}, u32[]{:S(2)}) %collective-permute-start.9) | collective-permute-done | bytes 24608 | tf_op jit(solution)/shard_map/ppermute | solution.py:603
  30.3 0.6 %collective-permute-done.8.two_ref.small2 = f32[48,128]{1,0:T(8,128)S(1)} collective-permute-done((f32[48,128]{1,0:T(8,128)S(1)}, f32[48,128]{1,0:T(8,128)S(1)}, u32[]{:S(2)}, u32[]{:S(2)}) %collective-permute-start.8) | collective-permute-done | bytes 24608 | tf_op jit(solution)/shard_map/ppermute | solution.py:603
  31.0 0.5 %collective-permute-done.7.one_ref.small1 = f32[48,128]{1,0:T(8,128)S(1)} collective-permute-done((f32[48,128]{1,0:T(8,128)S(1)}, f32[48,128]{1,0:T(8,128)S(1)}, u32[]{:S(2)}, u32[]{:S(2)}) %collective-permute-start.7) | collective-permute-done | bytes 24608 | tf_op jit(solution)/shard_map/ppermute | solution.py:603
  31.4 0.1 shard_map.44.large0
  31.6 2.3 %collective-permute-start.12 = (f32[48,128]{1,0:T(8,128)S(1)}, f32[48,128]{1,0:T(8,128)S(1)}, u32[]{:S(2)}, u32[]{:S(2)}) collective-permute-start(f32[48,128]{1,0:T(8,128)S(1)} %shard_map.44.large0), channel_id=1, source_target_pairs={{0,24},{1,25},{2,26},{3,27},{4,28},{5,29},{6,30},{7,31},{8,16},{9,... | collective-permute-start | bytes 73736 | tf_op jit(solution)/shard_map/ppermute | solution.py:605
  33.8 0.6 %collective-permute-start.11 = (f32[48,128]{1,0:T(8,128)S(1)}, f32[48,128]{1,0:T(8,128)S(1)}, u32[]{:S(2)}, u32[]{:S(2)}) collective-permute-start(f32[48,128]{1,0:T(8,128)S(1)} %shard_map.44.large0), channel_id=1, source_target_pairs={{0,16},{1,17},{2,18},{3,19},{4,20},{5,21},{6,22},{7,23},{8,24},{9,... | collective-permute-start | bytes 73736 | tf_op jit(solution)/shard_map/ppermute | solution.py:605
  34.5 1.3 %collective-permute-start.10 = (f32[48,128]{1,0:T(8,128)S(1)}, f32[48,128]{1,0:T(8,128)S(1)}, u32[]{:S(2)}, u32[]{:S(2)}) collective-permute-start(f32[48,128]{1,0:T(8,128)S(1)} %shard_map.44.large0), channel_id=1, source_target_pairs={{0,8},{1,9},{2,10},{3,11},{4,12},{5,13},{6,14},{7,15},{8,0},{9,1},... | collective-permute-start | bytes 73736 | tf_op jit(solution)/shard_map/ppermute | solution.py:605
  35.7 1.4 %shard_map.45 = (f32[896,128]{1,0:T(8,128)S(1)}, f32[768,128]{1,0:T(8,128)S(1)}, f32[128,128]{1,0:T(8,128)S(1)}, f32[384,128]{1,0:T(8,128)S(1)}) custom-call(f32[128,128]{1,0:T(8,128)S(1)} %get-tuple-element.48.k_ref), custom_call_target="tpu_custom_call" | custom-call | flops 4000000 | bytes 4000000 | tf_op jit(solution)/shard_map/pallas_call | solution.py:533
  37.1 0.0 collective-permute-done.12.large3
  37.2 2.0 %collective-permute-done.11.large2 = f32[48,128]{1,0:T(8,128)S(1)} collective-permute-done((f32[48,128]{1,0:T(8,128)S(1)}, f32[48,128]{1,0:T(8,128)S(1)}, u32[]{:S(2)}, u32[]{:S(2)}) %collective-permute-start.11) | collective-permute-done | bytes 24608 | tf_op jit(solution)/shard_map/ppermute | solution.py:605
  39.2 0.0 collective-permute-done.10.large1
  39.2 1.8 %shard_map.46 = f32[512,128]{1,0:T(8,128)} custom-call(f32[48,128]{1,0:T(8,128)S(1)} %shard_map.44.large0, f32[48,128]{1,0:T(8,128)S(1)} %collective-permute-done.10.large1, f32[48,128]{1,0:T(8,128)S(1)} %collective-permute-done.11.large2, f32[48,128]{1,0:T(8,128)S(1)} %collective-permute-done.12.large3, f32[48,128]{1,0:T(8,128)S(1)} %shard_map.43.own_ref.small0, ...), custom_call_target="tpu_custom_call" | custom-call | flops 20000 | bytes 20000 | tf_op jit(solution)/shard_map/pallas_call | solution.py:533
Async XLA Ops:
  0.0 5.7 %copy-start.1 = (s32[8,16,64]{2,1,0:T(8,128)S(1)}, s32[8,16,64]{2,1,0:T(8,128)}, u32[]{:S(2)}) copy-start(s32[8,16,64]{2,1,0:T(8,128)} %ids_hbm.1) | copy-start | bytes 98308
  0.0 7.5 %copy-start = (f32[16,32,128]{2,1,0:T(8,128)S(1)}, f32[16,32,128]{2,1,0:T(8,128)}, u32[]{:S(2)}) copy-start(f32[16,32,128]{2,1,0:T(8,128)} %heat_hbm.1) | copy-start | bytes 786436
  1.0 6.5 %collective-permute-start = (f32[24,128]{1,0:T(8,128)S(1)}, f32[24,128]{1,0:T(8,128)S(1)}, u32[]{:S(2)}, u32[]{:S(2)}) collective-permute-start(f32[24,128]{1,0:T(8,128)S(1)} %get-tuple-element.31), channel_id=1, source_target_pairs={{0,31},{1,2},{2,1},{3,4},{4,3},{5,6},{6,5},{7,8},{8,7},{9,10},{10,... | collective-permute-start | bytes 36872 | tf_op jit(solution)/shard_map/ppermute | solution.py:564
  5.7 0.7 %copy-start.2 = (f32[16]{0:T(128)S(1)}, f32[16]{0:T(128)}, u32[]{:S(2)}) copy-start(f32[16]{0:T(128)} %table_ref.1) | copy-start | bytes 196
  5.7 1.8 %collective-permute-start.1 = (f32[24,128]{1,0:T(8,128)S(1)}, f32[24,128]{1,0:T(8,128)S(1)}, u32[]{:S(2)}, u32[]{:S(2)}) collective-permute-start(f32[24,128]{1,0:T(8,128)S(1)} %get-tuple-element.32), channel_id=1, source_target_pairs={{0,1},{1,0},{2,3},{3,2},{4,5},{5,4},{6,7},{7,6},{8,9},{9,8},{10,11... | collective-permute-start | bytes 36872 | tf_op jit(solution)/shard_map/ppermute | solution.py:563
  7.8 4.8 %collective-permute-start.4 = (f32[104,128]{1,0:T(8,128)S(1)}, f32[104,128]{1,0:T(8,128)S(1)}, u32[]{:S(2)}, u32[]{:S(2)}) collective-permute-start(f32[104,128]{1,0:T(8,128)S(1)} %get-tuple-element.36.own_ref), channel_id=1, source_target_pairs={{0,96},{32,64},{64,32},{96,0},{128,224},{160,192},{192,160},{224,1... | collective-permute-start | bytes 159752 | tf_op jit(solution)/shard_map/ppermute | solution.py:579
  9.8 5.1 %collective-permute-start.3 = (f32[104,128]{1,0:T(8,128)S(1)}, f32[104,128]{1,0:T(8,128)S(1)}, u32[]{:S(2)}, u32[]{:S(2)}) collective-permute-start(f32[104,128]{1,0:T(8,128)S(1)} %get-tuple-element.36.own_ref), channel_id=1, source_target_pairs={{0,64},{32,96},{64,0},{96,32},{128,192},{160,224},{192,128},{224,1... | collective-permute-start | bytes 159752 | tf_op jit(solution)/shard_map/ppermute | solution.py:579
  12.1 4.1 %collective-permute-start.2 = (f32[104,128]{1,0:T(8,128)S(1)}, f32[104,128]{1,0:T(8,128)S(1)}, u32[]{:S(2)}, u32[]{:S(2)}) collective-permute-start(f32[104,128]{1,0:T(8,128)S(1)} %get-tuple-element.36.own_ref), channel_id=1, source_target_pairs={{0,32},{32,0},{64,96},{96,64},{128,160},{160,128},{192,224},{224,1... | collective-permute-start | bytes 159752 | tf_op jit(solution)/shard_map/ppermute | solution.py:579
  16.4 7.0 %collective-permute-start.5 = (f32[48,128]{1,0:T(8,128)S(1)}, f32[48,128]{1,0:T(8,128)S(1)}, u32[]{:S(2)}, u32[]{:S(2)}) collective-permute-start(f32[48,128]{1,0:T(8,128)S(1)} %shard_map.40), channel_id=1, source_target_pairs={{0,224},{32,192},{64,160},{96,128},{128,96},{160,64},{192,32},{224... | collective-permute-start | bytes 73736 | tf_op jit(solution)/shard_map/ppermute | solution.py:587
  23.8 1.3 %collective-permute-start.6 = (f32[48,128]{1,0:T(8,128)S(1)}, f32[48,128]{1,0:T(8,128)S(1)}, u32[]{:S(2)}, u32[]{:S(2)}) collective-permute-start(f32[48,128]{1,0:T(8,128)S(1)} %get-tuple-element.43.own_ref), channel_id=1, source_target_pairs={{0,1},{1,0},{2,3},{3,2},{4,5},{5,4},{6,7},{7,6},{8,9},{9,8},{10,11... | collective-permute-start | bytes 73736 | tf_op jit(solution)/shard_map/ppermute | solution.py:594
  25.2 5.1 %collective-permute-start.9 = (f32[48,128]{1,0:T(8,128)S(1)}, f32[48,128]{1,0:T(8,128)S(1)}, u32[]{:S(2)}, u32[]{:S(2)}) collective-permute-start(f32[48,128]{1,0:T(8,128)S(1)} %shard_map.43.own_ref.small0), channel_id=1, source_target_pairs={{0,6},{1,7},{2,4},{3,5},{4,2},{5,3},{6,0},{7,1},{8,14},{9,15},{10,... | collective-permute-start | bytes 73736 | tf_op jit(solution)/shard_map/ppermute | solution.py:603
  25.4 5.6 %collective-permute-start.8 = (f32[48,128]{1,0:T(8,128)S(1)}, f32[48,128]{1,0:T(8,128)S(1)}, u32[]{:S(2)}, u32[]{:S(2)}) collective-permute-start(f32[48,128]{1,0:T(8,128)S(1)} %shard_map.43.own_ref.small0), channel_id=1, source_target_pairs={{0,4},{1,5},{2,6},{3,7},{4,0},{5,1},{6,2},{7,3},{8,12},{9,13},{10,... | collective-permute-start | bytes 73736 | tf_op jit(solution)/shard_map/ppermute | solution.py:603
  26.0 5.4 %collective-permute-start.7 = (f32[48,128]{1,0:T(8,128)S(1)}, f32[48,128]{1,0:T(8,128)S(1)}, u32[]{:S(2)}, u32[]{:S(2)}) collective-permute-start(f32[48,128]{1,0:T(8,128)S(1)} %shard_map.43.own_ref.small0), channel_id=1, source_target_pairs={{0,2},{1,3},{2,0},{3,1},{4,6},{5,7},{6,4},{7,5},{8,10},{9,11},{10,... | collective-permute-start | bytes 73736 | tf_op jit(solution)/shard_map/ppermute | solution.py:603
  31.6 5.6 %collective-permute-start.12 = (f32[48,128]{1,0:T(8,128)S(1)}, f32[48,128]{1,0:T(8,128)S(1)}, u32[]{:S(2)}, u32[]{:S(2)}) collective-permute-start(f32[48,128]{1,0:T(8,128)S(1)} %shard_map.44.large0), channel_id=1, source_target_pairs={{0,24},{1,25},{2,26},{3,27},{4,28},{5,29},{6,30},{7,31},{8,16},{9,... | collective-permute-start | bytes 73736 | tf_op jit(solution)/shard_map/ppermute | solution.py:605
  33.8 5.3 %collective-permute-start.11 = (f32[48,128]{1,0:T(8,128)S(1)}, f32[48,128]{1,0:T(8,128)S(1)}, u32[]{:S(2)}, u32[]{:S(2)}) collective-permute-start(f32[48,128]{1,0:T(8,128)S(1)} %shard_map.44.large0), channel_id=1, source_target_pairs={{0,16},{1,17},{2,18},{3,19},{4,20},{5,21},{6,22},{7,23},{8,24},{9,... | collective-permute-start | bytes 73736 | tf_op jit(solution)/shard_map/ppermute | solution.py:605
  34.5 4.7 %collective-permute-start.10 = (f32[48,128]{1,0:T(8,128)S(1)}, f32[48,128]{1,0:T(8,128)S(1)}, u32[]{:S(2)}, u32[]{:S(2)}) collective-permute-start(f32[48,128]{1,0:T(8,128)S(1)} %shard_map.44.large0), channel_id=1, source_target_pairs={{0,8},{1,9},{2,10},{3,11},{4,12},{5,13},{6,14},{7,15},{8,0},{9,1},... | collective-permute-start | bytes 73736 | tf_op jit(solution)/shard_map/ppermute | solution.py:605

commit v6 on v5

--- a/solution.py
+++ b/solution.py
@@ -71,10 +71,10 @@
         pltpu.make_async_copy(source, place, sems.at[i])
         for i, (source, place) in enumerate(
             (
-                (heat_hbm.at[:, 0:8, :], heat_low),
-                (heat_hbm.at[:, NY - 8 : NY, :], heat_high),
-                (ids_hbm.at[:, 0:8, :], ids_low),
-                (ids_hbm.at[:, MY - 8 : MY, :], ids_high),
+                (heat_hbm.at[:, 0:1, :], heat_low),
+                (heat_hbm.at[:, NY - 1 : NY, :], heat_high),
+                (ids_hbm.at[:, 0:1, :], ids_low),
+                (ids_hbm.at[:, MY - 1 : MY, :], ids_high),
             )
         )
     ]
@@ -85,10 +85,10 @@
     outer_ref[NX:, :] = jnp.zeros((MX, NZ), f32)
     for copy in copies:
         copy.wait()
-    low, high = heat_low[:, 0, :], heat_high[:, 7, :]
+    low, high = heat_low[:, 0, :], heat_high[:, 0, :]
     inner_ref[:NX, :] = jnp.where(core == 0, high, low)
     outer_ref[:NX, :] = jnp.where(core == 0, low, high)
-    low, high = ids_low[:, 0, :], ids_high[:, 7, :]
+    low, high = ids_low[:, 0, :], ids_high[:, 0, :]
     inner_ref[NX:, : NZ // 2] = jnp.where(core == 0, high, low).astype(f32)
     outer_ref[NX:, : NZ // 2] = jnp.where(core == 0, low, high).astype(f32)
 
@@ -156,7 +156,12 @@
     my_ref[8:16, :] = pack(link, outer)
 
 
-def z_matrix_kernel(k_ref, za_ref, zc_ref, zi_ref, zo_ref):
+def z_matrix_kernel(k_ref, heat_ref, za_ref, zc_ref, zi_ref, zo_ref, turned_ref):
+    for y in range(NY):
+        for p in range(2):
+            turned_ref[y * NX + p * MX : y * NX + (p + 1) * MX, :] = heat_ref[
+                pl.ds(p * NY + y, MX, stride=2 * NY), :
+            ]
     ky = [k_ref[pl.ds(n, MX, stride=MY), :] for n in range(MY)]
     group = 16
     for start in range(0, MY, group):
@@ -525,7 +530,7 @@
             b = jnp.where(even, next_w, odd * b + (odd_low * w + odd_high * turned(w, -2)))
             for y, v in ((2 * n, a), (2 * n + 1, b)):
                 where = pl.ds(p * NY + y, MX, stride=2 * NY)
-                out_ref[where, :] = heat_ref[where, :] + v
+                out_ref[where, :] = heat_ref[y * NX + p * MX : y * NX + (p + 1) * MX, :] + v
 
 
 def call(kernel, ins, outs, scratch=(), outside=False, smem=(), cost=20000, limit=8 << 20):
@@ -550,10 +555,10 @@
         (material_zone_ids, starting_heat_state),
         [(NX + MX, NZ)] * 2,
         scratch=[
-            pltpu.VMEM((MX, 8, NZ // 2), jnp.int32),
-            pltpu.VMEM((MX, 8, NZ // 2), jnp.int32),
-            pltpu.VMEM((NX, 8, NZ), f32),
-            pltpu.VMEM((NX, 8, NZ), f32),
+            pltpu.VMEM((MX, 1, NZ // 2), jnp.int32),
+            pltpu.VMEM((MX, 1, NZ // 2), jnp.int32),
+            pltpu.VMEM((NX, 1, NZ), f32),
+            pltpu.VMEM((NX, 1, NZ), f32),
             pltpu.SemaphoreType.DMA((4,)),
         ],
         outside=True,
@@ -594,10 +599,10 @@
     other = lax.ppermute(own, "gy", cores)
     (chip,) = call(chip_kernel, (own, other, mid), [(YROWS, NZ)])
     chip, k = lax.optimization_barrier((chip, k))
-    za, zc, zi, zo = call(
+    za, zc, zi, zo, turned = call(
         z_matrix_kernel,
-        (k,),
-        [(7 * MX * MY, NZ), (6 * MX * MY, NZ), (MX * MY, NZ), (3 * MX * MY, NZ)],
+        (k, heat),
+        [(7 * MX * MY, NZ), (6 * MX * MY, NZ), (MX * MY, NZ), (3 * MX * MY, NZ), (NX * NY, NZ)],
         cost=4000000,
     )
     small = [chip] + [lax.ppermute(chip, "gy", [(i, i ^ (2 * d)) for i in range(ny)]) for d in (1, 2, 3)]
@@ -605,7 +610,7 @@
     large = [four] + [lax.ppermute(four, "gy", [(i, i ^ (8 * d)) for i in range(ny)]) for d in (1, 2, 3)]
     (out,) = call(
         y_solve_kernel,
-        (*large, *small, own, other, mid, rby, gy, hy, iy, za, zc, zi, zo, heat),
+        (*large, *small, own, other, mid, rby, gy, hy, iy, za, zc, zi, zo, turned),
         [(NX * NY, NZ)],
         scratch=[pltpu.VMEM((NX * NY, NZ), f32)],
     )

time: 41.1 us -> 40.8 us (level)
  no operation moved by 1% of the time
where the time goes in v6:
time: 40.8 us; the launch traced here: 40.7 us
  starting transfers between devices  23.1 us (57%)
  waiting for transfers between devices  10.7 us (26%)
  Pallas kernels  6.2 us (15%)
  local copies, waits for them, and re-layouts  0.66 us (2%)
    pallas_call x10, Pallas kernels, call(): pl.pallas_call(kernel, out_shape=tuple((jax.ShapeDtypeStruct(s, f32) for...  6.2 us
    ppermute x1, starting transfers between devices, on_device(): half = lax.ppermute(half, 'gx', [(i, nx - 1 - i) for i in range(nx)])  5.1 us
    ppermute x3, starting transfers between devices, on_device(): lax.ppermute(send, 'gx', [(i, i ^ d) for i in range(nx)])  4.82 us
    ppermute x1, starting transfers between devices, on_device(): lax.ppermute(outer, 'gy', [(i, (i + (1 if i % 2 else -1)) % ny) for i in...  4.74 us
    ppermute x3, starting transfers between devices, on_device(): lax.ppermute(chip, 'gy', [(i, i ^ 2 * d) for i in range(ny)])  4.18 us
    ppermute x3, starting transfers between devices, on_device(): lax.ppermute(four, 'gy', [(i, i ^ 8 * d) for i in range(ny)])  4.18 us
    ppermute x3, waiting for transfers between devices, on_device(): lax.ppermute(send, 'gx', [(i, i ^ d) for i in range(nx)])  3.6 us
    ppermute x3, waiting for transfers between devices, on_device(): lax.ppermute(chip, 'gy', [(i, i ^ 2 * d) for i in range(ny)])  2.06 us
  transfers between devices with their start and end apart: 13, of which 9 were waited for; matrix products, arithmetic and copies ran while one was open for 0% of the time, Pallas kernels for 6%

profile of v6, /device:TPU:32, one launch (start us, length us, event | category | flops | bytes accessed | tf_op | source)
XLA Modules:
  0.0 40.7 jit_solution(7858500652060626928)
XLA Ops:
  0.0 0.0 copy-start.1
  0.0 0.0 copy-start
  0.0 0.8 %shard_map.38 = (f32[24,128]{1,0:T(8,128)S(1)}, f32[24,128]{1,0:T(8,128)S(1)}) custom-call(s32[8,16,64]{2,1,0:T(8,128)} %ids_hbm.1, f32[16,32,128]{2,1,0:T(8,128)} %heat_hbm.1), custom_call_target="tpu_custom_call" | custom-call | flops 20000 | bytes 20000 | tf_op jit(solution)/shard_map/pallas_call | solution.py:538
  0.9 4.7 %collective-permute-start = (f32[24,128]{1,0:T(8,128)S(1)}, f32[24,128]{1,0:T(8,128)S(1)}, u32[]{:S(2)}, u32[]{:S(2)}) collective-permute-start(f32[24,128]{1,0:T(8,128)S(1)} %get-tuple-element.32), channel_id=1, source_target_pairs={{0,31},{1,2},{2,1},{3,4},{4,3},{5,6},{6,5},{7,8},{8,7},{9,10},{10,... | collective-permute-start | bytes 36872 | tf_op jit(solution)/shard_map/ppermute | solution.py:569
  5.6 0.0 copy-start.2
  5.6 0.0 collective-permute-start.1
  5.6 0.0 copy-done.1
  5.6 0.6 %copy-done.2 = f32[16]{0:T(128)S(1)} copy-done((f32[16]{0:T(128)S(1)}, f32[16]{0:T(128)}, u32[]{:S(2)}) %copy-start.2) | copy-done | bytes 88
  6.2 0.8 %shard_map.37 = (f32[128,128]{1,0:T(8,128)S(1)}, f32[8,128]{1,0:T(8,128)S(1)}, f32[224,128]{1,0:T(8,128)S(1)}, f32[224,128]{1,0:T(8,128)S(1)}, f32[224,128]{1,0:T(8,128)S(1)}, /*index=5*/f32[40,128]{1,0:T(8,128)S(1)}) custom-call(s32[128,64]{1,0:T(8,128)S(1)} %bitcast.6, f32[16]{0:T(128)S(1)} %copy-done.2), custom_call_target="tpu_custom_call" | custom-call | flops 2000000 | bytes 2000000 | tf_op jit(solution)/shard_map/pallas_call | solution.py:538
  7.1 0.3 collective-permute-done.outer_ref
  7.4 0.0 collective-permute-done.1.inner_ref
  7.4 0.0 copy-done
  7.4 0.3 shard_map.39
  7.7 2.0 %collective-permute-start.4 = (f32[104,128]{1,0:T(8,128)S(1)}, f32[104,128]{1,0:T(8,128)S(1)}, u32[]{:S(2)}, u32[]{:S(2)}) collective-permute-start(f32[104,128]{1,0:T(8,128)S(1)} %get-tuple-element.37.own_ref), channel_id=1, source_target_pairs={{0,96},{32,64},{64,32},{96,0},{128,224},{160,192},{192,160},{224,1... | collective-permute-start | bytes 159752 | tf_op jit(solution)/shard_map/ppermute | solution.py:584
  9.7 2.3 %collective-permute-start.3 = (f32[104,128]{1,0:T(8,128)S(1)}, f32[104,128]{1,0:T(8,128)S(1)}, u32[]{:S(2)}, u32[]{:S(2)}) collective-permute-start(f32[104,128]{1,0:T(8,128)S(1)} %get-tuple-element.37.own_ref), channel_id=1, source_target_pairs={{0,64},{32,96},{64,0},{96,32},{128,192},{160,224},{192,128},{224,1... | collective-permute-start | bytes 159752 | tf_op jit(solution)/shard_map/ppermute | solution.py:584
  12.0 0.5 %collective-permute-start.2 = (f32[104,128]{1,0:T(8,128)S(1)}, f32[104,128]{1,0:T(8,128)S(1)}, u32[]{:S(2)}, u32[]{:S(2)}) collective-permute-start(f32[104,128]{1,0:T(8,128)S(1)} %get-tuple-element.37.own_ref), channel_id=1, source_target_pairs={{0,32},{32,0},{64,96},{96,64},{128,160},{160,128},{192,224},{224,1... | collective-permute-start | bytes 159752 | tf_op jit(solution)/shard_map/ppermute | solution.py:584
  12.5 0.0 collective-permute-done.4.three_ref
  12.5 2.3 %collective-permute-done.3.two_ref = f32[104,128]{1,0:T(8,128)S(1)} collective-permute-done((f32[104,128]{1,0:T(8,128)S(1)}, f32[104,128]{1,0:T(8,128)S(1)}, u32[]{:S(2)}, u32[]{:S(2)}) %collective-permute-start.3) | collective-permute-done | bytes 53280 | tf_op jit(solution)/shard_map/ppermute | solution.py:584
  14.8 1.3 %collective-permute-done.2.one_ref = f32[104,128]{1,0:T(8,128)S(1)} collective-permute-done((f32[104,128]{1,0:T(8,128)S(1)}, f32[104,128]{1,0:T(8,128)S(1)}, u32[]{:S(2)}, u32[]{:S(2)}) %collective-permute-start.2) | collective-permute-done | bytes 53280 | tf_op jit(solution)/shard_map/ppermute | solution.py:584
  16.1 0.1 shard_map.40
  16.3 5.1 %collective-permute-start.5 = (f32[48,128]{1,0:T(8,128)S(1)}, f32[48,128]{1,0:T(8,128)S(1)}, u32[]{:S(2)}, u32[]{:S(2)}) collective-permute-start(f32[48,128]{1,0:T(8,128)S(1)} %shard_map.40), channel_id=1, source_target_pairs={{0,224},{32,192},{64,160},{96,128},{128,96},{160,64},{192,32},{224... | collective-permute-start | bytes 73736 | tf_op jit(solution)/shard_map/ppermute | solution.py:592
  21.4 0.3 shard_map.41
  21.7 1.6 %collective-permute-done.5.half_ref = f32[48,128]{1,0:T(8,128)S(1)} collective-permute-done((f32[48,128]{1,0:T(8,128)S(1)}, f32[48,128]{1,0:T(8,128)S(1)}, u32[]{:S(2)}, u32[]{:S(2)}) %collective-permute-start.5) | collective-permute-done | bytes 24608 | tf_op jit(solution)/shard_map/ppermute | solution.py:592
  23.3 0.4 shard_map.42
  23.7 0.1 collective-permute-start.6
  23.8 1.2 %collective-permute-done.6.other_ref = f32[48,128]{1,0:T(8,128)S(1)} collective-permute-done((f32[48,128]{1,0:T(8,128)S(1)}, f32[48,128]{1,0:T(8,128)S(1)}, u32[]{:S(2)}, u32[]{:S(2)}) %collective-permute-start.6) | collective-permute-done | bytes 24608 | tf_op jit(solution)/shard_map/ppermute | solution.py:599
  25.0 0.1 shard_map.43.own_ref.small0
  25.0 0.2 collective-permute-start.9
  25.2 0.6 %collective-permute-start.8 = (f32[48,128]{1,0:T(8,128)S(1)}, f32[48,128]{1,0:T(8,128)S(1)}, u32[]{:S(2)}, u32[]{:S(2)}) collective-permute-start(f32[48,128]{1,0:T(8,128)S(1)} %shard_map.43.own_ref.small0), channel_id=1, source_target_pairs={{0,4},{1,5},{2,6},{3,7},{4,0},{5,1},{6,2},{7,3},{8,12},{9,13},{10,... | collective-permute-start | bytes 73736 | tf_op jit(solution)/shard_map/ppermute | solution.py:608
  25.9 3.4 %collective-permute-start.7 = (f32[48,128]{1,0:T(8,128)S(1)}, f32[48,128]{1,0:T(8,128)S(1)}, u32[]{:S(2)}, u32[]{:S(2)}) collective-permute-start(f32[48,128]{1,0:T(8,128)S(1)} %shard_map.43.own_ref.small0), channel_id=1, source_target_pairs={{0,2},{1,3},{2,0},{3,1},{4,6},{5,7},{6,4},{7,5},{8,10},{9,11},{10,... | collective-permute-start | bytes 73736 | tf_op jit(solution)/shard_map/ppermute | solution.py:608
  29.2 0.9 %collective-permute-done.9.three_ref.small3 = f32[48,128]{1,0:T(8,128)S(1)} collective-permute-done((f32[48,128]{1,0:T(8,128)S(1)}, f32[48,128]{1,0:T(8,128)S(1)}, u32[]{:S(2)}, u32[]{:S(2)}) %collective-permute-start.9) | collective-permute-done | bytes 24608 | tf_op jit(solution)/shard_map/ppermute | solution.py:608
  30.2 0.6 %collective-permute-done.8.two_ref.small2 = f32[48,128]{1,0:T(8,128)S(1)} collective-permute-done((f32[48,128]{1,0:T(8,128)S(1)}, f32[48,128]{1,0:T(8,128)S(1)}, u32[]{:S(2)}, u32[]{:S(2)}) %collective-permute-start.8) | collective-permute-done | bytes 24608 | tf_op jit(solution)/shard_map/ppermute | solution.py:608
  30.8 0.5 %collective-permute-done.7.one_ref.small1 = f32[48,128]{1,0:T(8,128)S(1)} collective-permute-done((f32[48,128]{1,0:T(8,128)S(1)}, f32[48,128]{1,0:T(8,128)S(1)}, u32[]{:S(2)}, u32[]{:S(2)}) %collective-permute-start.7) | collective-permute-done | bytes 24608 | tf_op jit(solution)/shard_map/ppermute | solution.py:608
  31.3 0.1 shard_map.44.large0
  31.4 2.3 %collective-permute-start.12 = (f32[48,128]{1,0:T(8,128)S(1)}, f32[48,128]{1,0:T(8,128)S(1)}, u32[]{:S(2)}, u32[]{:S(2)}) collective-permute-start(f32[48,128]{1,0:T(8,128)S(1)} %shard_map.44.large0), channel_id=1, source_target_pairs={{0,24},{1,25},{2,26},{3,27},{4,28},{5,29},{6,30},{7,31},{8,16},{9,... | collective-permute-start | bytes 73736 | tf_op jit(solution)/shard_map/ppermute | solution.py:610
  33.7 0.6 %collective-permute-start.11 = (f32[48,128]{1,0:T(8,128)S(1)}, f32[48,128]{1,0:T(8,128)S(1)}, u32[]{:S(2)}, u32[]{:S(2)}) collective-permute-start(f32[48,128]{1,0:T(8,128)S(1)} %shard_map.44.large0), channel_id=1, source_target_pairs={{0,16},{1,17},{2,18},{3,19},{4,20},{5,21},{6,22},{7,23},{8,24},{9,... | collective-permute-start | bytes 73736 | tf_op jit(solution)/shard_map/ppermute | solution.py:610
  34.3 1.3 %collective-permute-start.10 = (f32[48,128]{1,0:T(8,128)S(1)}, f32[48,128]{1,0:T(8,128)S(1)}, u32[]{:S(2)}, u32[]{:S(2)}) collective-permute-start(f32[48,128]{1,0:T(8,128)S(1)} %shard_map.44.large0), channel_id=1, source_target_pairs={{0,8},{1,9},{2,10},{3,11},{4,12},{5,13},{6,14},{7,15},{8,0},{9,1},... | collective-permute-start | bytes 73736 | tf_op jit(solution)/shard_map/ppermute | solution.py:610
  35.6 1.5 %shard_map.45 = (f32[896,128]{1,0:T(8,128)S(1)}, f32[768,128]{1,0:T(8,128)S(1)}, f32[128,128]{1,0:T(8,128)S(1)}, f32[384,128]{1,0:T(8,128)S(1)}, f32[512,128]{1,0:T(8,128)S(1)}) custom-call(f32[128,128]{1,0:T(8,128)S(1)} %get-tuple-element.49.k_ref, f32[512,128]{1,0:T(8,128)S(1)} %bitcast.5), custom_call_target="tpu_custom_call" | custom-call | flops 4000000 | bytes 4000000 | tf_op jit(solution)/shard_map/pallas_call | solution.py:538
  37.1 0.0 collective-permute-done.12.large3
  37.1 1.9 %collective-permute-done.11.large2 = f32[48,128]{1,0:T(8,128)S(1)} collective-permute-done((f32[48,128]{1,0:T(8,128)S(1)}, f32[48,128]{1,0:T(8,128)S(1)}, u32[]{:S(2)}, u32[]{:S(2)}) %collective-permute-start.11) | collective-permute-done | bytes 24608 | tf_op jit(solution)/shard_map/ppermute | solution.py:610
  39.0 0.0 collective-permute-done.10.large1
  39.0 1.7 %shard_map.46 = f32[512,128]{1,0:T(8,128)} custom-call(f32[48,128]{1,0:T(8,128)S(1)} %shard_map.44.large0, f32[48,128]{1,0:T(8,128)S(1)} %collective-permute-done.10.large1, f32[48,128]{1,0:T(8,128)S(1)} %collective-permute-done.11.large2, f32[48,128]{1,0:T(8,128)S(1)} %collective-permute-done.12.large3, f32[48,128]{1,0:T(8,128)S(1)} %shard_map.43.own_ref.small0, ...), custom_call_target="tpu_custom_call" | custom-call | flops 20000 | bytes 20000 | tf_op jit(solution)/shard_map/pallas_call | solution.py:538
Async XLA Ops:
  0.0 5.6 %copy-start.1 = (s32[8,16,64]{2,1,0:T(8,128)S(1)}, s32[8,16,64]{2,1,0:T(8,128)}, u32[]{:S(2)}) copy-start(s32[8,16,64]{2,1,0:T(8,128)} %ids_hbm.1) | copy-start | bytes 98308
  0.0 7.4 %copy-start = (f32[16,32,128]{2,1,0:T(8,128)S(1)}, f32[16,32,128]{2,1,0:T(8,128)}, u32[]{:S(2)}) copy-start(f32[16,32,128]{2,1,0:T(8,128)} %heat_hbm.1) | copy-start | bytes 786436
  0.9 6.5 %collective-permute-start = (f32[24,128]{1,0:T(8,128)S(1)}, f32[24,128]{1,0:T(8,128)S(1)}, u32[]{:S(2)}, u32[]{:S(2)}) collective-permute-start(f32[24,128]{1,0:T(8,128)S(1)} %get-tuple-element.32), channel_id=1, source_target_pairs={{0,31},{1,2},{2,1},{3,4},{4,3},{5,6},{6,5},{7,8},{8,7},{9,10},{10,... | collective-permute-start | bytes 36872 | tf_op jit(solution)/shard_map/ppermute | solution.py:569
  5.6 0.7 %copy-start.2 = (f32[16]{0:T(128)S(1)}, f32[16]{0:T(128)}, u32[]{:S(2)}) copy-start(f32[16]{0:T(128)} %table_ref.1) | copy-start | bytes 196
  5.6 1.8 %collective-permute-start.1 = (f32[24,128]{1,0:T(8,128)S(1)}, f32[24,128]{1,0:T(8,128)S(1)}, u32[]{:S(2)}, u32[]{:S(2)}) collective-permute-start(f32[24,128]{1,0:T(8,128)S(1)} %get-tuple-element.33), channel_id=1, source_target_pairs={{0,1},{1,0},{2,3},{3,2},{4,5},{5,4},{6,7},{7,6},{8,9},{9,8},{10,11... | collective-permute-start | bytes 36872 | tf_op jit(solution)/shard_map/ppermute | solution.py:568
  7.7 4.8 %collective-permute-start.4 = (f32[104,128]{1,0:T(8,128)S(1)}, f32[104,128]{1,0:T(8,128)S(1)}, u32[]{:S(2)}, u32[]{:S(2)}) collective-permute-start(f32[104,128]{1,0:T(8,128)S(1)} %get-tuple-element.37.own_ref), channel_id=1, source_target_pairs={{0,96},{32,64},{64,32},{96,0},{128,224},{160,192},{192,160},{224,1... | collective-permute-start | bytes 159752 | tf_op jit(solution)/shard_map/ppermute | solution.py:584
  9.7 5.1 %collective-permute-start.3 = (f32[104,128]{1,0:T(8,128)S(1)}, f32[104,128]{1,0:T(8,128)S(1)}, u32[]{:S(2)}, u32[]{:S(2)}) collective-permute-start(f32[104,128]{1,0:T(8,128)S(1)} %get-tuple-element.37.own_ref), channel_id=1, source_target_pairs={{0,64},{32,96},{64,0},{96,32},{128,192},{160,224},{192,128},{224,1... | collective-permute-start | bytes 159752 | tf_op jit(solution)/shard_map/ppermute | solution.py:584
  12.0 4.1 %collective-permute-start.2 = (f32[104,128]{1,0:T(8,128)S(1)}, f32[104,128]{1,0:T(8,128)S(1)}, u32[]{:S(2)}, u32[]{:S(2)}) collective-permute-start(f32[104,128]{1,0:T(8,128)S(1)} %get-tuple-element.37.own_ref), channel_id=1, source_target_pairs={{0,32},{32,0},{64,96},{96,64},{128,160},{160,128},{192,224},{224,1... | collective-permute-start | bytes 159752 | tf_op jit(solution)/shard_map/ppermute | solution.py:584
  16.3 7.0 %collective-permute-start.5 = (f32[48,128]{1,0:T(8,128)S(1)}, f32[48,128]{1,0:T(8,128)S(1)}, u32[]{:S(2)}, u32[]{:S(2)}) collective-permute-start(f32[48,128]{1,0:T(8,128)S(1)} %shard_map.40), channel_id=1, source_target_pairs={{0,224},{32,192},{64,160},{96,128},{128,96},{160,64},{192,32},{224... | collective-permute-start | bytes 73736 | tf_op jit(solution)/shard_map/ppermute | solution.py:592
  23.7 1.3 %collective-permute-start.6 = (f32[48,128]{1,0:T(8,128)S(1)}, f32[48,128]{1,0:T(8,128)S(1)}, u32[]{:S(2)}, u32[]{:S(2)}) collective-permute-start(f32[48,128]{1,0:T(8,128)S(1)} %get-tuple-element.44.own_ref), channel_id=1, source_target_pairs={{0,1},{1,0},{2,3},{3,2},{4,5},{5,4},{6,7},{7,6},{8,9},{9,8},{10,11... | collective-permute-start | bytes 73736 | tf_op jit(solution)/shard_map/ppermute | solution.py:599
  25.0 5.1 %collective-permute-start.9 = (f32[48,128]{1,0:T(8,128)S(1)}, f32[48,128]{1,0:T(8,128)S(1)}, u32[]{:S(2)}, u32[]{:S(2)}) collective-permute-start(f32[48,128]{1,0:T(8,128)S(1)} %shard_map.43.own_ref.small0), channel_id=1, source_target_pairs={{0,6},{1,7},{2,4},{3,5},{4,2},{5,3},{6,0},{7,1},{8,14},{9,15},{10,... | collective-permute-start | bytes 73736 | tf_op jit(solution)/shard_map/ppermute | solution.py:608
  25.2 5.6 %collective-permute-start.8 = (f32[48,128]{1,0:T(8,128)S(1)}, f32[48,128]{1,0:T(8,128)S(1)}, u32[]{:S(2)}, u32[]{:S(2)}) collective-permute-start(f32[48,128]{1,0:T(8,128)S(1)} %shard_map.43.own_ref.small0), channel_id=1, source_target_pairs={{0,4},{1,5},{2,6},{3,7},{4,0},{5,1},{6,2},{7,3},{8,12},{9,13},{10,... | collective-permute-start | bytes 73736 | tf_op jit(solution)/shard_map/ppermute | solution.py:608
  25.9 5.4 %collective-permute-start.7 = (f32[48,128]{1,0:T(8,128)S(1)}, f32[48,128]{1,0:T(8,128)S(1)}, u32[]{:S(2)}, u32[]{:S(2)}) collective-permute-start(f32[48,128]{1,0:T(8,128)S(1)} %shard_map.43.own_ref.small0), channel_id=1, source_target_pairs={{0,2},{1,3},{2,0},{3,1},{4,6},{5,7},{6,4},{7,5},{8,10},{9,11},{10,... | collective-permute-start | bytes 73736 | tf_op jit(solution)/shard_map/ppermute | solution.py:608
  31.4 5.7 %collective-permute-start.12 = (f32[48,128]{1,0:T(8,128)S(1)}, f32[48,128]{1,0:T(8,128)S(1)}, u32[]{:S(2)}, u32[]{:S(2)}) collective-permute-start(f32[48,128]{1,0:T(8,128)S(1)} %shard_map.44.large0), channel_id=1, source_target_pairs={{0,24},{1,25},{2,26},{3,27},{4,28},{5,29},{6,30},{7,31},{8,16},{9,... | collective-permute-start | bytes 73736 | tf_op jit(solution)/shard_map/ppermute | solution.py:610
  33.7 5.3 %collective-permute-start.11 = (f32[48,128]{1,0:T(8,128)S(1)}, f32[48,128]{1,0:T(8,128)S(1)}, u32[]{:S(2)}, u32[]{:S(2)}) collective-permute-start(f32[48,128]{1,0:T(8,128)S(1)} %shard_map.44.large0), channel_id=1, source_target_pairs={{0,16},{1,17},{2,18},{3,19},{4,20},{5,21},{6,22},{7,23},{8,24},{9,... | collective-permute-start | bytes 73736 | tf_op jit(solution)/shard_map/ppermute | solution.py:610
  34.3 4.7 %collective-permute-start.10 = (f32[48,128]{1,0:T(8,128)S(1)}, f32[48,128]{1,0:T(8,128)S(1)}, u32[]{:S(2)}, u32[]{:S(2)}) collective-permute-start(f32[48,128]{1,0:T(8,128)S(1)} %shard_map.44.large0), channel_id=1, source_target_pairs={{0,8},{1,9},{2,10},{3,11},{4,12},{5,13},{6,14},{7,15},{8,0},{9,1},... | collective-permute-start | bytes 73736 | tf_op jit(solution)/shard_map/ppermute | solution.py:610

commit v7 on v5

--- a/solution.py
+++ b/solution.py
@@ -156,7 +156,12 @@
     my_ref[8:16, :] = pack(link, outer)
 
 
-def z_matrix_kernel(k_ref, za_ref, zc_ref, zi_ref, zo_ref):
+def z_matrix_kernel(k_ref, heat_ref, za_ref, zc_ref, zi_ref, zo_ref, turned_ref):
+    for y in range(NY):
+        for p in range(2):
+            turned_ref[y * NX + p * MX : y * NX + (p + 1) * MX, :] = heat_ref[
+                pl.ds(p * NY + y, MX, stride=2 * NY), :
+            ]
     ky = [k_ref[pl.ds(n, MX, stride=MY), :] for n in range(MY)]
     group = 16
     for start in range(0, MY, group):
@@ -525,7 +530,7 @@
             b = jnp.where(even, next_w, odd * b + (odd_low * w + odd_high * turned(w, -2)))
             for y, v in ((2 * n, a), (2 * n + 1, b)):
                 where = pl.ds(p * NY + y, MX, stride=2 * NY)
-                out_ref[where, :] = heat_ref[where, :] + v
+                out_ref[where, :] = heat_ref[y * NX + p * MX : y * NX + (p + 1) * MX, :] + v
 
 
 def call(kernel, ins, outs, scratch=(), outside=False, smem=(), cost=20000, limit=8 << 20):
@@ -594,10 +599,10 @@
     other = lax.ppermute(own, "gy", cores)
     (chip,) = call(chip_kernel, (own, other, mid), [(YROWS, NZ)])
     chip, k = lax.optimization_barrier((chip, k))
-    za, zc, zi, zo = call(
+    za, zc, zi, zo, turned = call(
         z_matrix_kernel,
-        (k,),
-        [(7 * MX * MY, NZ), (6 * MX * MY, NZ), (MX * MY, NZ), (3 * MX * MY, NZ)],
+        (k, heat),
+        [(7 * MX * MY, NZ), (6 * MX * MY, NZ), (MX * MY, NZ), (3 * MX * MY, NZ), (NX * NY, NZ)],
         cost=4000000,
     )
     small = [chip] + [lax.ppermute(chip, "gy", [(i, i ^ (2 * d)) for i in range(ny)]) for d in (1, 2, 3)]
@@ -605,7 +610,7 @@
     large = [four] + [lax.ppermute(four, "gy", [(i, i ^ (8 * d)) for i in range(ny)]) for d in (1, 2, 3)]
     (out,) = call(
         y_solve_kernel,
-        (*large, *small, own, other, mid, rby, gy, hy, iy, za, zc, zi, zo, heat),
+        (*large, *small, own, other, mid, rby, gy, hy, iy, za, zc, zi, zo, turned),
         [(NX * NY, NZ)],
         scratch=[pltpu.VMEM((NX * NY, NZ), f32)],
     )

time: 41.1 us -> 41 us (level)
  no operation moved by 1% of the time
where the time goes in v7:
time: 41 us; the launch traced here: 40.9 us
  starting transfers between devices  23.1 us (56%)
  waiting for transfers between devices  10.7 us (26%)
  Pallas kernels  6.34 us (15%)
  local copies, waits for them, and re-layouts  0.66 us (2%)
    pallas_call x10, Pallas kernels, call(): pl.pallas_call(kernel, out_shape=tuple((jax.ShapeDtypeStruct(s, f32) for...  6.34 us
    ppermute x1, starting transfers between devices, on_device(): half = lax.ppermute(half, 'gx', [(i, nx - 1 - i) for i in range(nx)])  5.1 us
    ppermute x3, starting transfers between devices, on_device(): lax.ppermute(send, 'gx', [(i, i ^ d) for i in range(nx)])  4.82 us
    ppermute x1, starting transfers between devices, on_device(): lax.ppermute(outer, 'gy', [(i, (i + (1 if i % 2 else -1)) % ny) for i in...  4.74 us
    ppermute x3, starting transfers between devices, on_device(): lax.ppermute(chip, 'gy', [(i, i ^ 2 * d) for i in range(ny)])  4.18 us
    ppermute x3, starting transfers between devices, on_device(): lax.ppermute(four, 'gy', [(i, i ^ 8 * d) for i in range(ny)])  4.18 us
    ppermute x3, waiting for transfers between devices, on_device(): lax.ppermute(send, 'gx', [(i, i ^ d) for i in range(nx)])  3.6 us
    ppermute x3, waiting for transfers between devices, on_device(): lax.ppermute(chip, 'gy', [(i, i ^ 2 * d) for i in range(ny)])  2.06 us
  transfers between devices with their start and end apart: 13, of which 9 were waited for; matrix products, arithmetic and copies ran while one was open for 0% of the time, Pallas kernels for 6%

profile of v7, /device:TPU:32, one launch (start us, length us, event | category | flops | bytes accessed | tf_op | source)
XLA Modules:
  0.0 40.9 jit_solution(10439092958977431005)
XLA Ops:
  0.0 0.0 copy-start.1
  0.0 0.0 copy-start
  0.0 1.0 %shard_map.38 = (f32[24,128]{1,0:T(8,128)S(1)}, f32[24,128]{1,0:T(8,128)S(1)}) custom-call(s32[8,16,64]{2,1,0:T(8,128)} %ids_hbm.1, f32[16,32,128]{2,1,0:T(8,128)} %heat_hbm.1), custom_call_target="tpu_custom_call" | custom-call | flops 20000 | bytes 20000 | tf_op jit(solution)/shard_map/pallas_call | solution.py:538
  1.0 4.7 %collective-permute-start = (f32[24,128]{1,0:T(8,128)S(1)}, f32[24,128]{1,0:T(8,128)S(1)}, u32[]{:S(2)}, u32[]{:S(2)}) collective-permute-start(f32[24,128]{1,0:T(8,128)S(1)} %get-tuple-element.32), channel_id=1, source_target_pairs={{0,31},{1,2},{2,1},{3,4},{4,3},{5,6},{6,5},{7,8},{8,7},{9,10},{10,... | collective-permute-start | bytes 36872 | tf_op jit(solution)/shard_map/ppermute | solution.py:569
  5.7 0.0 copy-start.2
  5.7 0.0 collective-permute-start.1
  5.7 0.0 copy-done.1
  5.7 0.6 %copy-done.2 = f32[16]{0:T(128)S(1)} copy-done((f32[16]{0:T(128)S(1)}, f32[16]{0:T(128)}, u32[]{:S(2)}) %copy-start.2) | copy-done | bytes 88
  6.4 0.8 %shard_map.37 = (f32[128,128]{1,0:T(8,128)S(1)}, f32[8,128]{1,0:T(8,128)S(1)}, f32[224,128]{1,0:T(8,128)S(1)}, f32[224,128]{1,0:T(8,128)S(1)}, f32[224,128]{1,0:T(8,128)S(1)}, /*index=5*/f32[40,128]{1,0:T(8,128)S(1)}) custom-call(s32[128,64]{1,0:T(8,128)S(1)} %bitcast.6, f32[16]{0:T(128)S(1)} %copy-done.2), custom_call_target="tpu_custom_call" | custom-call | flops 2000000 | bytes 2000000 | tf_op jit(solution)/shard_map/pallas_call | solution.py:538
  7.2 0.3 collective-permute-done.outer_ref
  7.5 0.0 collective-permute-done.1.inner_ref
  7.5 0.0 copy-done
  7.5 0.3 shard_map.39
  7.8 2.0 %collective-permute-start.4 = (f32[104,128]{1,0:T(8,128)S(1)}, f32[104,128]{1,0:T(8,128)S(1)}, u32[]{:S(2)}, u32[]{:S(2)}) collective-permute-start(f32[104,128]{1,0:T(8,128)S(1)} %get-tuple-element.37.own_ref), channel_id=1, source_target_pairs={{0,96},{32,64},{64,32},{96,0},{128,224},{160,192},{192,160},{224,1... | collective-permute-start | bytes 159752 | tf_op jit(solution)/shard_map/ppermute | solution.py:584
  9.8 2.3 %collective-permute-start.3 = (f32[104,128]{1,0:T(8,128)S(1)}, f32[104,128]{1,0:T(8,128)S(1)}, u32[]{:S(2)}, u32[]{:S(2)}) collective-permute-start(f32[104,128]{1,0:T(8,128)S(1)} %get-tuple-element.37.own_ref), channel_id=1, source_target_pairs={{0,64},{32,96},{64,0},{96,32},{128,192},{160,224},{192,128},{224,1... | collective-permute-start | bytes 159752 | tf_op jit(solution)/shard_map/ppermute | solution.py:584
  12.1 0.5 %collective-permute-start.2 = (f32[104,128]{1,0:T(8,128)S(1)}, f32[104,128]{1,0:T(8,128)S(1)}, u32[]{:S(2)}, u32[]{:S(2)}) collective-permute-start(f32[104,128]{1,0:T(8,128)S(1)} %get-tuple-element.37.own_ref), channel_id=1, source_target_pairs={{0,32},{32,0},{64,96},{96,64},{128,160},{160,128},{192,224},{224,1... | collective-permute-start | bytes 159752 | tf_op jit(solution)/shard_map/ppermute | solution.py:584
  12.6 0.0 collective-permute-done.4.three_ref
  12.6 2.3 %collective-permute-done.3.two_ref = f32[104,128]{1,0:T(8,128)S(1)} collective-permute-done((f32[104,128]{1,0:T(8,128)S(1)}, f32[104,128]{1,0:T(8,128)S(1)}, u32[]{:S(2)}, u32[]{:S(2)}) %collective-permute-start.3) | collective-permute-done | bytes 53280 | tf_op jit(solution)/shard_map/ppermute | solution.py:584
  14.9 1.3 %collective-permute-done.2.one_ref = f32[104,128]{1,0:T(8,128)S(1)} collective-permute-done((f32[104,128]{1,0:T(8,128)S(1)}, f32[104,128]{1,0:T(8,128)S(1)}, u32[]{:S(2)}, u32[]{:S(2)}) %collective-permute-start.2) | collective-permute-done | bytes 53280 | tf_op jit(solution)/shard_map/ppermute | solution.py:584
  16.2 0.1 shard_map.40
  16.4 5.1 %collective-permute-start.5 = (f32[48,128]{1,0:T(8,128)S(1)}, f32[48,128]{1,0:T(8,128)S(1)}, u32[]{:S(2)}, u32[]{:S(2)}) collective-permute-start(f32[48,128]{1,0:T(8,128)S(1)} %shard_map.40), channel_id=1, source_target_pairs={{0,224},{32,192},{64,160},{96,128},{128,96},{160,64},{192,32},{224... | collective-permute-start | bytes 73736 | tf_op jit(solution)/shard_map/ppermute | solution.py:592
  21.5 0.3 shard_map.41
  21.8 1.6 %collective-permute-done.5.half_ref = f32[48,128]{1,0:T(8,128)S(1)} collective-permute-done((f32[48,128]{1,0:T(8,128)S(1)}, f32[48,128]{1,0:T(8,128)S(1)}, u32[]{:S(2)}, u32[]{:S(2)}) %collective-permute-start.5) | collective-permute-done | bytes 24608 | tf_op jit(solution)/shard_map/ppermute | solution.py:592
  23.4 0.4 shard_map.42
  23.8 0.1 collective-permute-start.6
  23.9 1.2 %collective-permute-done.6.other_ref = f32[48,128]{1,0:T(8,128)S(1)} collective-permute-done((f32[48,128]{1,0:T(8,128)S(1)}, f32[48,128]{1,0:T(8,128)S(1)}, u32[]{:S(2)}, u32[]{:S(2)}) %collective-permute-start.6) | collective-permute-done | bytes 24608 | tf_op jit(solution)/shard_map/ppermute | solution.py:599
  25.1 0.1 shard_map.43.own_ref.small0
  25.2 0.2 collective-permute-start.9
  25.4 0.6 %collective-permute-start.8 = (f32[48,128]{1,0:T(8,128)S(1)}, f32[48,128]{1,0:T(8,128)S(1)}, u32[]{:S(2)}, u32[]{:S(2)}) collective-permute-start(f32[48,128]{1,0:T(8,128)S(1)} %shard_map.43.own_ref.small0), channel_id=1, source_target_pairs={{0,4},{1,5},{2,6},{3,7},{4,0},{5,1},{6,2},{7,3},{8,12},{9,13},{10,... | collective-permute-start | bytes 73736 | tf_op jit(solution)/shard_map/ppermute | solution.py:608
  26.0 3.4 %collective-permute-start.7 = (f32[48,128]{1,0:T(8,128)S(1)}, f32[48,128]{1,0:T(8,128)S(1)}, u32[]{:S(2)}, u32[]{:S(2)}) collective-permute-start(f32[48,128]{1,0:T(8,128)S(1)} %shard_map.43.own_ref.small0), channel_id=1, source_target_pairs={{0,2},{1,3},{2,0},{3,1},{4,6},{5,7},{6,4},{7,5},{8,10},{9,11},{10,... | collective-permute-start | bytes 73736 | tf_op jit(solution)/shard_map/ppermute | solution.py:608
  29.4 0.9 %collective-permute-done.9.three_ref.small3 = f32[48,128]{1,0:T(8,128)S(1)} collective-permute-done((f32[48,128]{1,0:T(8,128)S(1)}, f32[48,128]{1,0:T(8,128)S(1)}, u32[]{:S(2)}, u32[]{:S(2)}) %collective-permute-start.9) | collective-permute-done | bytes 24608 | tf_op jit(solution)/shard_map/ppermute | solution.py:608
  30.3 0.6 %collective-permute-done.8.two_ref.small2 = f32[48,128]{1,0:T(8,128)S(1)} collective-permute-done((f32[48,128]{1,0:T(8,128)S(1)}, f32[48,128]{1,0:T(8,128)S(1)}, u32[]{:S(2)}, u32[]{:S(2)}) %collective-permute-start.8) | collective-permute-done | bytes 24608 | tf_op jit(solution)/shard_map/ppermute | solution.py:608
  31.0 0.5 %collective-permute-done.7.one_ref.small1 = f32[48,128]{1,0:T(8,128)S(1)} collective-permute-done((f32[48,128]{1,0:T(8,128)S(1)}, f32[48,128]{1,0:T(8,128)S(1)}, u32[]{:S(2)}, u32[]{:S(2)}) %collective-permute-start.7) | collective-permute-done | bytes 24608 | tf_op jit(solution)/shard_map/ppermute | solution.py:608
  31.4 0.1 shard_map.44.large0
  31.6 2.3 %collective-permute-start.12 = (f32[48,128]{1,0:T(8,128)S(1)}, f32[48,128]{1,0:T(8,128)S(1)}, u32[]{:S(2)}, u32[]{:S(2)}) collective-permute-start(f32[48,128]{1,0:T(8,128)S(1)} %shard_map.44.large0), channel_id=1, source_target_pairs={{0,24},{1,25},{2,26},{3,27},{4,28},{5,29},{6,30},{7,31},{8,16},{9,... | collective-permute-start | bytes 73736 | tf_op jit(solution)/shard_map/ppermute | solution.py:610
  33.8 0.6 %collective-permute-start.11 = (f32[48,128]{1,0:T(8,128)S(1)}, f32[48,128]{1,0:T(8,128)S(1)}, u32[]{:S(2)}, u32[]{:S(2)}) collective-permute-start(f32[48,128]{1,0:T(8,128)S(1)} %shard_map.44.large0), channel_id=1, source_target_pairs={{0,16},{1,17},{2,18},{3,19},{4,20},{5,21},{6,22},{7,23},{8,24},{9,... | collective-permute-start | bytes 73736 | tf_op jit(solution)/shard_map/ppermute | solution.py:610
  34.5 1.3 %collective-permute-start.10 = (f32[48,128]{1,0:T(8,128)S(1)}, f32[48,128]{1,0:T(8,128)S(1)}, u32[]{:S(2)}, u32[]{:S(2)}) collective-permute-start(f32[48,128]{1,0:T(8,128)S(1)} %shard_map.44.large0), channel_id=1, source_target_pairs={{0,8},{1,9},{2,10},{3,11},{4,12},{5,13},{6,14},{7,15},{8,0},{9,1},... | collective-permute-start | bytes 73736 | tf_op jit(solution)/shard_map/ppermute | solution.py:610
  35.7 1.5 %shard_map.45 = (f32[896,128]{1,0:T(8,128)S(1)}, f32[768,128]{1,0:T(8,128)S(1)}, f32[128,128]{1,0:T(8,128)S(1)}, f32[384,128]{1,0:T(8,128)S(1)}, f32[512,128]{1,0:T(8,128)S(1)}) custom-call(f32[128,128]{1,0:T(8,128)S(1)} %get-tuple-element.49.k_ref, f32[512,128]{1,0:T(8,128)S(1)} %bitcast.5), custom_call_target="tpu_custom_call" | custom-call | flops 4000000 | bytes 4000000 | tf_op jit(solution)/shard_map/pallas_call | solution.py:538
  37.2 0.0 collective-permute-done.12.large3
  37.2 1.9 %collective-permute-done.11.large2 = f32[48,128]{1,0:T(8,128)S(1)} collective-permute-done((f32[48,128]{1,0:T(8,128)S(1)}, f32[48,128]{1,0:T(8,128)S(1)}, u32[]{:S(2)}, u32[]{:S(2)}) %collective-permute-start.11) | collective-permute-done | bytes 24608 | tf_op jit(solution)/shard_map/ppermute | solution.py:610
  39.2 0.0 collective-permute-done.10.large1
  39.2 1.7 %shard_map.46 = f32[512,128]{1,0:T(8,128)} custom-call(f32[48,128]{1,0:T(8,128)S(1)} %shard_map.44.large0, f32[48,128]{1,0:T(8,128)S(1)} %collective-permute-done.10.large1, f32[48,128]{1,0:T(8,128)S(1)} %collective-permute-done.11.large2, f32[48,128]{1,0:T(8,128)S(1)} %collective-permute-done.12.large3, f32[48,128]{1,0:T(8,128)S(1)} %shard_map.43.own_ref.small0, ...), custom_call_target="tpu_custom_call" | custom-call | flops 20000 | bytes 20000 | tf_op jit(solution)/shard_map/pallas_call | solution.py:538
Async XLA Ops:
  0.0 5.7 %copy-start.1 = (s32[8,16,64]{2,1,0:T(8,128)S(1)}, s32[8,16,64]{2,1,0:T(8,128)}, u32[]{:S(2)}) copy-start(s32[8,16,64]{2,1,0:T(8,128)} %ids_hbm.1) | copy-start | bytes 98308
  0.0 7.5 %copy-start = (f32[16,32,128]{2,1,0:T(8,128)S(1)}, f32[16,32,128]{2,1,0:T(8,128)}, u32[]{:S(2)}) copy-start(f32[16,32,128]{2,1,0:T(8,128)} %heat_hbm.1) | copy-start | bytes 786436
  1.0 6.5 %collective-permute-start = (f32[24,128]{1,0:T(8,128)S(1)}, f32[24,128]{1,0:T(8,128)S(1)}, u32[]{:S(2)}, u32[]{:S(2)}) collective-permute-start(f32[24,128]{1,0:T(8,128)S(1)} %get-tuple-element.32), channel_id=1, source_target_pairs={{0,31},{1,2},{2,1},{3,4},{4,3},{5,6},{6,5},{7,8},{8,7},{9,10},{10,... | collective-permute-start | bytes 36872 | tf_op jit(solution)/shard_map/ppermute | solution.py:569
  5.7 0.7 %copy-start.2 = (f32[16]{0:T(128)S(1)}, f32[16]{0:T(128)}, u32[]{:S(2)}) copy-start(f32[16]{0:T(128)} %table_ref.1) | copy-start | bytes 196
  5.7 1.8 %collective-permute-start.1 = (f32[24,128]{1,0:T(8,128)S(1)}, f32[24,128]{1,0:T(8,128)S(1)}, u32[]{:S(2)}, u32[]{:S(2)}) collective-permute-start(f32[24,128]{1,0:T(8,128)S(1)} %get-tuple-element.33), channel_id=1, source_target_pairs={{0,1},{1,0},{2,3},{3,2},{4,5},{5,4},{6,7},{7,6},{8,9},{9,8},{10,11... | collective-permute-start | bytes 36872 | tf_op jit(solution)/shard_map/ppermute | solution.py:568
  7.8 4.8 %collective-permute-start.4 = (f32[104,128]{1,0:T(8,128)S(1)}, f32[104,128]{1,0:T(8,128)S(1)}, u32[]{:S(2)}, u32[]{:S(2)}) collective-permute-start(f32[104,128]{1,0:T(8,128)S(1)} %get-tuple-element.37.own_ref), channel_id=1, source_target_pairs={{0,96},{32,64},{64,32},{96,0},{128,224},{160,192},{192,160},{224,1... | collective-permute-start | bytes 159752 | tf_op jit(solution)/shard_map/ppermute | solution.py:584
  9.8 5.1 %collective-permute-start.3 = (f32[104,128]{1,0:T(8,128)S(1)}, f32[104,128]{1,0:T(8,128)S(1)}, u32[]{:S(2)}, u32[]{:S(2)}) collective-permute-start(f32[104,128]{1,0:T(8,128)S(1)} %get-tuple-element.37.own_ref), channel_id=1, source_target_pairs={{0,64},{32,96},{64,0},{96,32},{128,192},{160,224},{192,128},{224,1... | collective-permute-start | bytes 159752 | tf_op jit(solution)/shard_map/ppermute | solution.py:584
  12.1 4.1 %collective-permute-start.2 = (f32[104,128]{1,0:T(8,128)S(1)}, f32[104,128]{1,0:T(8,128)S(1)}, u32[]{:S(2)}, u32[]{:S(2)}) collective-permute-start(f32[104,128]{1,0:T(8,128)S(1)} %get-tuple-element.37.own_ref), channel_id=1, source_target_pairs={{0,32},{32,0},{64,96},{96,64},{128,160},{160,128},{192,224},{224,1... | collective-permute-start | bytes 159752 | tf_op jit(solution)/shard_map/ppermute | solution.py:584
  16.4 7.0 %collective-permute-start.5 = (f32[48,128]{1,0:T(8,128)S(1)}, f32[48,128]{1,0:T(8,128)S(1)}, u32[]{:S(2)}, u32[]{:S(2)}) collective-permute-start(f32[48,128]{1,0:T(8,128)S(1)} %shard_map.40), channel_id=1, source_target_pairs={{0,224},{32,192},{64,160},{96,128},{128,96},{160,64},{192,32},{224... | collective-permute-start | bytes 73736 | tf_op jit(solution)/shard_map/ppermute | solution.py:592
  23.8 1.3 %collective-permute-start.6 = (f32[48,128]{1,0:T(8,128)S(1)}, f32[48,128]{1,0:T(8,128)S(1)}, u32[]{:S(2)}, u32[]{:S(2)}) collective-permute-start(f32[48,128]{1,0:T(8,128)S(1)} %get-tuple-element.44.own_ref), channel_id=1, source_target_pairs={{0,1},{1,0},{2,3},{3,2},{4,5},{5,4},{6,7},{7,6},{8,9},{9,8},{10,11... | collective-permute-start | bytes 73736 | tf_op jit(solution)/shard_map/ppermute | solution.py:599
  25.2 5.1 %collective-permute-start.9 = (f32[48,128]{1,0:T(8,128)S(1)}, f32[48,128]{1,0:T(8,128)S(1)}, u32[]{:S(2)}, u32[]{:S(2)}) collective-permute-start(f32[48,128]{1,0:T(8,128)S(1)} %shard_map.43.own_ref.small0), channel_id=1, source_target_pairs={{0,6},{1,7},{2,4},{3,5},{4,2},{5,3},{6,0},{7,1},{8,14},{9,15},{10,... | collective-permute-start | bytes 73736 | tf_op jit(solution)/shard_map/ppermute | solution.py:608
  25.4 5.6 %collective-permute-start.8 = (f32[48,128]{1,0:T(8,128)S(1)}, f32[48,128]{1,0:T(8,128)S(1)}, u32[]{:S(2)}, u32[]{:S(2)}) collective-permute-start(f32[48,128]{1,0:T(8,128)S(1)} %shard_map.43.own_ref.small0), channel_id=1, source_target_pairs={{0,4},{1,5},{2,6},{3,7},{4,0},{5,1},{6,2},{7,3},{8,12},{9,13},{10,... | collective-permute-start | bytes 73736 | tf_op jit(solution)/shard_map/ppermute | solution.py:608
  26.0 5.4 %collective-permute-start.7 = (f32[48,128]{1,0:T(8,128)S(1)}, f32[48,128]{1,0:T(8,128)S(1)}, u32[]{:S(2)}, u32[]{:S(2)}) collective-permute-start(f32[48,128]{1,0:T(8,128)S(1)} %shard_map.43.own_ref.small0), channel_id=1, source_target_pairs={{0,2},{1,3},{2,0},{3,1},{4,6},{5,7},{6,4},{7,5},{8,10},{9,11},{10,... | collective-permute-start | bytes 73736 | tf_op jit(solution)/shard_map/ppermute | solution.py:608
  31.6 5.7 %collective-permute-start.12 = (f32[48,128]{1,0:T(8,128)S(1)}, f32[48,128]{1,0:T(8,128)S(1)}, u32[]{:S(2)}, u32[]{:S(2)}) collective-permute-start(f32[48,128]{1,0:T(8,128)S(1)} %shard_map.44.large0), channel_id=1, source_target_pairs={{0,24},{1,25},{2,26},{3,27},{4,28},{5,29},{6,30},{7,31},{8,16},{9,... | collective-permute-start | bytes 73736 | tf_op jit(solution)/shard_map/ppermute | solution.py:610
  33.8 5.3 %collective-permute-start.11 = (f32[48,128]{1,0:T(8,128)S(1)}, f32[48,128]{1,0:T(8,128)S(1)}, u32[]{:S(2)}, u32[]{:S(2)}) collective-permute-start(f32[48,128]{1,0:T(8,128)S(1)} %shard_map.44.large0), channel_id=1, source_target_pairs={{0,16},{1,17},{2,18},{3,19},{4,20},{5,21},{6,22},{7,23},{8,24},{9,... | collective-permute-start | bytes 73736 | tf_op jit(solution)/shard_map/ppermute | solution.py:610
  34.5 4.7 %collective-permute-start.10 = (f32[48,128]{1,0:T(8,128)S(1)}, f32[48,128]{1,0:T(8,128)S(1)}, u32[]{:S(2)}, u32[]{:S(2)}) collective-permute-start(f32[48,128]{1,0:T(8,128)S(1)} %shard_map.44.large0), channel_id=1, source_target_pairs={{0,8},{1,9},{2,10},{3,11},{4,12},{5,13},{6,14},{7,15},{8,0},{9,1},... | collective-permute-start | bytes 73736 | tf_op jit(solution)/shard_map/ppermute | solution.py:610
